TPU v7x, 32 devices: a whole 2x2x4 slice. The times are simulated.
32 devices in a mesh: row: 4 (over z), seq: 8 (over y, x, core).
Axes of the slice: x: 2, y: 2, z: 4, core: 2. Of those that a mesh axis runs over, the one named last changes fastest.
Arguments:
- tokens: bfloat16 [8, 1024, 1024], P('row', 'seq'), may hold values from -6 to 6
- lengths: int32 [8, 2], P('row'), may hold values from 0 to 1024, as said below
- mixer_gain: bfloat16 [1024], replicated, may hold values from 0.5 to 1.5
- mixer_input: bfloat16 [1024, 3072], replicated, may hold values from -0.1875 to 0.1875
- mixer_kernel: bfloat16 [3, 1024], replicated, may hold values from -3.5 to 3.5
- mixer_output: bfloat16 [1024, 1024], replicated, may hold values from -0.1875 to 0.1875
- first_gain: bfloat16 [1024], replicated, may hold values from 0.5 to 1.5
- first_gate: bfloat16 [1024, 4608], replicated, may hold values from -0.1875 to 0.1875
- first_up: bfloat16 [1024, 4608], replicated, may hold values from -0.1875 to 0.1875
- first_down: bfloat16 [4608, 1024], replicated, may hold values from -0.09375 to 0.09375
- attend_gain: bfloat16 [1024], replicated, may hold values from 0.5 to 1.5
- query_weight: bfloat16 [1024, 1024], replicated, may hold values from -0.1875 to 0.1875
- key_weight: bfloat16 [1024, 512], replicated, may hold values from -0.1875 to 0.1875
- value_weight: bfloat16 [1024, 512], replicated, may hold values from -0.1875 to 0.1875
- query_gain: bfloat16 [64], replicated, may hold values from 0.5 to 1.5
- key_gain: bfloat16 [64], replicated, may hold values from 0.5 to 1.5
- attend_output: bfloat16 [1024, 1024], replicated, may hold values from -2 to 2
- second_gain: bfloat16 [1024], replicated, may hold values from 0.5 to 1.5
- second_gate: bfloat16 [1024, 4608], replicated, may hold values from -0.1875 to 0.1875
- second_up: bfloat16 [1024, 4608], replicated, may hold values from -0.1875 to 0.1875
- second_down: bfloat16 [4608, 1024], replicated, may hold values from -0.09375 to 0.09375
- cotangent: bfloat16 [8, 1024, 1024], P('row', 'seq'), may hold values from -6 to 6
Outputs:
- mixed: bfloat16 [8, 1024, 1024], P('row', 'seq')
- token_grad: bfloat16 [8, 1024, 1024], P('row', 'seq')
- mixer_gain_grad: float32 [1024], P('seq')
- mixer_input_grad: float32 [1024, 3072], P('seq')
- mixer_kernel_grad: float32 [3, 1024], P(None, 'seq')
- mixer_output_grad: float32 [1024, 1024], P('seq')
- first_gain_grad: float32 [1024], P('seq')
- first_gate_grad: float32 [1024, 4608], P('seq')
- first_up_grad: float32 [1024, 4608], P('seq')
- first_down_grad: float32 [4608, 1024], P('seq')
- attend_gain_grad: float32 [1024], P('seq')
- query_weight_grad: float32 [1024, 1024], P('seq')
- key_weight_grad: float32 [1024, 512], P('seq')
- value_weight_grad: float32 [1024, 512], P('seq')
- query_gain_grad: float32 [64], P('seq')
- key_gain_grad: float32 [64], P('seq')
- attend_output_grad: float32 [1024, 1024], P('seq')
- second_gain_grad: float32 [1024], P('seq')
- second_gate_grad: float32 [1024, 4608], P('seq')
- second_up_grad: float32 [1024, 4608], P('seq')
- second_down_grad: float32 [4608, 1024], P('seq')
Inputs may be any that keep to these rules, and one draw needn't show every extreme that they name: Each row's lengths are multiples of 512 that sum to 1024, the nonzero ones first and zeros after them. Of each device's 2 rows, exactly one holds a single sequence of 1024, and every other row holds two or more sequences.
All inputs are finite; a program needn't handle non-finite values.
Results may differ from a plain program's by a relative error of at most 0.029.
Values may be sent and summed in bfloat16 or wider, within the bound.
A program may use at most 384 MiB of HBM per device.

v0:
```python
import jax
import jax.numpy as jnp
from jax import lax
from jax.sharding import PartitionSpec as P

HEADS = 16
KV_HEADS = 8
HEAD_DIM = 64
GROUP = 2


EPS = 1e-05
THETA = 1000000.0
NEGATIVE = -1e30
HIGHEST = lax.Precision.HIGHEST


def passed_along(value, axis, steps):
    count = lax.axis_size(axis)
    initial, last = (max(0, -steps), min(count, count - steps))
    return lax.ppermute(value, axis, [(source, source + steps) for source in range(initial, last)])


def segment_info(lengths, positions):
    boundary = jnp.cumsum(lengths, axis=-1)
    passed = boundary[:, None, :] <= positions[None, :, None]
    segment = jnp.sum(passed.astype(jnp.int32), axis=-1)
    seg_start = jnp.max(jnp.where(passed, boundary[:, None, :], 0), axis=-1)
    return (segment, seg_start)


def norm_rows(values, norm_gain):
    return values * lax.rsqrt(jnp.mean(values * values, axis=-1, keepdims=True) + EPS) * norm_gain


def rotate(values, offsets):
    half_dim = values.shape[-1] // 2
    inverse = THETA ** (-2.0 * jnp.arange(half_dim, dtype=jnp.float32) / values.shape[-1])
    angles = offsets.astype(jnp.float32)[:, :, None, None] * inverse
    cosine = jnp.cos(angles)
    sine_table = jnp.sin(angles)
    leading = values[..., :half_dim]
    trailing = values[..., half_dim:]
    return jnp.concatenate(
        [leading * cosine - trailing * sine_table, trailing * cosine + leading * sine_table],
        axis=-1,
    )


def swiglu(gate_value, upward):
    return gate_value / (1.0 + jnp.exp(-gate_value)) * upward


def dense(inputs, matrix):
    return jnp.einsum("rtd,df->rtf", inputs, matrix, preferred_element_type=jnp.float32)


def weight_grad(inputs, gradient):
    return jnp.einsum("rtd,rtf->df", inputs, gradient, preferred_element_type=jnp.float32)


def back_dense(gradient, matrix):
    return jnp.einsum("rtf,df->rtd", gradient, matrix, preferred_element_type=jnp.float32)


def mixer_block(hidden, norm_gain, input_matrix, kernel, output_matrix, seg_start, positions):
    feature_columns = hidden.shape[-1]
    length = hidden.shape[1]
    normed, norm_back = jax.vjp(norm_rows, hidden, norm_gain.astype(jnp.float32))
    normed_low = normed.astype(jnp.bfloat16)
    projected_rows = dense(normed_low, input_matrix)
    input_gate_value = projected_rows[..., :feature_columns]
    exit_gate = projected_rows[..., feature_columns : 2 * feature_columns]
    carry_value = projected_rows[..., 2 * feature_columns :]
    gated_product_reduced = (input_gate_value * carry_value).astype(jnp.bfloat16)
    previous = passed_along(gated_product_reduced[:, length - 2 :, :], "seq", 1)
    extended = jnp.concatenate([previous, gated_product_reduced], axis=1).astype(jnp.float32)
    keep_one = (positions[None, :] - 1 >= seg_start).astype(jnp.float32)[..., None]
    keep_two = (positions[None, :] - 2 >= seg_start).astype(jnp.float32)[..., None]
    kernel_taps = kernel.astype(jnp.float32)
    two_back = extended[:, :length]
    one_back = extended[:, 1 : length + 1]
    current = extended[:, 2:]
    convolved = (
        kernel_taps[2] * current
        + kernel_taps[1] * keep_one * one_back
        + kernel_taps[0] * keep_two * two_back
    )
    gated_low = (exit_gate * convolved).astype(jnp.bfloat16)
    result = hidden + dense(gated_low, output_matrix)

    def mixer_backward(gradient):
        gradient_low = gradient.astype(jnp.bfloat16)
        grad_output = weight_grad(gated_low, gradient_low)
        grad_gated = back_dense(gradient_low, output_matrix)
        output_gate_gradient = grad_gated * convolved
        grad_conv = grad_gated * exit_gate
        grad_kernel = jnp.stack(
            [
                jnp.sum(grad_conv * keep_two * two_back, axis=(0, 1)),
                jnp.sum(grad_conv * keep_one * one_back, axis=(0, 1)),
                jnp.sum(grad_conv * current, axis=(0, 1)),
            ]
        )
        grad_extended = jnp.pad(kernel_taps[0] * keep_two * grad_conv, ((0, 0), (0, 2), (0, 0)))
        grad_extended = grad_extended + jnp.pad(
            kernel_taps[1] * keep_one * grad_conv, ((0, 0), (1, 1), (0, 0))
        )
        grad_extended = grad_extended + jnp.pad(
            kernel_taps[2] * grad_conv, ((0, 0), (2, 0), (0, 0))
        )
        returned = passed_along(grad_extended[:, :2, :], "seq", -1)
        gated_product_gradient = grad_extended[:, 2:] + jnp.pad(
            returned, ((0, 0), (length - 2, 0), (0, 0))
        )
        grad_projected = jnp.concatenate(
            [
                gated_product_gradient * carry_value,
                output_gate_gradient,
                gated_product_gradient * input_gate_value,
            ],
            axis=-1,
        ).astype(jnp.bfloat16)
        grad_input = weight_grad(normed_low, grad_projected)
        grad_normed = back_dense(grad_projected, input_matrix)
        grad_hidden, grad_gain = norm_back(grad_normed)
        return (gradient + grad_hidden, (grad_gain, grad_input, grad_kernel, grad_output))

    return (result, mixer_backward)


def feed_block(hidden, norm_gain, gate_matrix, up_matrix, down_matrix):
    normed, norm_back = jax.vjp(norm_rows, hidden, norm_gain.astype(jnp.float32))
    normed_low = normed.astype(jnp.bfloat16)
    gate_value = dense(normed_low, gate_matrix)
    upward = dense(normed_low, up_matrix)
    active, active_back = jax.vjp(swiglu, gate_value, upward)
    active_low = active.astype(jnp.bfloat16)
    result = hidden + dense(active_low, down_matrix)

    def feed_backward(gradient):
        gradient_low = gradient.astype(jnp.bfloat16)
        grad_down = weight_grad(active_low, gradient_low)
        grad_gate, grad_upward = active_back(back_dense(gradient_low, down_matrix))
        gate_low = grad_gate.astype(jnp.bfloat16)
        upward_low = grad_upward.astype(jnp.bfloat16)
        grad_normed = back_dense(gate_low, gate_matrix) + back_dense(upward_low, up_matrix)
        grad_hidden, grad_gain = norm_back(grad_normed)
        return (
            gradient + grad_hidden,
            (
                grad_gain,
                weight_grad(normed_low, gate_low),
                weight_grad(normed_low, upward_low),
                grad_down,
            ),
        )

    return (result, feed_backward)


def attend_block(
    hidden,
    lengths,
    norm_gain,
    query_matrix,
    key_matrix,
    value_matrix,
    query_norm,
    key_norm,
    output_matrix,
    segment,
    positions,
    offsets,
):
    row_count, length, feature_columns = hidden.shape
    score_scale = HEAD_DIM ** (-0.5)
    normed, norm_back = jax.vjp(norm_rows, hidden, norm_gain.astype(jnp.float32))
    normed_low = normed.astype(jnp.bfloat16)

    def head_path(projected_rows, head_gain):
        return rotate(norm_rows(projected_rows, head_gain), offsets)

    queries = dense(normed_low, query_matrix).reshape(row_count, length, HEADS, HEAD_DIM)
    keys_raw = dense(normed_low, key_matrix).reshape(row_count, length, KV_HEADS, HEAD_DIM)
    values_raw = dense(normed_low, value_matrix)
    query_rot, query_back = jax.vjp(head_path, queries, query_norm.astype(jnp.float32))
    key_rot, key_back = jax.vjp(head_path, keys_raw, key_norm.astype(jnp.float32))
    query_low = query_rot.astype(jnp.bfloat16).reshape(row_count, length, KV_HEADS, GROUP, HEAD_DIM)
    key_low = key_rot.astype(jnp.bfloat16)
    value_low = values_raw.astype(jnp.bfloat16).reshape(row_count, length, KV_HEADS, HEAD_DIM)
    all_keys, all_values = (
        lax.all_gather(key_low, "seq", axis=1, tiled=True),
        lax.all_gather(value_low, "seq", axis=1, tiled=True),
    )
    total_length = all_keys.shape[1]
    key_block = min(512, total_length)
    block_count = (positions[length - 1] + key_block) // key_block

    def block_scores(number, key_source, value_source):
        first_key = number * key_block
        keys_here = lax.dynamic_slice_in_dim(key_source, first_key, key_block, 1)
        values_here = lax.dynamic_slice_in_dim(value_source, first_key, key_block, 1)
        key_positions = first_key + jnp.arange(key_block, dtype=jnp.int32)
        key_segment, unused = segment_info(lengths, key_positions)
        scores = (
            jnp.einsum(
                "rtkgh,rskh->rkgts", query_low, keys_here, preferred_element_type=jnp.float32
            )
            * score_scale
        )
        allowed = (segment[:, :, None] == key_segment[:, None, :]) & (
            positions[None, :, None] >= key_positions[None, None, :]
        )
        allowed = allowed[:, None, None]
        return (jnp.where(allowed, scores, NEGATIVE), allowed, keys_here, values_here)

    stat_shape = (row_count, KV_HEADS, GROUP, length)

    def stats_step(number, carried):
        peak_score, running_sum = carried
        scores, allowed, unused_keys, unused_values = block_scores(number, all_keys, all_values)
        new_peak = jnp.maximum(peak_score, jnp.max(scores, axis=-1))
        fresh = jnp.sum(jnp.where(allowed, jnp.exp(scores - new_peak[..., None]), 0.0), axis=-1)
        return (new_peak, running_sum * jnp.exp(peak_score - new_peak) + fresh)

    peak_score, running_sum = lax.fori_loop(
        0,
        block_count,
        stats_step,
        (jnp.full(stat_shape, NEGATIVE, jnp.float32), jnp.zeros(stat_shape, jnp.float32)),
    )
    log_total = peak_score + jnp.log(running_sum)

    def probabilities(scores, allowed):
        return jnp.where(allowed, jnp.exp(scores - log_total[..., None]), 0.0)

    out_shape = (row_count, length, KV_HEADS, GROUP, HEAD_DIM)

    def output_step(number, carried):
        rounded, exact_sum = carried
        scores, allowed, keys_here, values_here = block_scores(number, all_keys, all_values)
        weights = probabilities(scores, allowed)
        rounded = rounded + jnp.einsum(
            "rkgts,rskh->rtkgh",
            weights.astype(jnp.bfloat16),
            values_here,
            preferred_element_type=jnp.float32,
        )
        exact_sum = exact_sum + jnp.einsum(
            "rkgts,rskh->rtkgh", weights, values_here.astype(jnp.float32), precision=HIGHEST
        )
        return (rounded, exact_sum)

    rounded, exact_sum = lax.fori_loop(
        0,
        block_count,
        output_step,
        (jnp.zeros(out_shape, jnp.float32), jnp.zeros(out_shape, jnp.float32)),
    )
    attended_low = rounded.reshape(row_count, length, HEADS * HEAD_DIM).astype(jnp.bfloat16)
    result = hidden + dense(attended_low, output_matrix)

    def attend_backward(gradient):
        gradient_low = gradient.astype(jnp.bfloat16)
        grad_output = weight_grad(attended_low, gradient_low)
        grad_attended = (
            back_dense(gradient_low, output_matrix).astype(jnp.bfloat16).reshape(out_shape)
        )
        row_delta = jnp.einsum(
            "rtkgh,rtkgh->rkgt", grad_attended.astype(jnp.float32), exact_sum, precision=HIGHEST
        )
        key_source, value_source = (all_keys, all_values)

        def grad_step(number, carried):
            grad_query, grad_keys, grad_values = carried
            scores, allowed, keys_here, values_here = block_scores(number, key_source, value_source)
            weights = probabilities(scores, allowed)
            grad_weights = jnp.einsum(
                "rtkgh,rskh->rkgts", grad_attended, values_here, preferred_element_type=jnp.float32
            )
            grad_scores = (weights * (grad_weights - row_delta[..., None])).astype(jnp.bfloat16)
            grad_query = (
                grad_query
                + jnp.einsum(
                    "rkgts,rskh->rtkgh", grad_scores, keys_here, preferred_element_type=jnp.float32
                )
                * score_scale
            )
            key_part = (
                jnp.einsum(
                    "rkgts,rtkgh->rskh", grad_scores, query_low, preferred_element_type=jnp.float32
                )
                * score_scale
            )
            value_part = jnp.einsum(
                "rkgts,rtkgh->rskh",
                weights.astype(jnp.bfloat16),
                grad_attended,
                preferred_element_type=jnp.float32,
            )
            grad_keys = lax.dynamic_update_slice_in_dim(grad_keys, key_part, number * key_block, 1)
            grad_values = lax.dynamic_update_slice_in_dim(
                grad_values, value_part, number * key_block, 1
            )
            return (grad_query, grad_keys, grad_values)

        key_shape = (row_count, total_length, KV_HEADS, HEAD_DIM)
        grad_query, grad_keys, grad_values = lax.fori_loop(
            0,
            block_count,
            grad_step,
            (
                jnp.zeros(out_shape, jnp.float32),
                jnp.zeros(key_shape, jnp.float32),
                jnp.zeros(key_shape, jnp.float32),
            ),
        )
        local_keys, local_values = (
            lax.psum_scatter(
                grad_keys.astype(jnp.bfloat16), "seq", scatter_dimension=1, tiled=True
            ).astype(jnp.float32),
            lax.psum_scatter(
                grad_values.astype(jnp.bfloat16), "seq", scatter_dimension=1, tiled=True
            ).astype(jnp.float32),
        )
        grad_queries, grad_query_norm = query_back(
            grad_query.reshape(row_count, length, HEADS, HEAD_DIM)
        )
        grad_keys_raw, grad_key_norm = key_back(local_keys)
        query_grad_low = grad_queries.reshape(row_count, length, HEADS * HEAD_DIM).astype(
            jnp.bfloat16
        )
        key_grad_low = grad_keys_raw.reshape(row_count, length, KV_HEADS * HEAD_DIM).astype(
            jnp.bfloat16
        )
        value_grad_low = local_values.reshape(row_count, length, KV_HEADS * HEAD_DIM).astype(
            jnp.bfloat16
        )
        grad_normed = (
            back_dense(query_grad_low, query_matrix)
            + back_dense(key_grad_low, key_matrix)
            + back_dense(value_grad_low, value_matrix)
        )
        grad_hidden, grad_gain = norm_back(grad_normed)
        return (
            gradient + grad_hidden,
            (
                grad_gain,
                weight_grad(normed_low, query_grad_low),
                weight_grad(normed_low, key_grad_low),
                weight_grad(normed_low, value_grad_low),
                grad_query_norm,
                grad_key_norm,
                grad_output,
            ),
        )

    return (result, attend_backward)


def body(
    tokens,
    lengths,
    mixer_gain,
    mixer_input,
    mixer_kernel,
    mixer_output,
    first_gain,
    first_gate,
    first_up,
    first_down,
    attend_gain,
    query_weight,
    key_weight,
    value_weight,
    query_gain,
    key_gain,
    attend_output,
    second_gain,
    second_gate,
    second_up,
    second_down,
    cotangent,
):
    length = tokens.shape[1]
    positions = lax.axis_index("seq") * length + jnp.arange(length, dtype=jnp.int32)
    segment, seg_start = segment_info(lengths, positions)
    offsets = positions[None, :] - seg_start
    hidden = tokens.astype(jnp.float32)
    hidden, mixer_back = mixer_block(
        hidden, mixer_gain, mixer_input, mixer_kernel, mixer_output, seg_start, positions
    )
    hidden, first_back = feed_block(hidden, first_gain, first_gate, first_up, first_down)
    hidden, attend_back = attend_block(
        hidden,
        lengths,
        attend_gain,
        query_weight,
        key_weight,
        value_weight,
        query_gain,
        key_gain,
        attend_output,
        segment,
        positions,
        offsets,
    )
    hidden, second_back = feed_block(hidden, second_gain, second_gate, second_up, second_down)
    gradient = cotangent.astype(jnp.float32)
    gradient, second_grads = second_back(gradient)
    gradient, attend_grads = attend_back(gradient)
    grad_second_gain, grad_second_gate, grad_second_up, grad_second_down = second_grads
    (
        grad_attend_gain,
        grad_query_weight,
        grad_key_weight,
        grad_value_weight,
        grad_query_gain,
        grad_key_gain,
        grad_attend_output,
    ) = attend_grads
    upper_shares = (
        lax.psum_scatter(
            grad_attend_gain.astype(jnp.bfloat16), "seq", scatter_dimension=0, tiled=True
        ).astype(jnp.float32),
        lax.psum_scatter(
            grad_query_weight.astype(jnp.bfloat16), "seq", scatter_dimension=0, tiled=True
        ).astype(jnp.float32),
        lax.psum_scatter(
            grad_key_weight.astype(jnp.bfloat16), "seq", scatter_dimension=0, tiled=True
        ).astype(jnp.float32),
        lax.psum_scatter(
            grad_value_weight.astype(jnp.bfloat16), "seq", scatter_dimension=0, tiled=True
        ).astype(jnp.float32),
        lax.psum_scatter(
            grad_query_gain.astype(jnp.bfloat16), "seq", scatter_dimension=0, tiled=True
        ).astype(jnp.float32),
        lax.psum_scatter(
            grad_key_gain.astype(jnp.bfloat16), "seq", scatter_dimension=0, tiled=True
        ).astype(jnp.float32),
        lax.psum_scatter(
            grad_attend_output.astype(jnp.bfloat16), "seq", scatter_dimension=0, tiled=True
        ).astype(jnp.float32),
        lax.psum_scatter(
            grad_second_gain.astype(jnp.bfloat16), "seq", scatter_dimension=0, tiled=True
        ).astype(jnp.float32),
        lax.psum_scatter(
            grad_second_gate.astype(jnp.bfloat16), "seq", scatter_dimension=0, tiled=True
        ).astype(jnp.float32),
        lax.psum_scatter(
            grad_second_up.astype(jnp.bfloat16), "seq", scatter_dimension=0, tiled=True
        ).astype(jnp.float32),
        lax.psum_scatter(
            grad_second_down.astype(jnp.bfloat16), "seq", scatter_dimension=0, tiled=True
        ).astype(jnp.float32),
    )
    (
        share_attend_gain,
        share_query_weight,
        share_key_weight,
        share_value_weight,
        share_query_gain,
        share_key_gain,
        share_attend_output,
        share_second_gain,
        share_second_gate,
        share_second_up,
        share_second_down,
    ) = upper_shares
    (
        grad_attend_gain,
        grad_query_weight,
        grad_key_weight,
        grad_value_weight,
        grad_query_gain,
        grad_key_gain,
        grad_attend_output,
        grad_second_gain,
        grad_second_gate,
        grad_second_up,
        grad_second_down,
    ) = (
        lax.psum(share_attend_gain.astype(jnp.bfloat16), "row").astype(jnp.float32),
        lax.psum(share_query_weight.astype(jnp.bfloat16), "row").astype(jnp.float32),
        lax.psum(share_key_weight.astype(jnp.bfloat16), "row").astype(jnp.float32),
        lax.psum(share_value_weight.astype(jnp.bfloat16), "row").astype(jnp.float32),
        lax.psum(share_query_gain.astype(jnp.bfloat16), "row").astype(jnp.float32),
        lax.psum(share_key_gain.astype(jnp.bfloat16), "row").astype(jnp.float32),
        lax.psum(share_attend_output.astype(jnp.bfloat16), "row").astype(jnp.float32),
        lax.psum(share_second_gain.astype(jnp.bfloat16), "row").astype(jnp.float32),
        lax.psum(share_second_gate.astype(jnp.bfloat16), "row").astype(jnp.float32),
        lax.psum(share_second_up.astype(jnp.bfloat16), "row").astype(jnp.float32),
        lax.psum(share_second_down.astype(jnp.bfloat16), "row").astype(jnp.float32),
    )
    gradient, first_grads = first_back(gradient)
    gradient, mixer_grads = mixer_back(gradient)
    grad_first_gain, grad_first_gate, grad_first_up, grad_first_down = first_grads
    grad_mixer_gain, grad_mixer_input, grad_mixer_kernel, grad_mixer_output = mixer_grads
    lower_shares = (
        lax.psum_scatter(
            grad_mixer_gain.astype(jnp.bfloat16), "seq", scatter_dimension=0, tiled=True
        ).astype(jnp.float32),
        lax.psum_scatter(
            grad_mixer_input.astype(jnp.bfloat16), "seq", scatter_dimension=0, tiled=True
        ).astype(jnp.float32),
        lax.psum_scatter(
            grad_mixer_kernel.astype(jnp.bfloat16), "seq", scatter_dimension=1, tiled=True
        ).astype(jnp.float32),
        lax.psum_scatter(
            grad_mixer_output.astype(jnp.bfloat16), "seq", scatter_dimension=0, tiled=True
        ).astype(jnp.float32),
        lax.psum_scatter(
            grad_first_gain.astype(jnp.bfloat16), "seq", scatter_dimension=0, tiled=True
        ).astype(jnp.float32),
        lax.psum_scatter(
            grad_first_gate.astype(jnp.bfloat16), "seq", scatter_dimension=0, tiled=True
        ).astype(jnp.float32),
        lax.psum_scatter(
            grad_first_up.astype(jnp.bfloat16), "seq", scatter_dimension=0, tiled=True
        ).astype(jnp.float32),
        lax.psum_scatter(
            grad_first_down.astype(jnp.bfloat16), "seq", scatter_dimension=0, tiled=True
        ).astype(jnp.float32),
    )
    (
        share_mixer_gain,
        share_mixer_input,
        share_mixer_kernel,
        share_mixer_output,
        share_first_gain,
        share_first_gate,
        share_first_up,
        share_first_down,
    ) = lower_shares
    (
        grad_mixer_gain,
        grad_mixer_input,
        grad_mixer_kernel,
        grad_mixer_output,
        grad_first_gain,
        grad_first_gate,
        grad_first_up,
        grad_first_down,
    ) = (
        lax.psum(share_mixer_gain.astype(jnp.bfloat16), "row").astype(jnp.float32),
        lax.psum(share_mixer_input.astype(jnp.bfloat16), "row").astype(jnp.float32),
        lax.psum(share_mixer_kernel.astype(jnp.bfloat16), "row").astype(jnp.float32),
        lax.psum(share_mixer_output.astype(jnp.bfloat16), "row").astype(jnp.float32),
        lax.psum(share_first_gain.astype(jnp.bfloat16), "row").astype(jnp.float32),
        lax.psum(share_first_gate.astype(jnp.bfloat16), "row").astype(jnp.float32),
        lax.psum(share_first_up.astype(jnp.bfloat16), "row").astype(jnp.float32),
        lax.psum(share_first_down.astype(jnp.bfloat16), "row").astype(jnp.float32),
    )
    return (
        hidden.astype(jnp.bfloat16),
        gradient.astype(jnp.bfloat16),
        grad_mixer_gain,
        grad_mixer_input,
        grad_mixer_kernel,
        grad_mixer_output,
        grad_first_gain,
        grad_first_gate,
        grad_first_up,
        grad_first_down,
        grad_attend_gain,
        grad_query_weight,
        grad_key_weight,
        grad_value_weight,
        grad_query_gain,
        grad_key_gain,
        grad_attend_output,
        grad_second_gain,
        grad_second_gate,
        grad_second_up,
        grad_second_down,
    )


def solution(mesh):
    in_specs = (
        P("row", "seq", None),
        P("row", None),
        P(),
        P(),
        P(),
        P(),
        P(),
        P(),
        P(),
        P(),
        P(),
        P(),
        P(),
        P(),
        P(),
        P(),
        P(),
        P(),
        P(),
        P(),
        P(),
        P("row", "seq", None),
    )
    out_specs = (
        P("row", "seq", None),
        P("row", "seq", None),
        P("seq"),
        P("seq", None),
        P(None, "seq"),
        P("seq", None),
        P("seq"),
        P("seq", None),
        P("seq", None),
        P("seq", None),
        P("seq"),
        P("seq", None),
        P("seq", None),
        P("seq", None),
        P("seq"),
        P("seq"),
        P("seq", None),
        P("seq"),
        P("seq", None),
        P("seq", None),
        P("seq", None),
    )
    return jax.shard_map(body, mesh=mesh, in_specs=in_specs, out_specs=out_specs, check_vma=False)
```

profile of v0, /device:TPU:0, one launch (start us, length us, event | category | flops | bytes accessed | tf_op | source)
XLA Modules:
  0.0 1442.1 jit_solution(16691452383330689882)
XLA Ops:
  44.5 11.6 fusion.82
  61.6 14.2 all-gather.5.cloned.1.call-done
  81.0 25.4 %all-gather.3.cloned.1.call-done = bf16[2,1024,8,64]{1,3,2,0:T(8,128)(2,1)} async-done(((bf16[2,128,8,64]{1,3,2,0:T(8,128)(2,1)}), bf16[2,1024,8,64]{1,3,2,0:T(8,128)(2,1)}) %all-gather.3.cloned.1.call-update) | async-done | bytes 2097168 | tf_op jit(solution)/shard_map/all_gather | solution.py:194
  108.6 12.0 while.48
  130.8 10.5 add_convert_fusion.1
  161.9 13.2 while.49
  212.7 40.9 %reduce-scatter.48.cloned.1.call-done = bf16[128,1024]{1,0:T(8,128)(2,1)} async-done(((bf16[1024,1024]{1,0:T(8,128)(2,1)}), bf16[128,1024]{1,0:T(8,128)(2,1)}) %reduce-scatter.48.cloned.1.call-update) | async-done | bytes 262160
  255.4 43.5 %reduce-scatter.46.cloned.1.call-done = bf16[128,1024]{1,0:T(8,128)(2,1)} async-done(((bf16[1024,1024]{1,0:T(8,128)(2,1)}), bf16[128,1024]{1,0:T(8,128)(2,1)}) %reduce-scatter.46.cloned.1.call-update) | async-done | bytes 262160
  309.1 15.4 %add_convert_fusion = (bf16[2,128,4608]{2,1,0:T(8,128)(2,1)}, bf16[2,128,4608]{2,1,0:T(8,128)(2,1)}) fusion(f32[2,128,4608]{2,1,0:T(8,128)} %copy-done.41, f32[2,128,4608]{2,1,0:T(8,128)} %get-tuple-element.671, bf16[4608,1024]{1,0:T(8,128)(2,1)} %param.37, f32[2,128,1024]{2,1,0:T(8,128)S(1)} %fusion.153), kind=kOutput, calls=%fused_computation.127 | convolution fusion | flops 2435055616 | bytes 24641536 | tf_op jit(solution)/shard_map/rtf,df->rtd/dot_general | solution.py:63
  326.0 8.2 fusion.98
  334.5 7.6 multiply_reduce_fusion.3
  360.0 6.8 bitcast_convert_fusion.2
  366.8 7.1 bitcast_convert_fusion.1
  375.0 6.8 bitcast_convert_fusion
  383.0 6.9 bitcast_convert_fusion.3
  390.9 6.8 bitcast_convert_fusion.5
  397.8 6.8 bitcast_convert_fusion.4
  405.8 21.5 %reduce-scatter.36.cloned.1.call-done = bf16[128,512]{1,0:T(8,128)(2,1)} async-done(((bf16[1024,512]{1,0:T(8,128)(2,1)}), bf16[128,512]{1,0:T(8,128)(2,1)}) %reduce-scatter.36.cloned.1.call-update) | async-done | bytes 131088 | tf_op jit(solution)/shard_map/reduce_scatter | solution.py:433
  427.3 39.2 %reduce-scatter.34.cloned.1.call-done = bf16[128,512]{1,0:T(8,128)(2,1)} async-done(((bf16[1024,512]{1,0:T(8,128)(2,1)}), bf16[128,512]{1,0:T(8,128)(2,1)}) %reduce-scatter.34.cloned.1.call-update) | async-done | bytes 131088 | tf_op jit(solution)/shard_map/reduce_scatter | solution.py:430
  466.5 44.5 %reduce-scatter.24.cloned.1.call-done = bf16[128,1024]{1,0:T(8,128)(2,1)} async-done(((bf16[1024,1024]{1,0:T(8,128)(2,1)}), bf16[128,1024]{1,0:T(8,128)(2,1)}) %reduce-scatter.24.cloned.1.call-update) | async-done | bytes 262160 | tf_op jit(solution)/shard_map/reduce_scatter | solution.py:510
  511.0 65.4 %reduce-scatter.22.cloned.1.call-done = bf16[128,3072]{1,0:T(8,128)(2,1)} async-done(((bf16[1024,3072]{1,0:T(8,128)(2,1)}), bf16[128,3072]{1,0:T(8,128)(2,1)}) %reduce-scatter.22.cloned.1.call-update) | async-done | bytes 786448 | tf_op jit(solution)/shard_map/reduce_scatter | solution.py:504
  576.4 80.0 %reduce-scatter.40.cloned.1.call-done = bf16[128,4608]{1,0:T(8,128)(2,1)} async-done(((bf16[1024,4608]{1,0:T(8,128)(2,1)}), bf16[128,4608]{1,0:T(8,128)(2,1)}) %reduce-scatter.40.cloned.1.call-update) | async-done | bytes 1179664 | tf_op jit(solution)/shard_map/reduce_scatter | solution.py:448
  656.3 79.9 %reduce-scatter.42.cloned.1.call-done = bf16[128,4608]{1,0:T(8,128)(2,1)} async-done(((bf16[1024,4608]{1,0:T(8,128)(2,1)}), bf16[128,4608]{1,0:T(8,128)(2,1)}) %reduce-scatter.42.cloned.1.call-update) | async-done | bytes 1179664 | tf_op jit(solution)/shard_map/reduce_scatter | solution.py:451
  736.2 80.0 %reduce-scatter.44.cloned.1.call-done = bf16[576,1024]{1,0:T(8,128)(2,1)} async-done(((bf16[4608,1024]{1,0:T(8,128)(2,1)}), bf16[576,1024]{1,0:T(8,128)(2,1)}) %reduce-scatter.44.cloned.1.call-update) | async-done | bytes 1179664 | tf_op jit(solution)/shard_map/reduce_scatter | solution.py:454
  816.2 79.9 %reduce-scatter.30.cloned.1.call-done = bf16[576,1024]{1,0:T(8,128)(2,1)} async-done(((bf16[4608,1024]{1,0:T(8,128)(2,1)}), bf16[576,1024]{1,0:T(8,128)(2,1)}) %reduce-scatter.30.cloned.1.call-update) | async-done | bytes 1179664 | tf_op jit(solution)/shard_map/reduce_scatter | solution.py:522
  896.1 79.9 %reduce-scatter.26.cloned.1.call-done = bf16[128,4608]{1,0:T(8,128)(2,1)} async-done(((bf16[1024,4608]{1,0:T(8,128)(2,1)}), bf16[128,4608]{1,0:T(8,128)(2,1)}) %reduce-scatter.26.cloned.1.call-update) | async-done | bytes 1179664 | tf_op jit(solution)/shard_map/reduce_scatter | solution.py:516
  975.9 79.9 %reduce-scatter.28.cloned.1.call-done = bf16[128,4608]{1,0:T(8,128)(2,1)} async-done(((bf16[1024,4608]{1,0:T(8,128)(2,1)}), bf16[128,4608]{1,0:T(8,128)(2,1)}) %reduce-scatter.28.cloned.1.call-update) | async-done | bytes 1179664 | tf_op jit(solution)/shard_map/reduce_scatter | solution.py:519
  1058.3 7.8 fusion.139
  1066.1 26.8 %reduce-scatter.50.cloned.1.call-done = bf16[128,3]{1,0:T(8,128)(2,1)} async-done(((bf16[1024,3]{1,0:T(8,128)(2,1)}), bf16[128,3]{1,0:T(8,128)(2,1)}) %reduce-scatter.50.cloned.1.call-update) | async-done | bytes 784
  1100.1 13.1 all-reduce.14
  1113.7 12.1 all-reduce.15
  1132.0 281.6 %all-reduce.19.cloned.1.call-done = (bf16[128,3072]{1,0:T(8,128)(2,1)}, bf16[128,1024]{1,0:T(8,128)(2,1)}, bf16[128,4608]{1,0:T(8,128)(2,1)}, bf16[128,4608]{1,0...) async-done(((bf16[128,3072]{1,0:T(8,128)(2,1)}, ...) | async-done | bytes 8912912 | tf_op jit(solution)/shard_map/psum | solution.py:547
  (479 shorter events, 217.6 us)
Async XLA Ops:
  7.2 50.2 %copy-start = (bf16[1024,1024]{1,0:T(8,128)(2,1)S(1)}, bf16[1024,1024]{1,0:T(8,128)(2,1)}, u32[]{:S(2)}) copy-start(bf16[1024,1024]{1,0:T(8,128)(2,1)} %param.39) | copy-start | bytes 6291460
  7.2 68.5 %all-gather.5.cloned.1.call-start = ((), (), s32[]{:S(2)}) async-start(), calls=%async_computation.16 | async-start | bytes 2359296 | tf_op jit(solution)/shard_map/all_gather | solution.py:193
  16.7 3.3 collective-permute-start
  19.7 39.9 %copy-start.66 = (f32[2,128,32]{1,2,0:T(8,128)}, f32[2,128,32]{1,2,0:T(8,128)S(1)}, u32[]{:S(2)}) copy-start(f32[2,128,32]{1,2,0:T(8,128)S(1)} %get-tuple-element.664) | copy-start | bytes 98308
  19.8 39.9 %copy-start.68 = (f32[2,128,32]{1,2,0:T(8,128)}, f32[2,128,32]{1,2,0:T(8,128)S(1)}, u32[]{:S(2)}) copy-start(f32[2,128,32]{1,2,0:T(8,128)S(1)} %get-tuple-element.665) | copy-start | bytes 98308
  19.8 21.3 %copy-start.106 = (f32[64]{0:T(128)}, f32[64]{0:T(128)S(1)}, u32[]{:S(2)}) copy-start(f32[64]{0:T(128)S(1)} %convert_element_type.355) | copy-start | bytes 772
  19.9 19.6 %copy-start.81 = (f32[1024]{0:T(1024)}, f32[1024]{0:T(1024)S(1)}, u32[]{:S(2)}) copy-start(f32[1024]{0:T(1024)S(1)} %convert_element_type.351) | copy-start | bytes 12292
  42.9 63.5 %all-gather.3.cloned.1.call-start = ((), (), s32[]{:S(2)}) async-start(), calls=%async_computation.15 | async-start | bytes 2359296 | tf_op jit(solution)/shard_map/all_gather | solution.py:194
  60.5 193.1 %reduce-scatter.48.cloned.1.call-start = ((), (), s32[]{:S(2)}) async-start(), calls=%async_computation.30 | async-start | bytes 2359296
  124.9 27.1 %copy-start.27 = (f32[2,128,1024]{2,1,0:T(8,128)}, f32[2,128,1024]{2,1,0:T(8,128)S(1)}, u32[]{:S(2)}) copy-start(f32[2,128,1024]{2,1,0:T(8,128)S(1)} %get-tuple-element.679) | copy-start | bytes 3145732
  187.8 111.1 %reduce-scatter.46.cloned.1.call-start = ((), (), s32[]{:S(2)}) async-start(), calls=%async_computation.29 | async-start | bytes 2359296
  200.7 205.0 %reduce-scatter.32.cloned.1.call-start = ((), (), s32[]{:S(2)}) async-start(), calls=%async_computation.22 | async-start | bytes 2359296 | tf_op jit(solution)/shard_map/reduce_scatter | solution.py:427
  206.4 199.3 %reduce-scatter.38.cloned.1.call-start = ((), (), s32[]{:S(2)}) async-start(), calls=%async_computation.25 | async-start | bytes 2359296 | tf_op jit(solution)/shard_map/reduce_scatter | solution.py:442
  209.8 92.8 %copy-start.19 = (f32[2,128,512]{1,2,0:T(8,128)S(1)}, f32[2,128,512]{1,2,0:T(8,128)}, u32[]{:S(2)}) copy-start(f32[2,128,512]{1,2,0:T(8,128)} %copy-done.18) | copy-start | bytes 1572868
  209.8 92.8 %copy-start.78 = (f32[2,128,8]{1,2,0:T(8,128)S(1)}, f32[2,128,8]{1,2,0:T(8,128)}, u32[]{:S(2)}) copy-start(f32[2,128,8]{1,2,0:T(8,128)} %copy-done.77) | copy-start | bytes 24580
  209.8 92.8 %copy-start.107 = (f32[64]{0:T(128)S(1)}, f32[64]{0:T(128)}, u32[]{:S(2)}) copy-start(f32[64]{0:T(128)} %copy-done.106) | copy-start | bytes 772
  209.8 217.4 %reduce-scatter.36.cloned.1.call-start = ((), (), s32[]{:S(2)}) async-start(), calls=%async_computation.24 | async-start | bytes 1179648 | tf_op jit(solution)/shard_map/reduce_scatter | solution.py:433
  212.7 90.2 %copy-start.80 = (f32[2,128,8]{1,2,0:T(8,128)S(1)}, f32[2,128,8]{1,2,0:T(8,128)}, u32[]{:S(2)}) copy-start(f32[2,128,8]{1,2,0:T(8,128)} %copy-done.79) | copy-start | bytes 24580
  306.9 159.6 %reduce-scatter.34.cloned.1.call-start = ((), (), s32[]{:S(2)}) async-start(), calls=%async_computation.23 | async-start | bytes 1179648 | tf_op jit(solution)/shard_map/reduce_scatter | solution.py:430
  334.2 176.8 %reduce-scatter.24.cloned.1.call-start = ((), (), s32[]{:S(2)}) async-start(), calls=%async_computation.18 | async-start | bytes 2359296 | tf_op jit(solution)/shard_map/reduce_scatter | solution.py:510
  345.6 230.7 %reduce-scatter.22.cloned.1.call-start = ((), (), s32[]{:S(2)}) async-start(), calls=%async_computation.17 | async-start | bytes 7077888 | tf_op jit(solution)/shard_map/reduce_scatter | solution.py:504
  349.7 3.2 collective-permute-start.1
  359.0 297.4 %reduce-scatter.40.cloned.1.call-start = ((), (), s32[]{:S(2)}) async-start(), calls=%async_computation.26 | async-start | bytes 10616832 | tf_op jit(solution)/shard_map/reduce_scatter | solution.py:448
  366.8 369.4 %reduce-scatter.42.cloned.1.call-start = ((), (), s32[]{:S(2)}) async-start(), calls=%async_computation.27 | async-start | bytes 10616832 | tf_op jit(solution)/shard_map/reduce_scatter | solution.py:451
  374.0 442.3 %reduce-scatter.44.cloned.1.call-start = ((), (), s32[]{:S(2)}) async-start(), calls=%async_computation.28 | async-start | bytes 10616832 | tf_op jit(solution)/shard_map/reduce_scatter | solution.py:454
  381.8 514.3 %reduce-scatter.30.cloned.1.call-start = ((), (), s32[]{:S(2)}) async-start(), calls=%async_computation.21 | async-start | bytes 10616832 | tf_op jit(solution)/shard_map/reduce_scatter | solution.py:522
  389.9 586.0 %reduce-scatter.26.cloned.1.call-start = ((), (), s32[]{:S(2)}) async-start(), calls=%async_computation.19 | async-start | bytes 10616832 | tf_op jit(solution)/shard_map/reduce_scatter | solution.py:516
  397.8 658.0 %reduce-scatter.28.cloned.1.call-start = ((), (), s32[]{:S(2)}) async-start(), calls=%async_computation.20 | async-start | bytes 10616832 | tf_op jit(solution)/shard_map/reduce_scatter | solution.py:519
  404.6 688.3 %reduce-scatter.50.cloned.1.call-start = ((), (), s32[]{:S(2)}) async-start(), calls=%async_computation.31 | async-start | bytes 294912
  405.7 1007.9 %all-reduce.19.cloned.1.call-start = ((), (), s32[]{:S(2)}) async-start(), calls=%async_computation.32 | async-start | bytes 17825792 | tf_op jit(solution)/shard_map/psum | solution.py:547
  1093.7 35.7 %copy-start.101 = (f32[2,128]{1,0:T(2,128)S(1)}, f32[2,128]{1,0:T(2,128)}, u32[]{:S(2)}) copy-start(f32[2,128]{1,0:T(2,128)} %copy-done.100) | copy-start | bytes 3076
  1093.7 35.7 %copy-start.17 = (f32[2,128,1024]{2,1,0:T(8,128)S(1)}, f32[2,128,1024]{2,1,0:T(8,128)}, u32[]{:S(2)}) copy-start(f32[2,128,1024]{2,1,0:T(8,128)} %copy-done.16) | copy-start | bytes 3145732
  (123 other events, 581.5 us)
Sparse Core Ops, SparseCore 0:
  43.0 32.6 all-gather.4
  78.2 28.1 all-gather.2
  187.9 65.5 reduce-scatter.47
  257.6 41.2 reduce-scatter.45
  302.0 41.1 reduce-scatter.31
  346.8 41.2 reduce-scatter.37
  391.2 36.0 reduce-scatter.35
  430.4 35.9 reduce-scatter.33
  469.7 41.1 reduce-scatter.23
  514.6 61.7 reduce-scatter.21
  579.9 76.4 reduce-scatter.39
  659.7 76.4 reduce-scatter.41
  739.7 76.4 reduce-scatter.43
  819.6 76.4 reduce-scatter.29
  899.4 76.4 reduce-scatter.25
  979.3 76.4 reduce-scatter.27
  1059.2 33.6 reduce-scatter.49
  1097.6 315.8 all-reduce.18
where the time goes:
time: 1450 us; the launch traced here: 1440 us
  waiting for transfers between devices  1080 us (74%)
  matrix products  196 us (14%)
  local copies, waits for them, and re-layouts  59.8 us (4%)
  other arithmetic  51.8 us (4%)
  blocking collectives  25.2 us (2%)
  between operations  18.6 us (1%)
    psum x1, waiting for transfers between devices, body(): lax.psum(share_mixer_input.astype(jnp.bfloat16), 'row').astype(jnp.float32)  282 us
    unnamed x21, waiting for transfers between devices  111 us
    reduce_scatter x1, waiting for transfers between devices, body(): lax.psum_scatter(grad_second_down.astype(jnp.bfloat16), 'seq', scatter_di...  80 us
    reduce_scatter x1, waiting for transfers between devices, body(): lax.psum_scatter(grad_second_gate.astype(jnp.bfloat16), 'seq', scatter_di...  80 us
    reduce_scatter x1, waiting for transfers between devices, body(): lax.psum_scatter(grad_first_down.astype(jnp.bfloat16), 'seq', scatter_dim...  79.9 us
    reduce_scatter x1, waiting for transfers between devices, body(): lax.psum_scatter(grad_second_up.astype(jnp.bfloat16), 'seq', scatter_dime...  79.9 us
    reduce_scatter x1, waiting for transfers between devices, body(): lax.psum_scatter(grad_first_up.astype(jnp.bfloat16), 'seq', scatter_dimen...  79.9 us
    reduce_scatter x1, waiting for transfers between devices, body(): lax.psum_scatter(grad_first_gate.astype(jnp.bfloat16), 'seq', scatter_dim...  79.9 us
  transfers between devices with their start and end apart: 20, of which 18 were waited for; matrix products, arithmetic and copies ran while one was open for 11% of the time, Pallas kernels for 0%

commit v1 on v0

--- a/solution.py
+++ b/solution.py
@@ -1,6 +1,11 @@
+import functools
+import math
+
 import jax
 import jax.numpy as jnp
 from jax import lax
+from jax.experimental import pallas as pl
+from jax.experimental.pallas import tpu as pltpu
 from jax.sharding import PartitionSpec as P
 
 HEADS = 16
@@ -13,6 +18,10 @@
 THETA = 1000000.0
 NEGATIVE = -1e30
 HIGHEST = lax.Precision.HIGHEST
+MESH = pl.DeviceIdType.MESH
+COLS = 512
+SLOTS = 4
+ZSLOTS = 8
 
 
 def passed_along(value, axis, steps):
@@ -56,7 +65,7 @@
 
 
 def weight_grad(inputs, gradient):
-    return jnp.einsum("rtd,rtf->df", inputs, gradient, preferred_element_type=jnp.float32)
+    return (inputs, gradient)
 
 
 def back_dense(gradient, matrix):
@@ -150,8 +159,7 @@
             gradient + grad_hidden,
             (
                 grad_gain,
-                weight_grad(normed_low, gate_low),
-                weight_grad(normed_low, upward_low),
+                weight_grad(normed_low, jnp.concatenate([gate_low, upward_low], axis=-1)),
                 grad_down,
             ),
         )
@@ -347,9 +355,10 @@
             gradient + grad_hidden,
             (
                 grad_gain,
-                weight_grad(normed_low, query_grad_low),
-                weight_grad(normed_low, key_grad_low),
-                weight_grad(normed_low, value_grad_low),
+                weight_grad(
+                    normed_low,
+                    jnp.concatenate([query_grad_low, key_grad_low, value_grad_low], axis=-1),
+                ),
                 grad_query_norm,
                 grad_key_norm,
                 grad_output,
@@ -357,6 +366,300 @@
         )
 
     return (result, attend_backward)
+
+
+def reduce_entries(pairs, shards, rows, block_rows):
+    entries = []
+    x_first = g_first = chunk = 0
+    for x, g in pairs:
+        x_count = x.shape[2]
+        g_count = g.shape[1] // COLS
+        entries.append((x_first, x_count, g_first, g_count, chunk))
+        x_first += x_count
+        g_first += g_count
+        chunk += x_count * g_count
+    return entries, x_first, g_first, chunk
+
+
+def locate(entries, q):
+    x_block, g_block = jnp.int32(0), jnp.int32(0)
+    for x_first, x_count, g_first, g_count, chunk in entries:
+        here = q - chunk
+        inside = here >= 0
+        x_block = jnp.where(inside, x_first + lax.rem(jnp.maximum(here, 0), x_count), x_block)
+        g_block = jnp.where(inside, g_first + jnp.maximum(here, 0) // x_count, g_block)
+    return x_block, g_block
+
+
+def seq_steps(bits):
+    upper = list(range(1, bits))
+    middle = (len(upper) + 1) // 2
+    kinds = []
+    for order in (upper, upper[middle:] + upper[:middle]):
+        held = sorted(upper, reverse=True)
+        steps = []
+        for bit in order:
+            place = held.index(bit)
+            steps.append((bit, 2**place, 2 ** (len(held) - 1 - place)))
+            held.remove(bit)
+        kinds.append(steps)
+    return kinds
+
+
+def reduce_kernel(entries, row_count, shards, chunks, *refs):
+    count = len(entries)
+    xs, gs = refs[:count], refs[count : 2 * count]
+    out = refs[2 * count]
+    (load_x, load_g, x_all, g_all, send_zero, recv_zero, *rest) = refs[2 * count + 1 :]
+    bits = shards.bit_length() - 1
+    kinds = seq_steps(bits)
+    held, received = [[], []], [[], []]
+    for kind in range(2):
+        for _ in kinds[kind]:
+            held[kind].append(rest.pop(0))
+            received[kind].append(rest.pop(0))
+    z_own, z_in, z_part, z_cross, z_total = rest[:5]
+    seq_send, seq_recv, z_send, z_recv, out_sem = rest[5:]
+    row, seq = lax.axis_index("row"), lax.axis_index("seq")
+    bit_value = [lax.rem(seq // (1 << bit), 2) for bit in range(bits)]
+    partner = [seq + (1 << bit) * (1 - 2 * bit_value[bit]) for bit in range(bits)]
+    pairs = chunks // 2
+
+    for at, (x_first, x_count, g_first, g_count, _) in enumerate(entries):
+        pltpu.make_async_copy(
+            xs[at], x_all.at[:, :, pl.ds(x_first, x_count)], load_x.at[at]
+        ).start()
+        pltpu.make_async_copy(
+            gs[at], g_all.at[:, pl.ds(g_first * COLS, g_count * COLS)], load_g.at[at]
+        ).start()
+
+    barrier = pltpu.get_barrier_semaphore()
+    for bit in range(bits):
+        pl.semaphore_signal(barrier, inc=1, device_id=(row, partner[bit]), device_id_type=MESH)
+    for step in (1, row_count - 1):
+        pl.semaphore_signal(
+            barrier, inc=1, device_id=(lax.rem(row + step, row_count), seq), device_id_type=MESH
+        )
+    pl.semaphore_wait(barrier, bits + 2)
+
+    for at, (x_first, x_count, g_first, g_count, _) in enumerate(entries):
+        pltpu.make_async_copy(
+            xs[at], x_all.at[:, :, pl.ds(x_first, x_count)], load_x.at[at]
+        ).wait()
+        pltpu.make_async_copy(
+            gs[at], g_all.at[:, pl.ds(g_first * COLS, g_count * COLS)], load_g.at[at]
+        ).wait()
+
+    def product(q, side):
+        x_block, g_block = locate(entries, q)
+        left = x_all[:, side, x_block]
+        columns = pl.ds(pl.multiple_of(g_block * COLS, COLS), COLS)
+        return jnp.dot(
+            left.reshape(left.shape[0] * left.shape[1], left.shape[2]),
+            g_all[:, columns],
+            preferred_element_type=jnp.float32,
+        )
+
+    def seq_copy(kind, step, slot):
+        if step == 0:
+            bit = 0
+            source, target = send_zero.at[kind, slot], recv_zero.at[kind, slot]
+        else:
+            bit = kinds[kind][step - 1][0]
+            source = held[kind][step - 1].at[slot, :, 1 - bit_value[bit]]
+            target = received[kind][step - 1].at[slot]
+        return pltpu.make_async_remote_copy(
+            src_ref=source,
+            dst_ref=target,
+            send_sem=seq_send.at[kind, step, slot],
+            recv_sem=seq_recv.at[kind, step, slot],
+            device_id=(row, partner[bit]),
+            device_id_type=MESH,
+        )
+
+    def seq_sum(kind, step, slot, q):
+        if step == 1:
+            mine = product(q, bit_value[0])
+            other = recv_zero[kind, slot].astype(jnp.float32)
+            return mine + other.reshape(mine.shape)
+        bit = kinds[kind][step - 2][0]
+        mine = held[kind][step - 2][slot, :, bit_value[bit]].astype(jnp.float32)
+        return mine + received[kind][step - 2][slot].astype(jnp.float32)
+
+    half = row_count // 2
+    depth = half - 1
+    lower = row < half
+    level = jnp.where(lower, row, row_count - 1 - row)
+    toward = jnp.where(lower, row + 1, row - 1)
+    away = jnp.where(lower, row - 1, row + 1)
+
+    def z_copy(kind, step, slot):
+        if step < depth:
+            source = z_own if step == 0 else z_part
+            target, where = z_in, toward
+        elif step == depth:
+            source = z_own if depth == 0 else z_part
+            target, where = z_cross, toward
+        else:
+            source, target, where = z_total, z_total, away
+        return pltpu.make_async_remote_copy(
+            src_ref=source.at[kind, slot],
+            dst_ref=target.at[kind, slot],
+            send_sem=z_send.at[kind, step, slot],
+            recv_sem=z_recv.at[kind, step, slot],
+            device_id=(where, seq),
+            device_id_type=MESH,
+        )
+
+    def out_copy(kind, slot, q):
+        return pltpu.make_async_copy(z_total.at[kind, slot], out.at[q], out_sem.at[kind, slot])
+
+    def each(stage, i, run):
+        index = i - stage
+
+        @pl.when(jnp.logical_and(index >= 0, index < pairs))
+        def _():
+            for kind in range(2):
+                run(kind, index, 2 * index + kind)
+
+    def first(kind, index, q):
+        slot = lax.rem(index, SLOTS)
+        send_zero[kind, slot] = product(q, 1 - bit_value[0]).astype(jnp.bfloat16).reshape(
+            send_zero.shape[2:]
+        )
+        seq_copy(kind, 0, slot).start()
+
+    def middle(step):
+        def run(kind, index, q):
+            slot = lax.rem(index, SLOTS)
+            seq_copy(kind, step - 1, slot).wait()
+            total = seq_sum(kind, step, slot, q)
+            target = held[kind][step - 1]
+            target[slot] = total.astype(jnp.bfloat16).reshape(target.shape[1:])
+            seq_copy(kind, step, slot).start()
+
+        return run
+
+    def last(kind, index, q):
+        slot, z_slot = lax.rem(index, SLOTS), lax.rem(index, ZSLOTS)
+        seq_copy(kind, bits - 1, slot).wait()
+        total = seq_sum(kind, bits, slot, q)
+        z_own[kind, z_slot] = total.astype(jnp.bfloat16).reshape(z_own.shape[2:])
+
+        @pl.when(level == 0)
+        def _():
+            z_copy(kind, 0, z_slot).start()
+
+    def z_stage(step):
+        def run(kind, index, q):
+            slot = lax.rem(index, ZSLOTS)
+            if step <= depth:
+
+                @pl.when(level == step)
+                def _():
+                    z_copy(kind, step - 1, slot).wait_recv()
+                    z_part[kind, slot] = (
+                        z_own[kind, slot].astype(jnp.float32) + z_in[kind, slot].astype(jnp.float32)
+                    ).astype(jnp.bfloat16)
+                    z_copy(kind, step, slot).start()
+
+                @pl.when(level == step - 1)
+                def _():
+                    z_copy(kind, step - 1, slot).wait_send()
+
+            elif step == depth + 1:
+
+                @pl.when(level == depth)
+                def _():
+                    z_copy(kind, depth, slot).wait()
+                    own = z_own if depth == 0 else z_part
+                    z_total[kind, slot] = (
+                        own[kind, slot].astype(jnp.float32) + z_cross[kind, slot].astype(jnp.float32)
+                    ).astype(jnp.bfloat16)
+                    if depth > 0:
+                        z_copy(kind, step, slot).start()
+                    out_copy(kind, slot, q).start()
+
+            else:
+                receiver = 2 * depth + 1 - step
+
+                @pl.when(level == receiver)
+                def _():
+                    z_copy(kind, step - 1, slot).wait_recv()
+                    if receiver > 0:
+                        z_copy(kind, step, slot).start()
+                    out_copy(kind, slot, q).start()
+
+                @pl.when(level == receiver + 1)
+                def _():
+                    z_copy(kind, step - 1, slot).wait_send()
+
+        return run
+
+    def finish(kind, index, q):
+        out_copy(kind, lax.rem(index, ZSLOTS), q).wait()
+
+    stages = [first]
+    stages += [middle(step) for step in range(1, bits)]
+    stages += [last]
+    stages += [z_stage(step) for step in range(1, 2 * depth + 2)]
+    stages += [finish]
+
+    def iteration(i, carried):
+        for stage, run in enumerate(stages):
+            each(stage, i, run)
+        return carried
+
+    lax.fori_loop(0, pairs + len(stages) - 1, iteration, 0)
+
+
+def reduce_gradients(pairs, row_count, shards, collective_id):
+    block_rows, tokens = pairs[0][0].shape[3:]
+    entries, x_blocks, g_blocks, chunks = reduce_entries(pairs, shards, row_count, block_rows)
+    bits = shards.bit_length() - 1
+    block = (block_rows, COLS)
+    comm = []
+    for steps in seq_steps(bits):
+        for _, above, below in steps:
+            comm.append(pltpu.VMEM((SLOTS, above, 2, below) + block, jnp.bfloat16))
+            comm.append(pltpu.VMEM((SLOTS, above, below) + block, jnp.bfloat16))
+    z_steps = row_count - 1
+    result = pl.pallas_call(
+        functools.partial(reduce_kernel, entries, row_count, shards, chunks),
+        out_shape=jax.ShapeDtypeStruct((chunks,) + block, jnp.bfloat16),
+        in_specs=[pl.BlockSpec(memory_space=pl.ANY)] * (2 * len(pairs)),
+        out_specs=pl.BlockSpec(memory_space=pl.ANY),
+        scratch_shapes=[
+            pltpu.SemaphoreType.DMA((len(pairs),)),
+            pltpu.SemaphoreType.DMA((len(pairs),)),
+            pltpu.VMEM((shards // 2, 2, x_blocks, block_rows, tokens), jnp.bfloat16),
+            pltpu.VMEM((tokens, g_blocks * COLS), jnp.bfloat16),
+            pltpu.VMEM((2, SLOTS, shards // 2) + block, jnp.bfloat16),
+            pltpu.VMEM((2, SLOTS, shards // 2) + block, jnp.bfloat16),
+            *comm,
+            *[pltpu.VMEM((2, ZSLOTS) + block, jnp.bfloat16) for _ in range(5)],
+            pltpu.SemaphoreType.DMA((2, bits, SLOTS)),
+            pltpu.SemaphoreType.DMA((2, bits, SLOTS)),
+            pltpu.SemaphoreType.DMA((2, z_steps, ZSLOTS)),
+            pltpu.SemaphoreType.DMA((2, z_steps, ZSLOTS)),
+            pltpu.SemaphoreType.DMA((2, ZSLOTS)),
+        ],
+        compiler_params=pltpu.CompilerParams(
+            collective_id=collective_id, has_side_effects=True, vmem_limit_bytes=52 * 2**20
+        ),
+        cost_estimate=pl.CostEstimate(
+            flops=2 * chunks * shards * block_rows * COLS * tokens,
+            bytes_accessed=2 * chunks * block_rows * COLS,
+            transcendentals=0,
+        ),
+    )(*[x for x, _ in pairs], *[g for _, g in pairs])
+    pieces = []
+    for _, x_count, _, g_count, chunk in entries:
+        piece = result[chunk : chunk + x_count * g_count].reshape((g_count, x_count) + block)
+        pieces.append(
+            piece.transpose(1, 2, 0, 3).reshape(x_count * block_rows, g_count * COLS)
+        )
+    return pieces
 
 
 def body(
@@ -410,170 +713,110 @@
     gradient = cotangent.astype(jnp.float32)
     gradient, second_grads = second_back(gradient)
     gradient, attend_grads = attend_back(gradient)
-    grad_second_gain, grad_second_gate, grad_second_up, grad_second_down = second_grads
-    (
-        grad_attend_gain,
-        grad_query_weight,
-        grad_key_weight,
-        grad_value_weight,
-        grad_query_gain,
-        grad_key_gain,
-        grad_attend_output,
-    ) = attend_grads
-    upper_shares = (
-        lax.psum_scatter(
-            grad_attend_gain.astype(jnp.bfloat16), "seq", scatter_dimension=0, tiled=True
-        ).astype(jnp.float32),
-        lax.psum_scatter(
-            grad_query_weight.astype(jnp.bfloat16), "seq", scatter_dimension=0, tiled=True
-        ).astype(jnp.float32),
-        lax.psum_scatter(
-            grad_key_weight.astype(jnp.bfloat16), "seq", scatter_dimension=0, tiled=True
-        ).astype(jnp.float32),
-        lax.psum_scatter(
-            grad_value_weight.astype(jnp.bfloat16), "seq", scatter_dimension=0, tiled=True
-        ).astype(jnp.float32),
-        lax.psum_scatter(
-            grad_query_gain.astype(jnp.bfloat16), "seq", scatter_dimension=0, tiled=True
-        ).astype(jnp.float32),
-        lax.psum_scatter(
-            grad_key_gain.astype(jnp.bfloat16), "seq", scatter_dimension=0, tiled=True
-        ).astype(jnp.float32),
-        lax.psum_scatter(
-            grad_attend_output.astype(jnp.bfloat16), "seq", scatter_dimension=0, tiled=True
-        ).astype(jnp.float32),
-        lax.psum_scatter(
-            grad_second_gain.astype(jnp.bfloat16), "seq", scatter_dimension=0, tiled=True
-        ).astype(jnp.float32),
-        lax.psum_scatter(
-            grad_second_gate.astype(jnp.bfloat16), "seq", scatter_dimension=0, tiled=True
-        ).astype(jnp.float32),
-        lax.psum_scatter(
-            grad_second_up.astype(jnp.bfloat16), "seq", scatter_dimension=0, tiled=True
-        ).astype(jnp.float32),
-        lax.psum_scatter(
-            grad_second_down.astype(jnp.bfloat16), "seq", scatter_dimension=0, tiled=True
-        ).astype(jnp.float32),
-    )
-    (
-        share_attend_gain,
-        share_query_weight,
-        share_key_weight,
-        share_value_weight,
-        share_query_gain,
-        share_key_gain,
-        share_attend_output,
-        share_second_gain,
-        share_second_gate,
-        share_second_up,
-        share_second_down,
-    ) = upper_shares
-    (
-        grad_attend_gain,
-        grad_query_weight,
-        grad_key_weight,
-        grad_value_weight,
-        grad_query_gain,
-        grad_key_gain,
-        grad_attend_output,
-        grad_second_gain,
-        grad_second_gate,
-        grad_second_up,
-        grad_second_down,
-    ) = (
-        lax.psum(share_attend_gain.astype(jnp.bfloat16), "row").astype(jnp.float32),
-        lax.psum(share_query_weight.astype(jnp.bfloat16), "row").astype(jnp.float32),
-        lax.psum(share_key_weight.astype(jnp.bfloat16), "row").astype(jnp.float32),
-        lax.psum(share_value_weight.astype(jnp.bfloat16), "row").astype(jnp.float32),
-        lax.psum(share_query_gain.astype(jnp.bfloat16), "row").astype(jnp.float32),
-        lax.psum(share_key_gain.astype(jnp.bfloat16), "row").astype(jnp.float32),
-        lax.psum(share_attend_output.astype(jnp.bfloat16), "row").astype(jnp.float32),
-        lax.psum(share_second_gain.astype(jnp.bfloat16), "row").astype(jnp.float32),
-        lax.psum(share_second_gate.astype(jnp.bfloat16), "row").astype(jnp.float32),
-        lax.psum(share_second_up.astype(jnp.bfloat16), "row").astype(jnp.float32),
-        lax.psum(share_second_down.astype(jnp.bfloat16), "row").astype(jnp.float32),
-    )
     gradient, first_grads = first_back(gradient)
     gradient, mixer_grads = mixer_back(gradient)
-    grad_first_gain, grad_first_gate, grad_first_up, grad_first_down = first_grads
-    grad_mixer_gain, grad_mixer_input, grad_mixer_kernel, grad_mixer_output = mixer_grads
-    lower_shares = (
-        lax.psum_scatter(
-            grad_mixer_gain.astype(jnp.bfloat16), "seq", scatter_dimension=0, tiled=True
-        ).astype(jnp.float32),
-        lax.psum_scatter(
-            grad_mixer_input.astype(jnp.bfloat16), "seq", scatter_dimension=0, tiled=True
-        ).astype(jnp.float32),
-        lax.psum_scatter(
-            grad_mixer_kernel.astype(jnp.bfloat16), "seq", scatter_dimension=1, tiled=True
-        ).astype(jnp.float32),
-        lax.psum_scatter(
-            grad_mixer_output.astype(jnp.bfloat16), "seq", scatter_dimension=0, tiled=True
-        ).astype(jnp.float32),
-        lax.psum_scatter(
-            grad_first_gain.astype(jnp.bfloat16), "seq", scatter_dimension=0, tiled=True
-        ).astype(jnp.float32),
-        lax.psum_scatter(
-            grad_first_gate.astype(jnp.bfloat16), "seq", scatter_dimension=0, tiled=True
-        ).astype(jnp.float32),
-        lax.psum_scatter(
-            grad_first_up.astype(jnp.bfloat16), "seq", scatter_dimension=0, tiled=True
-        ).astype(jnp.float32),
-        lax.psum_scatter(
-            grad_first_down.astype(jnp.bfloat16), "seq", scatter_dimension=0, tiled=True
-        ).astype(jnp.float32),
-    )
+    second_gain_sum, second_wide, second_down_pair = second_grads
+    attend_gain_sum, attend_wide, query_gain_sum, key_gain_sum, attend_output_pair = attend_grads
+    first_gain_sum, first_wide, first_down_pair = first_grads
+    mixer_gain_sum, mixer_input_pair, mixer_kernel_sum, mixer_output_pair = mixer_grads
+    row_count, shards = lax.axis_size("row"), lax.axis_size("seq")
+    block_rows = math.gcd(tokens.shape[2] // shards, first_down.shape[0] // shards)
+
+    def operands(pair):
+        inputs, gradient_low = pair
+        token_count = inputs.shape[0] * inputs.shape[1]
+        inputs = inputs.reshape(token_count, -1).T
+        blocks = inputs.shape[0] // shards // block_rows
+        return (
+            inputs.reshape(shards // 2, 2, blocks, block_rows, token_count),
+            gradient_low.reshape(token_count, -1),
+        )
+
+    wide_vectors = jnp.concatenate(
+        [
+            mixer_kernel_sum,
+            jnp.stack([mixer_gain_sum, first_gain_sum, attend_gain_sum, second_gain_sum]),
+        ]
+    )
+    vector_count = wide_vectors.shape[0]
+    vectors = jnp.concatenate(
+        [
+            part.reshape(-1, shards, part.shape[-1] // shards)
+            .transpose(1, 0, 2)
+            .reshape(shards, -1)
+            for part in (wide_vectors, jnp.stack([query_gain_sum, key_gain_sum]))
+        ],
+        axis=1,
+    )
+    vector_rows = -(-vectors.shape[1] // COLS)
+    token_count = tokens.shape[0] * tokens.shape[1]
+    vectors = jnp.pad(vectors, ((0, 0), (0, vector_rows * COLS - vectors.shape[1])))
+    vectors = vectors.reshape(shards * vector_rows, COLS).astype(jnp.bfloat16)
+    vectors = jnp.pad(vectors, ((0, token_count - shards * vector_rows), (0, 0)))
+    shard_at = lax.broadcasted_iota(jnp.int32, (shards, 2 * block_rows, token_count), 0)
+    row_at = lax.broadcasted_iota(jnp.int32, (shards, 2 * block_rows, token_count), 1)
+    token_at = lax.broadcasted_iota(jnp.int32, (shards, 2 * block_rows, token_count), 2)
+    picks = (row_at < vector_rows) & (token_at == shard_at * vector_rows + row_at)
+    picks = picks.astype(jnp.bfloat16).reshape(shards // 2, 2, 2, block_rows, token_count)
     (
-        share_mixer_gain,
-        share_mixer_input,
-        share_mixer_kernel,
-        share_mixer_output,
-        share_first_gain,
-        share_first_gate,
-        share_first_up,
-        share_first_down,
-    ) = lower_shares
-    (
-        grad_mixer_gain,
+        grad_second_down,
+        second_both,
+        grad_attend_output,
+        attend_three,
+        grad_first_down,
+        first_both,
+        grad_mixer_output,
         grad_mixer_input,
-        grad_mixer_kernel,
-        grad_mixer_output,
-        grad_first_gain,
-        grad_first_gate,
-        grad_first_up,
-        grad_first_down,
-    ) = (
-        lax.psum(share_mixer_gain.astype(jnp.bfloat16), "row").astype(jnp.float32),
-        lax.psum(share_mixer_input.astype(jnp.bfloat16), "row").astype(jnp.float32),
-        lax.psum(share_mixer_kernel.astype(jnp.bfloat16), "row").astype(jnp.float32),
-        lax.psum(share_mixer_output.astype(jnp.bfloat16), "row").astype(jnp.float32),
-        lax.psum(share_first_gain.astype(jnp.bfloat16), "row").astype(jnp.float32),
-        lax.psum(share_first_gate.astype(jnp.bfloat16), "row").astype(jnp.float32),
-        lax.psum(share_first_up.astype(jnp.bfloat16), "row").astype(jnp.float32),
-        lax.psum(share_first_down.astype(jnp.bfloat16), "row").astype(jnp.float32),
-    )
+        vector_sums,
+    ) = reduce_gradients(
+        [
+            operands(second_down_pair),
+            operands(second_wide),
+            operands(attend_output_pair),
+            operands(attend_wide),
+            operands(first_down_pair),
+            operands(first_wide),
+            operands(mixer_output_pair),
+            operands(mixer_input_pair),
+            (picks, vectors),
+        ],
+        row_count,
+        shards,
+        0,
+    )
+
+    def single(value):
+        return value.astype(jnp.float32)
+
+    hidden_columns = first_gate.shape[1]
+    query_columns, key_columns = query_weight.shape[1], key_weight.shape[1]
+    vector_sums = single(vector_sums[:vector_rows]).reshape(-1)
+    width = tokens.shape[2] // shards
+    wide_sums = vector_sums[: vector_count * width].reshape(vector_count, width)
+    head_width = HEAD_DIM // shards
+    head_sums = vector_sums[vector_count * width :][: 2 * head_width].reshape(2, head_width)
     return (
         hidden.astype(jnp.bfloat16),
         gradient.astype(jnp.bfloat16),
-        grad_mixer_gain,
-        grad_mixer_input,
-        grad_mixer_kernel,
-        grad_mixer_output,
-        grad_first_gain,
-        grad_first_gate,
-        grad_first_up,
-        grad_first_down,
-        grad_attend_gain,
-        grad_query_weight,
-        grad_key_weight,
-        grad_value_weight,
-        grad_query_gain,
-        grad_key_gain,
-        grad_attend_output,
-        grad_second_gain,
-        grad_second_gate,
-        grad_second_up,
-        grad_second_down,
+        wide_sums[3],
+        single(grad_mixer_input),
+        wide_sums[:3],
+        single(grad_mixer_output),
+        wide_sums[4],
+        single(first_both[:, :hidden_columns]),
+        single(first_both[:, hidden_columns:]),
+        single(grad_first_down),
+        wide_sums[5],
+        single(attend_three[:, :query_columns]),
+        single(attend_three[:, query_columns : query_columns + key_columns]),
+        single(attend_three[:, query_columns + key_columns :]),
+        head_sums[0],
+        head_sums[1],
+        single(grad_attend_output),
+        wide_sums[6],
+        single(second_both[:, :hidden_columns]),
+        single(second_both[:, hidden_columns:]),
+        single(grad_second_down),
     )
 
 

time: 1450 us -> 739 us (0.51)
  waiting for transfers between devices: 1080 us -> 86.6 us
  Pallas kernels: 0 us -> 320 us
  matrix products: 196 us -> 129 us
  local copies, waits for them, and re-layouts: 59.8 us -> 115 us
  blocking collectives: 25.2 us -> 0 us
    reduce_scatter x12 -> x0, waiting for transfers between devices: 650 us -> none  [the longest x1 80 us: body(): lax.psum_scatter(grad_second_down.astype(jnp.bfloat16), 'seq', scatter_di...]
    pallas_call x0 -> x1, Pallas kernels: none -> 320 us  [reduce_gradients(): pl.pallas_call(functools.partial(reduce_kernel, entries, row_count, shard...]
    psum x1 -> x0, waiting for transfers between devices: 282 us -> none  [body(): lax.psum(share_mixer_input.astype(jnp.bfloat16), 'row').astype(jnp.float32)]
    unnamed x21 -> x6, waiting for transfers between devices: 111 us -> 47 us
    dot_general x12 -> x0, matrix products: 56 us -> none  [weight_grad(): jnp.einsum('rtd,rtf->df', inputs, gradient, preferred_element_type=jnp.fl...]
    reshape x0 -> x10, local copies, waits for them, and re-layouts: none -> 19 us  [the longest x7 16.2 us: operands(): inputs = inputs.reshape(token_count, -1).T]
    convert_element_type x0 -> x13, local copies, waits for them, and re-layouts: none -> 17.3 us  [the longest x2 5.36 us: attend_backward(): grad_queries.reshape(row_count, length, HEADS * HEAD_DIM)]
    unnamed x261 -> x268, local copies, waits for them, and re-layouts: 47.6 us -> 54 us
  transfers between devices with their start and end apart: 20 -> 6, of which waited for: 18 -> 5; matrix products, arithmetic and copies ran while one was open for 11% -> 12% of each run, Pallas kernels for 0% -> 0%
where the time goes in v1:
time: 739 us; the launch traced here: 730 us
  Pallas kernels  320 us (43%)
  matrix products  129 us (17%)
  local copies, waits for them, and re-layouts  115 us (16%)
  waiting for transfers between devices  86.6 us (12%)
  other arithmetic  57.4 us (8%)
  between operations  16.7 us (2%)
    pallas_call x1, Pallas kernels, reduce_gradients(): pl.pallas_call(functools.partial(reduce_kernel, entries, row_count, shard...  320 us
    dot_general x12, matrix products, back_dense(): jnp.einsum('rtf,df->rtd', gradient, matrix, preferred_element_type=jnp.fl...  58.4 us
    unnamed x268, local copies, waits for them, and re-layouts  54 us
    dot_general x12, matrix products, dense(): jnp.einsum('rtd,df->rtf', inputs, matrix, preferred_element_type=jnp.floa...  47.7 us
    unnamed x6, waiting for transfers between devices  47 us
    all_gather x1, waiting for transfers between devices, attend_block(): lax.all_gather(value_low, 'seq', axis=1, tiled=True)  25.4 us
    reshape x7, local copies, waits for them, and re-layouts, operands(): inputs = inputs.reshape(token_count, -1).T  16.2 us
  transfers between devices with their start and end apart: 6, of which 5 were waited for; matrix products, arithmetic and copies ran while one was open for 12% of the time, Pallas kernels for 0%

profile of v1, /device:TPU:0, one launch (start us, length us, event | category | flops | bytes accessed | tf_op | source)
XLA Modules:
  0.0 730.2 jit_solution(9390805804334061509)
XLA Ops:
  11.7 4.8 fusion.108
  21.9 3.2 multiply_convert_fusion.10
  26.2 6.1 fusion.104
  32.4 4.6 multiply_convert_fusion.3
  46.2 11.6 %fusion.82 = f32[2,128,4608]{2,1,0:T(8,128)} fusion(bf16[2,128,1024]{2,1,0:T(8,128)(2,1)S(1)} %copy-done.30, bf16[4608,1024]{1,0:T(8,128)(2,1)} %param.48), kind=kOutput, calls=%fused_computation.91 | convolution fusion | flops 2415919104 | bytes 14680064 | tf_op jit(solution)/shard_map/rtf,df->rtd/dot_general | solution.py:72
  63.4 14.1 %all-gather.5.cloned.1.call-done = bf16[2,1024,8,64]{1,3,2,0:T(8,128)(2,1)} async-done(((bf16[2,128,8,64]{1,3,2,0:T(8,128)(2,1)}), bf16[2,1024,8,64]{1,3,2,0:T(8,128)(2,1)}) %all-gather.5.cloned.1.call-update) | async-done | bytes 2097168 | tf_op jit(solution)/shard_map/all_gather | solution.py:201
  77.5 5.2 while.47
  82.7 25.4 %all-gather.3.cloned.1.call-done = bf16[2,1024,8,64]{1,3,2,0:T(8,128)(2,1)} async-done(((bf16[2,128,8,64]{1,3,2,0:T(8,128)(2,1)}), bf16[2,1024,8,64]{1,3,2,0:T(8,128)(2,1)}) %all-gather.3.cloned.1.call-update) | async-done | bytes 2097168 | tf_op jit(solution)/shard_map/all_gather | solution.py:202
  110.3 12.3 %while.48 = (s32[]{:T(128)}, f32[2,128,8,2,64]{1,4,3,2,0:T(8,128)}, f32[2,128,8,2,64]{1,4,3,2,0:T(8,128)}, s32[]{:T(128)}, bf16[2,1024,8,64]{1,3,2,0:T(8,128)(2,...) while((s32[]{:T(128)}, f32[2,128,8,2,64]{1,4,3,2,0:T(8,128)}, ...), condition=%wide.region_15.16_spmd.clone, body=%wide.region_13.15_spmd.clone.sunk | while | flops 2167215616 | bytes 58769768 | solution.py:263
  113.8 5.3 fusion.268
  124.0 2.9 multiply_reduce_fusion.11
  127.1 5.6 fusion.88
  132.8 10.1 %add_convert_fusion.1 = (bf16[2,128,4608]{2,1,0:T(8,128)(2,1)S(1)}, bf16[2,128,4608]{2,1,0:T(8,128)(2,1)}, bf16[2,128,4608]{2,1,0:T(8,128)(2,1)}) fusion(f32[2,128,4608]{2,1,0:T(8,128)S(1)} %bitcast.524, f32[2,128,4608]{2,1,0:T(8,128)S(1)} %fusion.88, bf16[2,128,1024]{2,1,0:T(8,128)(2,1)S(1)} %multiply_convert_fusion.7, bf16[1024,4608]{1,0:T(8,128)(2,1)} %param.46), kind=kOutput, calls=%fused_computation.125 | convolution fusion | flops 2437152768 | bytes 26476544 | tf_op jit(solution)/shard_map/rtd,df->rtf/dot_general | solution.py:64
  142.9 5.1 fusion.86
  148.1 6.2 multiply_reduce_fusion.1
  164.6 12.9 %while.49 = (s32[]{:T(128)}, f32[2,128,8,2,64]{1,4,3,2,0:T(8,128)}, bf16[2,1024,8,64]{1,3,2,0:T(8,128)(2,1)}, bf16[2,1024,8,64]{1,3,2,0:T(8,128)(2,1)}, s32[]{:T...) while((s32[]{:T(128)}, f32[2,128,8,2,64]{1,4,3,2,0:T(8,128)}, ...), condition=%wide.region_20.21_spmd.clone, body=%wide.region_18.20_spmd.clone.sunk | while | flops 1368725120 | bytes 108593632 | solution.py:317
  170.0 3.2 fusion.281
  177.5 6.2 copy.219
  183.7 6.6 reshape.696
  197.1 4.3 copy.169
  201.4 6.2 copy.217
  207.6 6.6 reshape.694
  230.0 4.5 copy.165
  237.3 8.2 %fusion.144 = bf16[2,128,1024]{2,1,0:T(8,128)(2,1)} fusion(f32[2,128,1024]{2,1,0:T(8,128)} %copy-done.11, bf16[2,128,4608]{2,1,0:T(8,128)(2,1)} %get-tuple-element.625, bf16[4608,1024]{1,0:T(8,128)(2,1)} %param.48), kind=kOutput, calls=%fused_computation.172 | convolution fusion | flops 2416443392 | bytes 13369344 | tf_op jit(solution)/shard_map/rtd,df->rtf/dot_general | solution.py:64
  248.3 7.8 %reduce-scatter.9.cloned.1.call-done = bf16[128,1024]{1,0:T(8,128)(2,1)} async-done(((bf16[1024,1024]{1,0:T(8,128)(2,1)}), bf16[128,1024]{1,0:T(8,128)(2,1)}) %reduce-scatter.9.cloned.1.call-update) | async-done | bytes 262160
  262.3 39.2 %reduce-scatter.7.cloned.1.call-done = bf16[128,1024]{1,0:T(8,128)(2,1)} async-done(((bf16[1024,1024]{1,0:T(8,128)(2,1)}), bf16[128,1024]{1,0:T(8,128)(2,1)}) %reduce-scatter.7.cloned.1.call-update) | async-done | bytes 262160
  311.2 3.0 multiply_reduce_fusion.2
  315.7 9.7 %add_convert_fusion = (bf16[2,128,4608]{2,1,0:T(8,128)(2,1)}, bf16[2,128,4608]{2,1,0:T(8,128)(2,1)}) fusion(f32[2,128,4608]{2,1,0:T(8,128)S(1)} %bitcast.511, f32[2,128,4608]{2,1,0:T(8,128)} %get-tuple-element.670, bf16[2,128,1024]{2,1,0:T(8,128)(2,1)} %get-tuple-element.615, bf16[4608,1024]{1,0:T(8,128)(2,1)} %param.37), kind=kOutput, calls=%fused_computation.122 | convolution fusion | flops 2434793472 | bytes 24117248 | tf_op jit(solution)/shard_map/rtf,df->rtd/dot_general | solution.py:72
  325.3 6.6 fusion.98
  354.2 6.1 fusion.153
  364.0 320.3 %shard_map.373 = bf16[138,64,512]{2,1,0:T(8,128)(2,1)} custom-call(bf16[4,2,9,64,256]{4,3,2,1,0:T(8,128)(2,1)} %bitcast.529, bf16[4,2,2,64,256]{4,3,2,1,0:T(8,128)(2,1)S(1)} %bitcast.486, bf16[4,2,2,64,256]{4,3,2,1,0:T(8,128)(2,1)S(1)} %bitcast.485, bf16[4,2,2,64,256]{4,3,2,1,0:T(8,128)(2,1)S(1)} %bitcast.484, bf16[4,2,9,64,256]{4,3,2,1,0:T(8,128)(2,1)} %bitcast.528, ...), custom_call_target="tpu_custom_call" | custom-call | flops 18522046464 | bytes 9043968 | tf_op jit(solution)/shard_map/pallas_call | solution.py:627
  691.5 3.3 fusion.192
  (470 shorter events, 165.8 us)
Async XLA Ops:
  7.2 52.0 %copy-start = (bf16[1024,1024]{1,0:T(8,128)(2,1)S(1)}, bf16[1024,1024]{1,0:T(8,128)(2,1)}, u32[]{:S(2)}) copy-start(bf16[1024,1024]{1,0:T(8,128)(2,1)} %param.39) | copy-start | bytes 6291460
  7.2 70.3 %all-gather.5.cloned.1.call-start = ((), (), s32[]{:S(2)}) async-start(), calls=%async_computation.3 | async-start | bytes 2359296 | tf_op jit(solution)/shard_map/all_gather | solution.py:201
  11.7 9.8 %copy-start.117 = (bf16[64]{0:T(256)(128)(2,1)S(1)}, bf16[64]{0:T(256)(128)(2,1)}, u32[]{:S(2)}) copy-start(bf16[64]{0:T(256)(128)(2,1)} %param.43) | copy-start | bytes 388
  11.7 9.8 %copy-start.110 = (bf16[1024]{0:T(1024)(128)(2,1)S(1)}, bf16[1024]{0:T(1024)(128)(2,1)}, u32[]{:S(2)}) copy-start(bf16[1024]{0:T(1024)(128)(2,1)} %param.34) | copy-start | bytes 6148
  11.7 9.9 %copy-start.111 = (bf16[1024]{0:T(1024)(128)(2,1)S(1)}, bf16[1024]{0:T(1024)(128)(2,1)}, u32[]{:S(2)}) copy-start(bf16[1024]{0:T(1024)(128)(2,1)} %param.38) | copy-start | bytes 6148
  18.4 3.3 collective-permute-start
  21.5 40.0 %copy-start.64 = (f32[2,128,32]{1,2,0:T(8,128)}, f32[2,128,32]{1,2,0:T(8,128)S(1)}, u32[]{:S(2)}) copy-start(f32[2,128,32]{1,2,0:T(8,128)S(1)} %get-tuple-element.663) | copy-start | bytes 98308
  21.5 40.0 %copy-start.66 = (f32[2,128,32]{1,2,0:T(8,128)}, f32[2,128,32]{1,2,0:T(8,128)S(1)}, u32[]{:S(2)}) copy-start(f32[2,128,32]{1,2,0:T(8,128)S(1)} %get-tuple-element.664) | copy-start | bytes 98308
  21.6 21.3 %copy-start.104 = (f32[64]{0:T(128)}, f32[64]{0:T(128)S(1)}, u32[]{:S(2)}) copy-start(f32[64]{0:T(128)S(1)} %convert_element_type.318) | copy-start | bytes 772
  21.6 19.6 %copy-start.77 = (f32[1024]{0:T(1024)}, f32[1024]{0:T(1024)S(1)}, u32[]{:S(2)}) copy-start(f32[1024]{0:T(1024)S(1)} %convert_element_type.314) | copy-start | bytes 12292
  21.9 10.5 %slice-start.14 = ((s8[9437184]{0:T(1024)(128)(4,1)}), s8[4194304]{0:T(1024)(128)(4,1)S(1)}, s32[]{:S(2)}) async-start(s8[9437184]{0:T(1024)(128)(4,1)} %bitcast.583), calls=%async_computation.20 | async-start | bytes 8388608
  25.9 11.2 %copy-start.16 = (f32[2,128,1024]{2,1,0:T(8,128)}, f32[2,128,1024]{2,1,0:T(8,128)S(1)}, u32[]{:S(2)}) copy-start(f32[2,128,1024]{2,1,0:T(8,128)S(1)} %get-tuple-element.668) | copy-start | bytes 3145732
  26.2 10.9 %slice-start.11 = ((s8[9437184]{0:T(1024)(128)(4,1)}), s8[4194304]{0:T(1024)(128)(4,1)S(1)}, s32[]{:S(2)}) async-start(s8[9437184]{0:T(1024)(128)(4,1)} %bitcast.581), calls=%async_computation.17 | async-start | bytes 8388608
  42.3 16.9 %copy-start.13 = (bf16[2,128,1024]{2,1,0:T(8,128)(2,1)}, bf16[2,128,1024]{2,1,0:T(8,128)(2,1)S(1)}, u32[]{:S(2)}) copy-start(bf16[2,128,1024]{2,1,0:T(8,128)(2,1)S(1)} %multiply_convert_fusion.8) | copy-start | bytes 1572868
  44.6 63.5 %all-gather.3.cloned.1.call-start = ((), (), s32[]{:S(2)}) async-start(), calls=%async_computation.2 | async-start | bytes 2359296 | tf_op jit(solution)/shard_map/all_gather | solution.py:202
  46.2 14.0 %copy-start.106 = (f32[64]{0:T(128)}, f32[64]{0:T(128)S(1)}, u32[]{:S(2)}) copy-start(f32[64]{0:T(128)S(1)} %convert_element_type.320) | copy-start | bytes 772
  46.2 11.6 %copy-start.42 = (bf16[1024,512]{1,0:T(8,128)(2,1)S(1)}, bf16[1024,512]{1,0:T(8,128)(2,1)}, u32[]{:S(2)}) copy-start(bf16[1024,512]{1,0:T(8,128)(2,1)} %param.41) | copy-start | bytes 3145732
  62.3 193.7 %reduce-scatter.9.cloned.1.call-start = ((), (), s32[]{:S(2)}) async-start(), calls=%async_computation.5 | async-start | bytes 2359296
  126.9 27.4 %copy-start.11 = (f32[2,128,1024]{2,1,0:T(8,128)}, f32[2,128,1024]{2,1,0:T(8,128)S(1)}, u32[]{:S(2)}) copy-start(f32[2,128,1024]{2,1,0:T(8,128)S(1)} %get-tuple-element.678) | copy-start | bytes 3145732
  127.1 15.8 %slice-start = ((s8[9437184]{0:T(1024)(128)(4,1)}), s8[4194304]{0:T(1024)(128)(4,1)S(1)}, s32[]{:S(2)}) async-start(s8[9437184]{0:T(1024)(128)(4,1)} %bitcast.495), calls=%async_computation.6 | async-start | bytes 8388608
  132.8 10.1 %slice-start.1 = ((s8[9437184]{0:T(1024)(128)(4,1)}), s8[4194304]{0:T(1024)(128)(4,1)S(1)}, s32[]{:S(2)}) async-start(s8[9437184]{0:T(1024)(128)(4,1)} %bitcast.495), calls=%async_computation.7 | async-start | bytes 8388608
  132.8 10.1 %slice-start.2 = ((s8[9437184]{0:T(1024)(128)(4,1)}), s8[1048576]{0:T(1024)(128)(4,1)S(1)}, s32[]{:S(2)}) async-start(s8[9437184]{0:T(1024)(128)(4,1)} %bitcast.495), calls=%async_computation.8 | async-start | bytes 2097152
  190.3 111.1 %reduce-scatter.7.cloned.1.call-start = ((), (), s32[]{:S(2)}) async-start(), calls=%async_computation.4 | async-start | bytes 2359296
  248.3 56.9 %copy-start.74 = (f32[2,128,8]{1,2,0:T(8,128)S(1)}, f32[2,128,8]{1,2,0:T(8,128)}, u32[]{:S(2)}) copy-start(f32[2,128,8]{1,2,0:T(8,128)} %copy-done.73) | copy-start | bytes 24580
  248.3 56.9 %copy-start.105 = (f32[64]{0:T(128)S(1)}, f32[64]{0:T(128)}, u32[]{:S(2)}) copy-start(f32[64]{0:T(128)} %copy-done.104) | copy-start | bytes 772
  248.3 58.4 %copy-start.76 = (f32[2,128,8]{1,2,0:T(8,128)S(1)}, f32[2,128,8]{1,2,0:T(8,128)}, u32[]{:S(2)}) copy-start(f32[2,128,8]{1,2,0:T(8,128)} %copy-done.75) | copy-start | bytes 24580
  314.3 20.4 %slice-start.3 = ((s8[9437184]{0:T(1024)(128)(4,1)}), s8[4194304]{0:T(1024)(128)(4,1)S(1)}, s32[]{:S(2)}) async-start(s8[9437184]{0:T(1024)(128)(4,1)} %bitcast.497), calls=%async_computation.9 | async-start | bytes 8388608
  315.7 19.0 %slice-start.4 = ((s8[9437184]{0:T(1024)(128)(4,1)}), s8[4194304]{0:T(1024)(128)(4,1)S(1)}, s32[]{:S(2)}) async-start(s8[9437184]{0:T(1024)(128)(4,1)} %bitcast.497), calls=%async_computation.10 | async-start | bytes 8388608
  315.7 19.0 %slice-start.5 = ((s8[9437184]{0:T(1024)(128)(4,1)}), s8[1048576]{0:T(1024)(128)(4,1)S(1)}, s32[]{:S(2)}) async-start(s8[9437184]{0:T(1024)(128)(4,1)} %bitcast.497), calls=%async_computation.11 | async-start | bytes 2097152
  344.6 9.6 %copy-start.80 = (f32[1024]{0:T(1024)S(1)}, f32[1024]{0:T(1024)}, u32[]{:S(2)}) copy-start(f32[1024]{0:T(1024)} %copy-done.79) | copy-start | bytes 12292
  344.6 9.6 %copy-start.97 = (f32[2,128]{1,0:T(2,128)S(1)}, f32[2,128]{1,0:T(2,128)}, u32[]{:S(2)}) copy-start(f32[2,128]{1,0:T(2,128)} %copy-done.96) | copy-start | bytes 3076
  348.2 3.6 collective-permute-start.1
  (110 other events, 446.2 us)
Sparse Core Ops, SparseCore 0:
  44.8 32.6 all-gather.4
  79.9 28.1 all-gather.2
  190.4 65.5 reduce-scatter.8
  260.1 41.2 reduce-scatter.6

commit v2 on v1

--- a/solution.py
+++ b/solution.py
@@ -1,5 +1,6 @@
 import functools
 import math
+import types
 
 import jax
 import jax.numpy as jnp
@@ -21,7 +22,7 @@
 MESH = pl.DeviceIdType.MESH
 COLS = 512
 SLOTS = 4
-ZSLOTS = 8
+ZSLOTS = 6
 
 
 def passed_along(value, axis, steps):
@@ -368,12 +369,10 @@
     return (result, attend_backward)
 
 
-def reduce_entries(pairs, shards, rows, block_rows):
+def reduce_entries(pairs):
     entries = []
     x_first = g_first = chunk = 0
-    for x, g in pairs:
-        x_count = x.shape[2]
-        g_count = g.shape[1] // COLS
+    for x_count, g_count in pairs:
         entries.append((x_first, x_count, g_first, g_count, chunk))
         x_first += x_count
         g_first += g_count
@@ -406,216 +405,7 @@
     return kinds
 
 
-def reduce_kernel(entries, row_count, shards, chunks, *refs):
-    count = len(entries)
-    xs, gs = refs[:count], refs[count : 2 * count]
-    out = refs[2 * count]
-    (load_x, load_g, x_all, g_all, send_zero, recv_zero, *rest) = refs[2 * count + 1 :]
-    bits = shards.bit_length() - 1
-    kinds = seq_steps(bits)
-    held, received = [[], []], [[], []]
-    for kind in range(2):
-        for _ in kinds[kind]:
-            held[kind].append(rest.pop(0))
-            received[kind].append(rest.pop(0))
-    z_own, z_in, z_part, z_cross, z_total = rest[:5]
-    seq_send, seq_recv, z_send, z_recv, out_sem = rest[5:]
-    row, seq = lax.axis_index("row"), lax.axis_index("seq")
-    bit_value = [lax.rem(seq // (1 << bit), 2) for bit in range(bits)]
-    partner = [seq + (1 << bit) * (1 - 2 * bit_value[bit]) for bit in range(bits)]
-    pairs = chunks // 2
-
-    for at, (x_first, x_count, g_first, g_count, _) in enumerate(entries):
-        pltpu.make_async_copy(
-            xs[at], x_all.at[:, :, pl.ds(x_first, x_count)], load_x.at[at]
-        ).start()
-        pltpu.make_async_copy(
-            gs[at], g_all.at[:, pl.ds(g_first * COLS, g_count * COLS)], load_g.at[at]
-        ).start()
-
-    barrier = pltpu.get_barrier_semaphore()
-    for bit in range(bits):
-        pl.semaphore_signal(barrier, inc=1, device_id=(row, partner[bit]), device_id_type=MESH)
-    for step in (1, row_count - 1):
-        pl.semaphore_signal(
-            barrier, inc=1, device_id=(lax.rem(row + step, row_count), seq), device_id_type=MESH
-        )
-    pl.semaphore_wait(barrier, bits + 2)
-
-    for at, (x_first, x_count, g_first, g_count, _) in enumerate(entries):
-        pltpu.make_async_copy(
-            xs[at], x_all.at[:, :, pl.ds(x_first, x_count)], load_x.at[at]
-        ).wait()
-        pltpu.make_async_copy(
-            gs[at], g_all.at[:, pl.ds(g_first * COLS, g_count * COLS)], load_g.at[at]
-        ).wait()
-
-    def product(q, side):
-        x_block, g_block = locate(entries, q)
-        left = x_all[:, side, x_block]
-        columns = pl.ds(pl.multiple_of(g_block * COLS, COLS), COLS)
-        return jnp.dot(
-            left.reshape(left.shape[0] * left.shape[1], left.shape[2]),
-            g_all[:, columns],
-            preferred_element_type=jnp.float32,
-        )
-
-    def seq_copy(kind, step, slot):
-        if step == 0:
-            bit = 0
-            source, target = send_zero.at[kind, slot], recv_zero.at[kind, slot]
-        else:
-            bit = kinds[kind][step - 1][0]
-            source = held[kind][step - 1].at[slot, :, 1 - bit_value[bit]]
-            target = received[kind][step - 1].at[slot]
-        return pltpu.make_async_remote_copy(
-            src_ref=source,
-            dst_ref=target,
-            send_sem=seq_send.at[kind, step, slot],
-            recv_sem=seq_recv.at[kind, step, slot],
-            device_id=(row, partner[bit]),
-            device_id_type=MESH,
-        )
-
-    def seq_sum(kind, step, slot, q):
-        if step == 1:
-            mine = product(q, bit_value[0])
-            other = recv_zero[kind, slot].astype(jnp.float32)
-            return mine + other.reshape(mine.shape)
-        bit = kinds[kind][step - 2][0]
-        mine = held[kind][step - 2][slot, :, bit_value[bit]].astype(jnp.float32)
-        return mine + received[kind][step - 2][slot].astype(jnp.float32)
-
-    half = row_count // 2
-    depth = half - 1
-    lower = row < half
-    level = jnp.where(lower, row, row_count - 1 - row)
-    toward = jnp.where(lower, row + 1, row - 1)
-    away = jnp.where(lower, row - 1, row + 1)
-
-    def z_copy(kind, step, slot):
-        if step < depth:
-            source = z_own if step == 0 else z_part
-            target, where = z_in, toward
-        elif step == depth:
-            source = z_own if depth == 0 else z_part
-            target, where = z_cross, toward
-        else:
-            source, target, where = z_total, z_total, away
-        return pltpu.make_async_remote_copy(
-            src_ref=source.at[kind, slot],
-            dst_ref=target.at[kind, slot],
-            send_sem=z_send.at[kind, step, slot],
-            recv_sem=z_recv.at[kind, step, slot],
-            device_id=(where, seq),
-            device_id_type=MESH,
-        )
-
-    def out_copy(kind, slot, q):
-        return pltpu.make_async_copy(z_total.at[kind, slot], out.at[q], out_sem.at[kind, slot])
-
-    def each(stage, i, run):
-        index = i - stage
-
-        @pl.when(jnp.logical_and(index >= 0, index < pairs))
-        def _():
-            for kind in range(2):
-                run(kind, index, 2 * index + kind)
-
-    def first(kind, index, q):
-        slot = lax.rem(index, SLOTS)
-        send_zero[kind, slot] = product(q, 1 - bit_value[0]).astype(jnp.bfloat16).reshape(
-            send_zero.shape[2:]
-        )
-        seq_copy(kind, 0, slot).start()
-
-    def middle(step):
-        def run(kind, index, q):
-            slot = lax.rem(index, SLOTS)
-            seq_copy(kind, step - 1, slot).wait()
-            total = seq_sum(kind, step, slot, q)
-            target = held[kind][step - 1]
-            target[slot] = total.astype(jnp.bfloat16).reshape(target.shape[1:])
-            seq_copy(kind, step, slot).start()
-
-        return run
-
-    def last(kind, index, q):
-        slot, z_slot = lax.rem(index, SLOTS), lax.rem(index, ZSLOTS)
-        seq_copy(kind, bits - 1, slot).wait()
-        total = seq_sum(kind, bits, slot, q)
-        z_own[kind, z_slot] = total.astype(jnp.bfloat16).reshape(z_own.shape[2:])
-
-        @pl.when(level == 0)
-        def _():
-            z_copy(kind, 0, z_slot).start()
-
-    def z_stage(step):
-        def run(kind, index, q):
-            slot = lax.rem(index, ZSLOTS)
-            if step <= depth:
-
-                @pl.when(level == step)
-                def _():
-                    z_copy(kind, step - 1, slot).wait_recv()
-                    z_part[kind, slot] = (
-                        z_own[kind, slot].astype(jnp.float32) + z_in[kind, slot].astype(jnp.float32)
-                    ).astype(jnp.bfloat16)
-                    z_copy(kind, step, slot).start()
-
-                @pl.when(level == step - 1)
-                def _():
-                    z_copy(kind, step - 1, slot).wait_send()
-
-            elif step == depth + 1:
-
-                @pl.when(level == depth)
-                def _():
-                    z_copy(kind, depth, slot).wait()
-                    own = z_own if depth == 0 else z_part
-                    z_total[kind, slot] = (
-                        own[kind, slot].astype(jnp.float32) + z_cross[kind, slot].astype(jnp.float32)
-                    ).astype(jnp.bfloat16)
-                    if depth > 0:
-                        z_copy(kind, step, slot).start()
-                    out_copy(kind, slot, q).start()
-
-            else:
-                receiver = 2 * depth + 1 - step
-
-                @pl.when(level == receiver)
-                def _():
-                    z_copy(kind, step - 1, slot).wait_recv()
-                    if receiver > 0:
-                        z_copy(kind, step, slot).start()
-                    out_copy(kind, slot, q).start()
-
-                @pl.when(level == receiver + 1)
-                def _():
-                    z_copy(kind, step - 1, slot).wait_send()
-
-        return run
-
-    def finish(kind, index, q):
-        out_copy(kind, lax.rem(index, ZSLOTS), q).wait()
-
-    stages = [first]
-    stages += [middle(step) for step in range(1, bits)]
-    stages += [last]
-    stages += [z_stage(step) for step in range(1, 2 * depth + 2)]
-    stages += [finish]
-
-    def iteration(i, carried):
-        for stage, run in enumerate(stages):
-            each(stage, i, run)
-        return carried
-
-    lax.fori_loop(0, pairs + len(stages) - 1, iteration, 0)
-
-
-def reduce_gradients(pairs, row_count, shards, collective_id):
-    block_rows, tokens = pairs[0][0].shape[3:]
-    entries, x_blocks, g_blocks, chunks = reduce_entries(pairs, shards, row_count, block_rows)
+def exchange_scratch(row_count, shards, block_rows, x_blocks, g_blocks, tokens):
     bits = shards.bit_length() - 1
     block = (block_rows, COLS)
     comm = []
@@ -624,25 +414,333 @@
             comm.append(pltpu.VMEM((SLOTS, above, 2, below) + block, jnp.bfloat16))
             comm.append(pltpu.VMEM((SLOTS, above, below) + block, jnp.bfloat16))
     z_steps = row_count - 1
-    result = pl.pallas_call(
-        functools.partial(reduce_kernel, entries, row_count, shards, chunks),
-        out_shape=jax.ShapeDtypeStruct((chunks,) + block, jnp.bfloat16),
+    return [
+        pltpu.VMEM((shards // 2, 2, x_blocks, block_rows, tokens), jnp.bfloat16),
+        pltpu.VMEM((tokens, g_blocks * COLS), jnp.bfloat16),
+        pltpu.VMEM((2, SLOTS, shards // 2) + block, jnp.bfloat16),
+        pltpu.VMEM((2, SLOTS, shards // 2) + block, jnp.bfloat16),
+        *comm,
+        *[pltpu.VMEM((2, ZSLOTS) + block, jnp.bfloat16) for _ in range(5)],
+        pltpu.SemaphoreType.DMA((2, bits, SLOTS)),
+        pltpu.SemaphoreType.DMA((2, bits, SLOTS)),
+        pltpu.SemaphoreType.DMA((2, z_steps, ZSLOTS)),
+        pltpu.SemaphoreType.DMA((2, z_steps, ZSLOTS)),
+        pltpu.SemaphoreType.DMA((2, ZSLOTS)),
+    ]
+
+
+class Exchange:
+    def __init__(self, entries, row_count, shards, outs, scratch, locals_at=(), local=None):
+        self.entries, self.outs = entries, outs
+        self.locals_at, self.local = locals_at, local
+        self.bits = bits = shards.bit_length() - 1
+        self.kinds = seq_steps(bits)
+        (self.x_all, self.g_all, self.send_zero, self.recv_zero, *rest) = scratch
+        self.held, self.received = [[], []], [[], []]
+        for kind in range(2):
+            for _ in self.kinds[kind]:
+                self.held[kind].append(rest.pop(0))
+                self.received[kind].append(rest.pop(0))
+        self.z_own, self.z_in, self.z_part, self.z_cross, self.z_total = rest[:5]
+        self.seq_send, self.seq_recv, self.z_send, self.z_recv, self.out_sem = rest[5:]
+        self.row, self.seq = lax.axis_index("row"), lax.axis_index("seq")
+        self.row_count, self.shards = row_count, shards
+        self.value = [lax.rem(self.seq // (1 << bit), 2) for bit in range(bits)]
+        self.partner = [self.seq + (1 << bit) * (1 - 2 * self.value[bit]) for bit in range(bits)]
+        last = entries[-1]
+        self.pairs = (last[4] + last[1] * last[3]) // 2 + len(locals_at)
+        half = row_count // 2
+        self.depth = half - 1
+        lower = self.row < half
+        self.level = jnp.where(lower, self.row, row_count - 1 - self.row)
+        self.toward = jnp.where(lower, self.row + 1, self.row - 1)
+        self.away = jnp.where(lower, self.row - 1, self.row + 1)
+
+    def meet(self):
+        barrier = pltpu.get_barrier_semaphore()
+        others = [(self.row, partner) for partner in self.partner]
+        for step in (1, self.row_count - 1):
+            others.append((lax.rem(self.row + step, self.row_count), self.seq))
+        for step in (1, self.shards - 1):
+            others.append((self.row, lax.rem(self.seq + step, self.shards)))
+        for other in others:
+            pl.semaphore_signal(barrier, inc=1, device_id=other, device_id_type=MESH)
+        pl.semaphore_wait(barrier, len(others))
+
+    def is_local(self, index):
+        found = index < 0
+        for at in self.locals_at:
+            found = jnp.logical_or(found, index == at)
+        return found
+
+    def chunk(self, kind, index):
+        before = sum([jnp.where(index > at, 1, 0) for at in self.locals_at], 0)
+        return 2 * (index - before) + kind
+
+    def product(self, kind, index, side):
+        x_block, g_block = locate(self.entries, self.chunk(kind, index))
+        left = self.x_all[:, side, x_block]
+        columns = pl.ds(pl.multiple_of(g_block * COLS, COLS), COLS)
+        return jnp.dot(
+            left.reshape(left.shape[0] * left.shape[1], left.shape[2]),
+            self.g_all[:, columns],
+            preferred_element_type=jnp.float32,
+        )
+
+    def seq_copy(self, kind, step, slot):
+        if step == 0:
+            bit = 0
+            source, target = self.send_zero.at[kind, slot], self.recv_zero.at[kind, slot]
+        else:
+            bit = self.kinds[kind][step - 1][0]
+            source = self.held[kind][step - 1].at[slot, :, 1 - self.value[bit]]
+            target = self.received[kind][step - 1].at[slot]
+        return pltpu.make_async_remote_copy(
+            src_ref=source,
+            dst_ref=target,
+            send_sem=self.seq_send.at[kind, step, slot],
+            recv_sem=self.seq_recv.at[kind, step, slot],
+            device_id=(self.row, self.partner[bit]),
+            device_id_type=MESH,
+        )
+
+    def seq_sum(self, kind, step, slot):
+        bit = self.kinds[kind][step - 2][0]
+        mine = self.held[kind][step - 2][slot, :, self.value[bit]].astype(jnp.float32)
+        return mine + self.received[kind][step - 2][slot].astype(jnp.float32)
+
+    def z_copy(self, kind, step, slot):
+        if step < self.depth:
+            source = self.z_own if step == 0 else self.z_part
+            target, where = self.z_in, self.toward
+        elif step == self.depth:
+            source = self.z_own if self.depth == 0 else self.z_part
+            target, where = self.z_cross, self.toward
+        else:
+            source, target, where = self.z_total, self.z_total, self.away
+        return pltpu.make_async_remote_copy(
+            src_ref=source.at[kind, slot],
+            dst_ref=target.at[kind, slot],
+            send_sem=self.z_send.at[kind, step, slot],
+            recv_sem=self.z_recv.at[kind, step, slot],
+            device_id=(where, self.seq),
+            device_id_type=MESH,
+        )
+
+    def start_out(self, kind, slot, index):
+        q = self.chunk(kind, index)
+        rows = self.z_total.shape[2]
+        for out, (_, x_count, _, g_count, chunk) in zip(self.outs, self.entries):
+            here = q - chunk
+
+            @pl.when(jnp.logical_and(here >= 0, here < x_count * g_count))
+            def _():
+                row_at = pl.multiple_of(lax.rem(here, x_count) * rows, rows)
+                column_at = pl.multiple_of(here // x_count * COLS, COLS)
+                pltpu.make_async_copy(
+                    self.z_total.at[kind, slot],
+                    out.at[pl.ds(row_at, rows), pl.ds(column_at, COLS)],
+                    self.out_sem.at[kind, slot],
+                ).start()
+
+    def first(self, kind, index):
+        slot = lax.rem(index, SLOTS)
+        target = self.send_zero
+
+        def put():
+            target[kind, slot] = (
+                self.product(kind, index, 1 - self.value[0])
+                .astype(jnp.bfloat16)
+                .reshape(target.shape[2:])
+            )
+
+        if self.local is None:
+            put()
+        else:
+            pl.when(jnp.logical_not(self.is_local(index)))(put)
+
+            @pl.when(self.is_local(index))
+            def _():
+                target[kind, slot] = self.local.part(kind, index, 1 - self.value[0])
+
+        self.seq_copy(kind, 0, slot).start()
+
+    def second(self, kind, index):
+        slot = lax.rem(index, SLOTS)
+        self.seq_copy(kind, 0, slot).wait()
+        target = self.held[kind][0]
+
+        def put():
+            mine = self.product(kind, index, self.value[0])
+            total = mine + self.recv_zero[kind, slot].astype(jnp.float32).reshape(mine.shape)
+            target[slot] = total.astype(jnp.bfloat16).reshape(target.shape[1:])
+
+        if self.local is None:
+            put()
+        else:
+            pl.when(jnp.logical_not(self.is_local(index)))(put)
+
+            @pl.when(self.is_local(index))
+            def _():
+                mine = self.local.part(kind, index, self.value[0]).astype(jnp.float32)
+                total = mine + self.recv_zero[kind, slot].astype(jnp.float32)
+                target[slot] = total.astype(jnp.bfloat16).reshape(target.shape[1:])
+
+        self.seq_copy(kind, 1, slot).start()
+
+    def middle(self, step):
+        def run(kind, index):
+            slot = lax.rem(index, SLOTS)
+            self.seq_copy(kind, step - 1, slot).wait()
+            total = self.seq_sum(kind, step, slot)
+            target = self.held[kind][step - 1]
+            target[slot] = total.astype(jnp.bfloat16).reshape(target.shape[1:])
+            self.seq_copy(kind, step, slot).start()
+
+        return run
+
+    def last(self, kind, index):
+        slot, z_slot = lax.rem(index, SLOTS), lax.rem(index, ZSLOTS)
+        self.seq_copy(kind, self.bits - 1, slot).wait()
+        total = self.seq_sum(kind, self.bits, slot).reshape(self.z_own.shape[2:])
+
+        def put():
+            self.z_own[kind, z_slot] = total.astype(jnp.bfloat16)
+
+            @pl.when(self.level == 0)
+            def _():
+                self.z_copy(kind, 0, z_slot).start()
+
+        if self.local is None:
+            put()
+        else:
+            pl.when(jnp.logical_not(self.is_local(index)))(put)
+
+            @pl.when(self.is_local(index))
+            def _():
+                self.local.take(kind, index, total)
+
+    def z_stage(self, step):
+        level, depth = self.level, self.depth
+
+        def run(kind, index):
+            slot = lax.rem(index, ZSLOTS)
+            if step <= depth:
+
+                @pl.when(level == step)
+                def _():
+                    self.z_copy(kind, step - 1, slot).wait_recv()
+                    self.z_part[kind, slot] = (
+                        self.z_own[kind, slot].astype(jnp.float32)
+                        + self.z_in[kind, slot].astype(jnp.float32)
+                    ).astype(jnp.bfloat16)
+                    self.z_copy(kind, step, slot).start()
+
+                @pl.when(level == step - 1)
+                def _():
+                    self.z_copy(kind, step - 1, slot).wait_send()
+
+            elif step == depth + 1:
+
+                @pl.when(level == depth)
+                def _():
+                    self.z_copy(kind, depth, slot).wait()
+                    own = self.z_own if depth == 0 else self.z_part
+                    self.z_total[kind, slot] = (
+                        own[kind, slot].astype(jnp.float32)
+                        + self.z_cross[kind, slot].astype(jnp.float32)
+                    ).astype(jnp.bfloat16)
+                    if depth > 0:
+                        self.z_copy(kind, step, slot).start()
+                    self.start_out(kind, slot, index)
+
+            else:
+                receiver = 2 * depth + 1 - step
+
+                @pl.when(level == receiver)
+                def _():
+                    self.z_copy(kind, step - 1, slot).wait_recv()
+                    if receiver > 0:
+                        self.z_copy(kind, step, slot).start()
+                    self.start_out(kind, slot, index)
+
+                @pl.when(level == receiver + 1)
+                def _():
+                    self.z_copy(kind, step - 1, slot).wait_send()
+
+        return run
+
+    def finish(self, kind, index):
+        slot = lax.rem(index, ZSLOTS)
+        rows = self.z_total.shape[2]
+        pltpu.make_async_copy(
+            self.z_total.at[kind, slot],
+            self.outs[0].at[pl.ds(0, rows), pl.ds(0, COLS)],
+            self.out_sem.at[kind, slot],
+        ).wait()
+
+    def run(self, task):
+        stages = [(self.first, False), (self.second, False)]
+        stages += [(self.middle(step), False) for step in range(2, self.bits)]
+        stages += [(self.last, False)]
+        stages += [(self.z_stage(step), True) for step in range(1, 2 * self.depth + 2)]
+        stages += [(self.finish, True)]
+
+        def iteration(i, carried):
+            for at, (stage, summed_only) in enumerate(stages):
+                index = i - at
+                here = jnp.logical_and(index >= 0, index < self.pairs)
+                if summed_only and self.locals_at:
+                    here = jnp.logical_and(here, jnp.logical_not(self.is_local(index)))
+
+                @pl.when(here)
+                def _():
+                    for kind in range(2):
+                        stage(kind, index)
+
+            if task is not None:
+                task(i)
+            return carried
+
+        lax.fori_loop(0, self.pairs + len(stages) - 1, iteration, 0)
+
+
+def reduce_kernel(entries, row_count, shards, *refs):
+    count = len(entries)
+    xs, gs, outs = refs[:count], refs[count : 2 * count], refs[2 * count : 3 * count]
+    load_x, load_g, *scratch = refs[3 * count :]
+    exchange = Exchange(entries, row_count, shards, outs, scratch)
+    copies = []
+    for at, (x_first, x_count, g_first, g_count, _) in enumerate(entries):
+        x_part = exchange.x_all.at[:, :, pl.ds(x_first, x_count)]
+        g_part = exchange.g_all.at[:, pl.ds(g_first * COLS, g_count * COLS)]
+        copies.append(pltpu.make_async_copy(xs[at], x_part, load_x.at[at]))
+        copies.append(pltpu.make_async_copy(gs[at], g_part, load_g.at[at]))
+    for copy in copies:
+        copy.start()
+    exchange.meet()
+    for copy in copies:
+        copy.wait()
+    exchange.run(None)
+
+
+def reduce_gradients(pairs, row_count, shards, collective_id):
+    block_rows, tokens = pairs[0][0].shape[3:]
+    entries, x_blocks, g_blocks, chunks = reduce_entries(
+        [(x.shape[2], g.shape[1] // COLS) for x, g in pairs]
+    )
+    return pl.pallas_call(
+        functools.partial(reduce_kernel, entries, row_count, shards),
+        out_shape=[
+            jax.ShapeDtypeStruct((x_count * block_rows, g_count * COLS), jnp.bfloat16)
+            for _, x_count, _, g_count, _ in entries
+        ],
         in_specs=[pl.BlockSpec(memory_space=pl.ANY)] * (2 * len(pairs)),
-        out_specs=pl.BlockSpec(memory_space=pl.ANY),
+        out_specs=[pl.BlockSpec(memory_space=pl.ANY)] * len(pairs),
         scratch_shapes=[
             pltpu.SemaphoreType.DMA((len(pairs),)),
             pltpu.SemaphoreType.DMA((len(pairs),)),
-            pltpu.VMEM((shards // 2, 2, x_blocks, block_rows, tokens), jnp.bfloat16),
-            pltpu.VMEM((tokens, g_blocks * COLS), jnp.bfloat16),
-            pltpu.VMEM((2, SLOTS, shards // 2) + block, jnp.bfloat16),
-            pltpu.VMEM((2, SLOTS, shards // 2) + block, jnp.bfloat16),
-            *comm,
-            *[pltpu.VMEM((2, ZSLOTS) + block, jnp.bfloat16) for _ in range(5)],
-            pltpu.SemaphoreType.DMA((2, bits, SLOTS)),
-            pltpu.SemaphoreType.DMA((2, bits, SLOTS)),
-            pltpu.SemaphoreType.DMA((2, z_steps, ZSLOTS)),
-            pltpu.SemaphoreType.DMA((2, z_steps, ZSLOTS)),
-            pltpu.SemaphoreType.DMA((2, ZSLOTS)),
+            *exchange_scratch(row_count, shards, block_rows, x_blocks, g_blocks, tokens),
         ],
         compiler_params=pltpu.CompilerParams(
             collective_id=collective_id, has_side_effects=True, vmem_limit_bytes=52 * 2**20
@@ -653,13 +751,6 @@
             transcendentals=0,
         ),
     )(*[x for x, _ in pairs], *[g for _, g in pairs])
-    pieces = []
-    for _, x_count, _, g_count, chunk in entries:
-        piece = result[chunk : chunk + x_count * g_count].reshape((g_count, x_count) + block)
-        pieces.append(
-            piece.transpose(1, 2, 0, 3).reshape(x_count * block_rows, g_count * COLS)
-        )
-    return pieces
 
 
 def body(
@@ -820,6 +911,845 @@
     )
 
 
+def dot_nt(left, right):
+    return lax.dot_general(
+        left, right, (((1,), (1,)), ((), ())), preferred_element_type=jnp.float32
+    )
+
+
+def dot_tn(left, right):
+    return lax.dot_general(
+        left, right, (((0,), (0,)), ((), ())), preferred_element_type=jnp.float32
+    )
+
+
+def lanes_below(shape, bound, period):
+    return lax.rem(lax.broadcasted_iota(jnp.int32, shape, len(shape) - 1), period) < bound
+
+
+def two_heads(pair, low):
+    pair = pair.astype(jnp.float32)
+    turned = pltpu.roll(pair, HEAD_DIM, 1)
+    first = lanes_below(pair.shape, HEAD_DIM, 2 * HEAD_DIM)
+    if low:
+        parts = [jnp.where(first, pair, 0.0), jnp.where(first, turned, 0.0)]
+    else:
+        parts = [jnp.where(first, 0.0, turned), jnp.where(first, 0.0, pair)]
+    return jnp.concatenate(parts, axis=0).astype(jnp.bfloat16)
+
+
+BACKWARD_STARTS = {
+    "second": 0,
+    "attend_output": 9,
+    "attention": 11,
+    "queries": 19,
+    "keys": 24,
+    "first": 25,
+    "mixer_output": 34,
+    "halo": 36,
+    "mixer_input": 37,
+    "close": 40,
+}
+LOCAL_PAIRS = (15, 16, 19, 20)
+
+
+def backward_kernel(names, entries, row_count, shards, *refs):
+    at = types.SimpleNamespace(**dict(zip(names, refs)))
+    outs = refs[len(names) : len(names) + len(entries)]
+    token_out = refs[len(names) + len(entries)]
+    scratch = refs[len(names) + len(entries) + 1 :]
+    (
+        tiles_a,
+        tiles_b,
+        tiles_c,
+        saved,
+        keys_values,
+        key_grads,
+        key_sums,
+        queries,
+        attended_grad,
+        wide,
+        mask,
+        queries_raw,
+        keys_raw,
+        gradient,
+        normed_grad,
+        hidden,
+        halo_out,
+        halo_in,
+        small,
+        tile_sem,
+        load_sem,
+        halo_sem,
+        *scratch,
+    ) = scratch
+    local = types.SimpleNamespace()
+    exchange = Exchange(entries, row_count, shards, outs, scratch, LOCAL_PAIRS, local)
+    x_all, g_all = exchange.x_all, exchange.g_all
+    seq, row = exchange.seq, exchange.row
+    tokens, width = gradient.shape
+    rows = keys_values.shape[0]
+    length = tokens // rows
+    hidden_blocks = at.first_gate.shape[1] // COLS
+    blocks = width // COLS
+    g_at = [entry[2] * COLS for entry in entries]
+    second_down, second_wide, output_at, heads_at, first_down, first_wide = g_at[:6]
+    mixer_out_at, mixer_in_at, small_at = g_at[6:]
+    starts = BACKWARD_STARTS
+
+    def local_place(kind, index):
+        first, second, third, fourth = LOCAL_PAIRS
+        row_at = jnp.where(index >= third, 1, 0)
+        quad = jnp.where(jnp.logical_or(index == second, index == fourth), 1, 0)
+        return row_at, pl.ds(pl.multiple_of(quad * COLS, COLS), COLS)
+
+    def part(kind, index, side):
+        row_at, columns = local_place(kind, index)
+        return key_grads[row_at, :, side, kind, :, columns]
+
+    def take(kind, index, total):
+        row_at, columns = local_place(kind, index)
+        key_sums[row_at, kind, :, columns] = total
+
+    local.part, local.take = part, take
+
+    def tile_copies(name, j, slot):
+        columns = pl.ds(pl.multiple_of(j * COLS, COLS), COLS)
+        a, b, c = tiles_a.at[slot], tiles_b.at[slot], tiles_c.at[slot]
+        if name in ("second", "first"):
+            down, gate, up, gate_value, up_value = (
+                (at.second_down, at.second_gate, at.second_up, at.gate_two, at.up_two)
+                if name == "second"
+                else (at.first_down, at.first_gate, at.first_up, at.gate_one, at.up_one)
+            )
+            moves = [
+                (down.at[columns], a),
+                (gate.at[:, columns], b),
+                (up.at[:, columns], c),
+                (gate_value.at[:, columns], saved.at[slot, 0]),
+                (up_value.at[:, columns], saved.at[slot, 1]),
+            ]
+        elif name == "attend_output":
+            moves = [(at.attend_output.at[columns], a)]
+        elif name == "mixer_output":
+            moves = [(at.mixer_output.at[columns], a)]
+        elif name == "queries":
+            moves = [
+                (at.query_weight.at[:, pl.ds(0, COLS)], b),
+                (at.query_weight.at[:, pl.ds(COLS, COLS)], c),
+            ]
+        elif name == "keys":
+            moves = [(at.key_weight, b), (at.value_weight, c)]
+        else:
+            even = pl.multiple_of(2 * j * COLS, COLS)
+            odd = pl.multiple_of((2 * j + 1) * COLS, COLS)
+            moves = [
+                (at.mixer_input.at[:, pl.ds(even, COLS)], b),
+                (at.mixer_input.at[:, pl.ds(odd, COLS)], c),
+            ]
+        return [
+            pltpu.make_async_copy(source, target, tile_sem.at[slot, place])
+            for place, (source, target) in enumerate(moves)
+        ]
+
+    steps = [
+        ("second", hidden_blocks),
+        ("attend_output", blocks),
+        ("queries", 1),
+        ("keys", 1),
+        ("first", hidden_blocks),
+        ("mixer_output", blocks),
+        ("mixer_input", 3 * blocks // 2),
+    ]
+    first_step, total = {}, 0
+    for name, number in steps:
+        first_step[name] = total
+        total += number
+    order = [name for name, _ in steps]
+    numbers = dict(steps)
+
+    def tile_step(name, j):
+        slot = lax.rem(first_step[name] + j, 2)
+        for copy in tile_copies(name, j, slot):
+            copy.wait()
+
+        @pl.when(j + 1 < numbers[name])
+        def _():
+            for copy in tile_copies(name, j + 1, 1 - slot):
+                copy.start()
+
+        if name != order[-1]:
+            following = order[order.index(name) + 1]
+
+            @pl.when(j + 1 == numbers[name])
+            def _():
+                for copy in tile_copies(following, 0, 1 - slot):
+                    copy.start()
+
+        return slot
+
+    def load(place, source, target):
+        return pltpu.make_async_copy(source, target, load_sem.at[place])
+
+    count = len(entries)
+    x_loads = [
+        load(number, at.xs[number], x_all.at[:, :, pl.ds(x_first, x_count)])
+        for number, (x_first, x_count, _, _, _) in enumerate(entries)
+    ]
+    cotangent_load = load(count, at.cotangent, g_all.at[:, pl.ds(second_down, width)])
+    middle_loads = [
+        load(count + 1, at.queries_low, queries),
+        load(count + 2, at.keys_values, keys_values),
+        load(count + 3, at.mask, mask),
+        load(count + 4, at.queries_raw, queries_raw),
+        load(count + 5, at.keys_raw, keys_raw),
+    ]
+    late_loads = [
+        load(count + 6, at.mixer_saved, keys_values.at[0]),
+        load(count + 7, at.projected, keys_values.at[1, pl.ds(0, 3 * tokens)]),
+    ]
+    hidden_loads = [
+        load(count + 8, source, hidden)
+        for source in (at.hidden_three, at.hidden_two, at.hidden_one, at.hidden_zero)
+    ]
+    out_copy = load(count + 9, attended_grad, token_out)
+
+    x_loads[0].start()
+    cotangent_load.start()
+    for copy in tile_copies("second", 0, 0):
+        copy.start()
+    for copy in x_loads[1:] + middle_loads + hidden_loads[:1]:
+        copy.start()
+    normed_grad[...] = jnp.zeros_like(normed_grad)
+    small[...] = jnp.zeros_like(small)
+    g_all[:, pl.ds(small_at, COLS)] = jnp.zeros((tokens, COLS), jnp.bfloat16)
+    exchange.meet()
+    x_loads[0].wait()
+    cotangent_load.wait()
+    gradient[...] = g_all[:, pl.ds(second_down, width)].astype(jnp.float32)
+
+    def low_gradient(place):
+        g_all[:, pl.ds(place, width)] = gradient[...].astype(jnp.bfloat16)
+
+    def norm_back(number):
+        hidden_loads[number].wait()
+        gain = at.gains[number : number + 1, :]
+        sums = jnp.zeros((1, width), jnp.float32)
+        piece = 64
+        for first in range(0, tokens, piece):
+            span = pl.ds(first, piece)
+            value, upper = hidden[span], normed_grad[span]
+            inverse = lax.rsqrt(jnp.mean(value * value, axis=-1, keepdims=True) + EPS)
+            value = value * inverse
+            sums = sums + jnp.sum(upper * value, axis=0, keepdims=True)
+            upper = upper * gain
+            shift = jnp.mean(upper * value, axis=-1, keepdims=True)
+            gradient[span] = gradient[span] + inverse * (upper - value * shift)
+        for block in range(blocks):
+            place = blocks * number + block
+            small[place : place + 1, :] = sums[:, block * COLS : (block + 1) * COLS]
+        normed_grad[...] = jnp.zeros_like(normed_grad)
+        if number + 1 < len(hidden_loads):
+            hidden_loads[number + 1].start()
+
+    def feed_tile(name, j, gradient_at, wide_at):
+        slot = tile_step(name, j)
+        low = g_all[:, pl.ds(gradient_at, width)]
+        active_grad = dot_nt(low, tiles_a[slot])
+        gate_value = saved[slot, 0].astype(jnp.float32)
+        up_value = saved[slot, 1].astype(jnp.float32)
+        share = 1.0 / (1.0 + jnp.exp(-gate_value))
+        up_grad = (active_grad * gate_value * share).astype(jnp.bfloat16)
+        gate_grad = active_grad * up_value * share * (1.0 + gate_value * (1.0 - share))
+        gate_grad = gate_grad.astype(jnp.bfloat16)
+        gate_place = pl.multiple_of(wide_at + j * COLS, COLS)
+        up_place = pl.multiple_of(wide_at + (hidden_blocks + j) * COLS, COLS)
+        g_all[:, pl.ds(gate_place, COLS)] = gate_grad
+        g_all[:, pl.ds(up_place, COLS)] = up_grad
+        normed_grad[...] += dot_nt(gate_grad, tiles_b[slot]) + dot_nt(up_grad, tiles_c[slot])
+
+    def output_tile(name, j, gradient_at, target):
+        slot = tile_step(name, j)
+        low = g_all[:, pl.ds(gradient_at, width)]
+        value = dot_nt(low, tiles_a[slot])
+        target[:, j * COLS : (j + 1) * COLS] = value.astype(target.dtype)
+
+    def attention_head(row_at, head):
+        span = pl.ds(pl.multiple_of(row_at * length, length), length)
+        columns = pl.ds(pl.multiple_of(head * 2 * HEAD_DIM, 2 * HEAD_DIM), 2 * HEAD_DIM)
+        query = two_heads(queries[span, columns], True)
+        upper = two_heads(attended_grad[span, columns], False)
+        both = keys_values[row_at, :, columns]
+        weights = jnp.exp(dot_nt(both, query)) * mask[row_at].astype(jnp.float32)
+        weights = weights * (1.0 / jnp.sum(weights, axis=0, keepdims=True))
+        weight_grad_value = dot_nt(both, upper)
+        delta = jnp.sum(weights * weight_grad_value, axis=0, keepdims=True)
+        score_grad = (weights * (weight_grad_value - delta)).astype(jnp.bfloat16)
+        both_grad = jnp.dot(score_grad, query, preferred_element_type=jnp.float32)
+        both_grad += jnp.dot(
+            weights.astype(jnp.bfloat16), upper, preferred_element_type=jnp.float32
+        )
+        shape = key_grads.shape[1:5] + (2 * HEAD_DIM,)
+        key_grads[row_at, :, :, :, :, columns] = both_grad.astype(jnp.bfloat16).reshape(shape)
+        query_grad = dot_tn(score_grad, both) * HEAD_DIM ** (-0.5)
+        first = lanes_below((length, 2 * HEAD_DIM), HEAD_DIM, 2 * HEAD_DIM)
+        wide[span, columns] = jnp.where(
+            first, query_grad[:length], pltpu.roll(query_grad[length:], HEAD_DIM, 1)
+        )
+
+    lane = 2 * HEAD_DIM
+    head_of = lax.broadcasted_iota(jnp.int32, (lane, lane), 0) // HEAD_DIM
+    ones = head_of == lax.broadcasted_iota(jnp.int32, (lane, lane), 1) // HEAD_DIM
+    ones = ones.astype(jnp.float32).astype(jnp.bfloat16)
+
+    def head_mean(value):
+        total = jnp.dot(value.astype(jnp.bfloat16), ones, preferred_element_type=jnp.float32)
+        return total * (1.0 / HEAD_DIM)
+
+    def head_back(value, raw, gain):
+        half = HEAD_DIM // 2
+        first = lanes_below(value.shape, half, HEAD_DIM)
+        turned = jnp.where(first, pltpu.roll(value, lane - half, 1), pltpu.roll(value, half, 1))
+        value = value * at.cosine[...] - turned * at.sine[...]
+        raw = raw.astype(jnp.float32)
+        inverse = lax.rsqrt(head_mean(raw * raw) + EPS)
+        raw = raw * inverse
+        sums = jnp.sum(value * raw, axis=0, keepdims=True)
+        value = value * gain
+        return inverse * (value - raw * head_mean(value * raw)), sums
+
+    def both_halves(sums):
+        return sums + pltpu.roll(sums, HEAD_DIM, 1)
+
+    head_row = 7 * blocks
+
+    def query_heads():
+        sums = jnp.zeros((8, lane), jnp.float32)
+        for part_at in range(0, width, lane):
+            columns = pl.ds(part_at, lane)
+            value, more = head_back(wide[:, columns], queries_raw[:, columns], at.head_gains[0:1])
+            g_all[:, pl.ds(heads_at + part_at, lane)] = value.astype(jnp.bfloat16)
+            sums = sums + more
+        small[head_row : head_row + 1, 0:lane] = both_halves(sums)[0:1]
+
+    def key_heads():
+        sums = jnp.zeros((8, lane), jnp.float32)
+        first = lanes_below((tokens, lane), HEAD_DIM, lane)
+        for pair in range(width // lane // 2):
+            even, odd = [
+                key_sums[:, :, :, pl.ds((2 * pair + which) * lane, lane)].reshape(tokens, lane)
+                for which in range(2)
+            ]
+            key_value = jnp.where(first, even, pltpu.roll(odd, HEAD_DIM, 1))
+            value_value = jnp.where(first, pltpu.roll(even, HEAD_DIM, 1), odd)
+            columns = pl.ds(pair * lane, lane)
+            value, more = head_back(key_value, keys_raw[:, columns], at.head_gains[1:2])
+            place = heads_at + width + pair * lane
+            g_all[:, pl.ds(place, lane)] = value.astype(jnp.bfloat16)
+            place += width // 2
+            g_all[:, pl.ds(place, lane)] = value_value.astype(jnp.bfloat16)
+            sums = sums + more
+        small[head_row : head_row + 1, lane : 2 * lane] = both_halves(sums)[0:1]
+
+    def project_back(name, j, even_at, odd_at):
+        slot = tile_step(name, j)
+        normed_grad[...] += dot_nt(g_all[:, pl.ds(even_at, COLS)], tiles_b[slot]) + dot_nt(
+            g_all[:, pl.ds(odd_at, COLS)], tiles_c[slot]
+        )
+
+    def halo_copy():
+        return pltpu.make_async_remote_copy(
+            src_ref=halo_out,
+            dst_ref=halo_in,
+            send_sem=halo_sem.at[0],
+            recv_sem=halo_sem.at[1],
+            device_id=(row, jnp.maximum(seq - 1, 0)),
+            device_id_type=MESH,
+        )
+
+    def saved_part(number, columns):
+        return keys_values[0, pl.ds(number * tokens, tokens), columns].astype(jnp.float32)
+
+    def projected_part(number, columns):
+        return keys_values[1, pl.ds(number * tokens, tokens), columns].astype(jnp.float32)
+
+    def convolution_back():
+        within = lax.rem(lax.broadcasted_iota(jnp.int32, (tokens, lane), 0), length)
+        edge = lax.broadcasted_iota(jnp.int32, (8, lane), 0)
+        for part_at in range(0, width, lane):
+            columns = pl.ds(part_at, lane)
+            gated_grad = wide[:, columns]
+            exit_grad = gated_grad * saved_part(0, columns)
+            place = mixer_in_at + width + part_at
+            g_all[:, pl.ds(place, lane)] = exit_grad.astype(jnp.bfloat16)
+            conv_grad = gated_grad * projected_part(1, columns)
+            block, inside = part_at // COLS, part_at % COLS
+            for tap in range(3):
+                sums = jnp.sum(conv_grad * saved_part(1 + tap, columns), axis=0, keepdims=True)
+                place = blocks * (4 + tap) + block
+                small[place : place + 1, inside : inside + lane] = sums
+            two = at.taps[0:1, columns] * at.keep[1] * conv_grad
+            one = at.taps[1:2, columns] * at.keep[0] * conv_grad
+            here = at.taps[2:3, columns] * conv_grad
+            here += jnp.where(within < length - 1, pltpu.roll(one, tokens - 1, 0), 0.0)
+            here += jnp.where(within < length - 2, pltpu.roll(two, tokens - 2, 0), 0.0)
+            normed_grad[:, columns] = here
+            for which in range(rows):
+                span = slice(which * length, which * length + 8)
+                sent = two[span] + jnp.where(edge == 1, pltpu.roll(one[span], 1, 0), 0.0)
+                halo_out[which, :, columns] = jnp.where(edge < 2, sent, 0.0)
+
+        @pl.when(seq > 0)
+        def _():
+            halo_copy().start()
+
+    def product_back():
+        @pl.when(seq < shards - 1)
+        def _():
+            halo_copy().wait_recv()
+            for which in range(rows):
+                span = pl.ds((which + 1) * length - 8, 8)
+                normed_grad[span] = normed_grad[span] + pltpu.roll(halo_in[which], 6, 0)
+
+        @pl.when(seq > 0)
+        def _():
+            halo_copy().wait_send()
+
+        for part_at in range(0, width, lane):
+            columns = pl.ds(part_at, lane)
+            product_grad = normed_grad[:, columns]
+            entry_grad = product_grad * projected_part(2, columns)
+            carrier_grad = product_grad * projected_part(0, columns)
+            g_all[:, pl.ds(mixer_in_at + part_at, lane)] = entry_grad.astype(jnp.bfloat16)
+            place = mixer_in_at + 2 * width + part_at
+            g_all[:, pl.ds(place, lane)] = carrier_grad.astype(jnp.bfloat16)
+        normed_grad[...] = jnp.zeros_like(normed_grad)
+
+    def task(i):
+        def when(name, run, after=0, number=1):
+            j = i - (starts[name] + after)
+
+            @pl.when(jnp.logical_and(j >= 0, j < number))
+            def _():
+                run(j)
+
+        when("second", lambda j: feed_tile("second", j, second_down, second_wide), 0, hidden_blocks)
+
+        def waits(j):
+            for copy in x_loads[1:] + middle_loads:
+                copy.wait()
+
+        when("second", waits, hidden_blocks - 1)
+
+        def to_attended(j):
+            norm_back(0)
+            low_gradient(output_at)
+            output_tile("attend_output", 0, output_at, attended_grad)
+
+        when("attend_output", to_attended)
+        when("attend_output", lambda j: output_tile("attend_output", 1, output_at, attended_grad), 1)
+
+        def attention(j):
+            pairs = KV_HEADS // 2
+            for which in range(2):
+                attention_head(j // pairs, 2 * lax.rem(j, pairs) + which)
+
+        when("attention", attention, 0, rows * KV_HEADS // 2)
+
+        def to_queries(j):
+            for copy in late_loads:
+                copy.start()
+            query_heads()
+
+        when("queries", to_queries)
+        when("queries", lambda j: project_back("queries", 0, heads_at, heads_at + COLS), 1)
+
+        def to_keys(j):
+            key_heads()
+            project_back("keys", 0, heads_at + width, heads_at + width + COLS)
+            norm_back(1)
+            low_gradient(first_down)
+
+        when("keys", to_keys)
+        when("first", lambda j: feed_tile("first", j, first_down, first_wide), 0, hidden_blocks)
+
+        def to_gated(j):
+            norm_back(2)
+            low_gradient(mixer_out_at)
+            output_tile("mixer_output", 0, mixer_out_at, wide)
+            for copy in late_loads:
+                copy.wait()
+
+        when("mixer_output", to_gated)
+
+        def to_convolved(j):
+            output_tile("mixer_output", 1, mixer_out_at, wide)
+            convolution_back()
+
+        when("mixer_output", to_convolved, 1)
+        when("halo", lambda j: product_back())
+
+        def mixer_tile(j):
+            even = pl.multiple_of(mixer_in_at + 2 * j * COLS, COLS)
+            project_back("mixer_input", j, even, pl.multiple_of(even + COLS, COLS))
+
+        when("mixer_input", mixer_tile, 0, numbers["mixer_input"])
+
+        def close(j):
+            norm_back(3)
+            attended_grad[...] = gradient[...].astype(jnp.bfloat16)
+            out_copy.start()
+            g_all[pl.ds(0, small.shape[0]), pl.ds(small_at, COLS)] = small[...].astype(jnp.bfloat16)
+
+        when("close", close)
+        when("close", lambda j: out_copy.wait(), 1)
+
+    exchange.run(task)
+
+
+def backward(groups, arrays, resident, row_count, shards, collective_id):
+    xs = [x for x, _ in groups]
+    block_rows, tokens = xs[0].shape[3:]
+    width = arrays["cotangent"].shape[1]
+    entries, x_blocks, g_blocks, chunks = reduce_entries(
+        [(x.shape[2], columns // COLS) for x, columns in groups]
+    )
+    names = ["xs_%d" % number for number in range(len(xs))] + list(arrays)
+    values = list(xs) + list(arrays.values())
+    rows, total_length = arrays["keys_values"].shape[:2]
+    any_space = pl.BlockSpec(memory_space=pl.ANY)
+    vmem_space = pl.BlockSpec(memory_space=pltpu.VMEM)
+    key_blocks = total_length // shards // block_rows
+
+    def kernel(*refs):
+        xs_refs, others = refs[: len(xs)], refs[len(xs) : len(values)]
+        named = [("xs", xs_refs)] + list(zip(arrays, others))
+        backward_kernel(
+            [name for name, _ in named],
+            entries,
+            row_count,
+            shards,
+            *[ref for _, ref in named],
+            *refs[len(values) :],
+        )
+
+    low, full = jnp.bfloat16, jnp.float32
+    return pl.pallas_call(
+        kernel,
+        out_shape=[
+            jax.ShapeDtypeStruct((x_count * block_rows, g_count * COLS), low)
+            for _, x_count, _, g_count, _ in entries
+        ]
+        + [jax.ShapeDtypeStruct((tokens, width), low)],
+        in_specs=[vmem_space if name in resident else any_space for name in names],
+        out_specs=[any_space] * (len(entries) + 1),
+        scratch_shapes=[
+            pltpu.VMEM((2, COLS, width), low),
+            pltpu.VMEM((2, width, COLS), low),
+            pltpu.VMEM((2, width, COLS), low),
+            pltpu.VMEM((2, 2, tokens, COLS), low),
+            pltpu.VMEM((rows, total_length, width), low),
+            pltpu.VMEM((rows, shards // 2, 2, key_blocks, block_rows, width), low),
+            pltpu.VMEM((rows, key_blocks, block_rows, width), full),
+            pltpu.VMEM((tokens, width), low),
+            pltpu.VMEM((tokens, width), low),
+            pltpu.VMEM((tokens, width), full),
+            pltpu.VMEM((rows, total_length, 2 * tokens // rows), low),
+            pltpu.VMEM((tokens, width), low),
+            pltpu.VMEM((tokens, width // 2), low),
+            pltpu.VMEM((tokens, width), full),
+            pltpu.VMEM((tokens, width), full),
+            pltpu.VMEM((tokens, width), full),
+            pltpu.VMEM((rows, 8, width), full),
+            pltpu.VMEM((rows, 8, width), full),
+            pltpu.VMEM((16, COLS), full),
+            pltpu.SemaphoreType.DMA((2, 5)),
+            pltpu.SemaphoreType.DMA((len(entries) + 10,)),
+            pltpu.SemaphoreType.DMA((2,)),
+            *exchange_scratch(row_count, shards, block_rows, x_blocks, g_blocks, tokens),
+        ],
+        compiler_params=pltpu.CompilerParams(
+            collective_id=collective_id, has_side_effects=True, vmem_limit_bytes=63 * 2**20
+        ),
+        cost_estimate=pl.CostEstimate(
+            flops=4 * chunks * shards * block_rows * COLS * tokens,
+            bytes_accessed=2 * chunks * shards * block_rows * COLS,
+            transcendentals=0,
+        ),
+    )(*values)
+
+
+def attention_kernel(query_ref, both_ref, mask_ref, out_ref):
+    query = two_heads(query_ref[...], True)
+    both = both_ref[0]
+    allowed = mask_ref[0].astype(jnp.float32)
+    weights = jnp.exp(dot_nt(query, both)) * jnp.concatenate([allowed, allowed], axis=0)
+    weights = weights * (1.0 / jnp.sum(weights, axis=-1, keepdims=True))
+    value = jnp.dot(weights.astype(jnp.bfloat16), both, preferred_element_type=jnp.float32)
+    length = out_ref.shape[0]
+    first = lanes_below((length, 2 * HEAD_DIM), HEAD_DIM, 2 * HEAD_DIM)
+    out_ref[...] = jnp.where(
+        first, pltpu.roll(value[:length], HEAD_DIM, 1), value[length:]
+    ).astype(out_ref.dtype)
+
+
+def attention(queries, keys_values, mask):
+    rows, total_length, width = keys_values.shape
+    length = queries.shape[0] // rows
+    lane = 2 * HEAD_DIM
+    return pl.pallas_call(
+        attention_kernel,
+        grid=(rows, width // lane),
+        in_specs=[
+            pl.BlockSpec((length, lane), lambda r, h: (r, h)),
+            pl.BlockSpec((1, total_length, lane), lambda r, h: (r, 0, h)),
+            pl.BlockSpec((1, length, total_length), lambda r, h: (r, 0, 0)),
+        ],
+        out_specs=pl.BlockSpec((length, lane), lambda r, h: (r, h)),
+        out_shape=jax.ShapeDtypeStruct(queries.shape, jnp.bfloat16),
+        compiler_params=pltpu.CompilerParams(vmem_limit_bytes=32 * 2**20),
+        cost_estimate=pl.CostEstimate(
+            flops=8 * queries.shape[0] * total_length * width,
+            bytes_accessed=4 * keys_values.size,
+            transcendentals=2 * queries.shape[0] * total_length * KV_HEADS,
+        ),
+    )(queries, keys_values, mask)
+
+
+def fused_body(
+    tokens,
+    lengths,
+    mixer_gain,
+    mixer_input,
+    mixer_kernel,
+    mixer_output,
+    first_gain,
+    first_gate,
+    first_up,
+    first_down,
+    attend_gain,
+    query_weight,
+    key_weight,
+    value_weight,
+    query_gain,
+    key_gain,
+    attend_output,
+    second_gain,
+    second_gate,
+    second_up,
+    second_down,
+    cotangent,
+):
+    full, low = jnp.float32, jnp.bfloat16
+    rows, length, width = tokens.shape
+    token_count = rows * length
+    row_count, shards = lax.axis_size("row"), lax.axis_size("seq")
+    seq = lax.axis_index("seq")
+    positions = seq * length + jnp.arange(length, dtype=jnp.int32)
+    segment, seg_start = segment_info(lengths, positions)
+    offsets = positions[None, :] - seg_start
+
+    def flat(value):
+        return value.reshape(token_count, -1)
+
+    hidden_zero = tokens.astype(full)
+    mixer_in = norm_rows(hidden_zero, mixer_gain.astype(full)).astype(low)
+    projected = dense(mixer_in, mixer_input)
+    entry, exit_gate, carrier = [
+        projected[..., number * width : (number + 1) * width] for number in range(3)
+    ]
+    product = (entry * carrier).astype(low)
+    previous = passed_along(product[:, length - 2 :, :], "seq", 1)
+    extended = jnp.concatenate([previous, product], axis=1).astype(full)
+    keep_one = (positions[None, :] - 1 >= seg_start).astype(full)[..., None]
+    keep_two = (positions[None, :] - 2 >= seg_start).astype(full)[..., None]
+    taps = mixer_kernel.astype(full)
+    two_back = keep_two * extended[:, :length]
+    one_back = keep_one * extended[:, 1 : length + 1]
+    current = extended[:, 2:]
+    convolved = taps[2] * current + taps[1] * one_back + taps[0] * two_back
+    gated = (exit_gate * convolved).astype(low)
+    hidden_one = hidden_zero + dense(gated, mixer_output)
+    mixer_saved = jnp.concatenate(
+        [flat(part).astype(low) for part in (convolved, two_back, one_back, current)]
+    )
+    projected_saved = jnp.concatenate(
+        [flat(part).astype(low) for part in (entry, exit_gate, carrier)]
+    )
+
+    def feed(hidden, gain, gate_matrix, up_matrix, down_matrix):
+        normed = norm_rows(hidden, gain.astype(full)).astype(low)
+        gate_value, upward = dense(normed, gate_matrix), dense(normed, up_matrix)
+        active = swiglu(gate_value, upward).astype(low)
+        saved = (normed, active, flat(gate_value.astype(low)), flat(upward.astype(low)))
+        return hidden + dense(active, down_matrix), saved
+
+    hidden_two, first_saved = feed(hidden_one, first_gain, first_gate, first_up, first_down)
+
+    attend_in = norm_rows(hidden_two, attend_gain.astype(full)).astype(low)
+    queries_raw, keys_raw = dense(attend_in, query_weight), dense(attend_in, key_weight)
+    values = dense(attend_in, value_weight)
+
+    def head_path(value, heads, gain):
+        value = value.reshape(rows, length, heads, HEAD_DIM)
+        return rotate(norm_rows(value, gain.astype(full)), offsets)
+
+    queries_low = flat(
+        (head_path(queries_raw, HEADS, query_gain).astype(low) * low(HEAD_DIM**-0.5))
+    )
+    keys_low = head_path(keys_raw, KV_HEADS, key_gain).astype(low)
+    values_low = values.astype(low).reshape(keys_low.shape)
+    both = jnp.stack([keys_low, values_low], axis=3).reshape(rows, length, width)
+    keys_values = lax.all_gather(both, "seq", axis=1, tiled=True)
+    total_length = keys_values.shape[1]
+    key_positions = jnp.arange(total_length, dtype=jnp.int32)
+    key_segment, _ = segment_info(lengths, key_positions)
+    allowed = (segment[:, :, None] == key_segment[:, None, :]) & (
+        positions[None, :, None] >= key_positions[None, None, :]
+    )
+    allowed_turned = (segment[:, None, :] == key_segment[:, :, None]) & (
+        positions[None, None, :] >= key_positions[None, :, None]
+    )
+    mask_turned = jnp.concatenate([allowed_turned, allowed_turned], axis=-1).astype(low)
+    attended = attention(queries_low, keys_values, allowed.astype(low))
+    hidden_three = hidden_two + dense(attended.reshape(tokens.shape), attend_output)
+    mixed, second_saved = feed(hidden_three, second_gain, second_gate, second_up, second_down)
+
+    half = HEAD_DIM // 2
+    inverse = THETA ** (-2.0 * jnp.arange(half, dtype=full) / HEAD_DIM)
+    angles = offsets.astype(full).reshape(token_count, 1) * inverse
+    cosine, sine = jnp.cos(angles), jnp.sin(angles)
+    block_rows = math.gcd(width // shards, first_down.shape[0] // shards)
+
+    def turned(inputs):
+        inputs = flat(inputs).T
+        blocks = inputs.shape[0] // shards // block_rows
+        return inputs.reshape(shards // 2, 2, blocks, block_rows, token_count)
+
+    blocks = width // COLS
+    shape = (shards, 2 * block_rows, token_count)
+    shard_at, row_at, token_at = [lax.broadcasted_iota(jnp.int32, shape, dim) for dim in range(3)]
+    wanted = blocks * row_at + jnp.where(row_at < 7, shard_at * blocks // shards, 0)
+    picks = ((row_at < 8) & (token_at == wanted)).astype(low)
+    picks = picks.reshape(shards // 2, 2, 2, block_rows, token_count)
+
+    def padded(value):
+        return jnp.pad(value.astype(full), ((0, 8 - value.shape[0]), (0, 0)))
+
+    lane = 2 * HEAD_DIM
+    arrays = dict(
+        cotangent=flat(cotangent),
+        gate_two=second_saved[2],
+        up_two=second_saved[3],
+        gate_one=first_saved[2],
+        up_one=first_saved[3],
+        hidden_three=flat(hidden_three),
+        hidden_two=flat(hidden_two),
+        hidden_one=flat(hidden_one),
+        hidden_zero=flat(hidden_zero),
+        queries_low=queries_low,
+        keys_values=keys_values,
+        mask=mask_turned,
+        queries_raw=flat(queries_raw).astype(low),
+        keys_raw=flat(keys_raw).astype(low),
+        mixer_saved=mixer_saved,
+        projected=projected_saved,
+        cosine=jnp.concatenate([cosine] * 4, axis=1),
+        sine=jnp.concatenate([-sine, sine] * 2, axis=1),
+        keep=jnp.broadcast_to(
+            jnp.stack([keep_one, keep_two]).reshape(2, token_count, 1), (2, token_count, lane)
+        ),
+        gains=padded(jnp.stack([second_gain, attend_gain, first_gain, mixer_gain])),
+        taps=padded(mixer_kernel),
+        head_gains=padded(jnp.tile(jnp.stack([query_gain, key_gain]), (1, 2))),
+        second_down=second_down,
+        second_gate=second_gate,
+        second_up=second_up,
+        attend_output=attend_output,
+        query_weight=query_weight,
+        key_weight=key_weight,
+        value_weight=value_weight,
+        first_down=first_down,
+        first_gate=first_gate,
+        first_up=first_up,
+        mixer_output=mixer_output,
+        mixer_input=mixer_input,
+    )
+    resident = ("cosine", "sine", "keep", "gains", "taps", "head_gains")
+    hidden_columns = first_gate.shape[1]
+    head_columns = width + 2 * key_weight.shape[1]
+    groups = [
+        (turned(second_saved[1]), width),
+        (turned(second_saved[0]), 2 * hidden_columns),
+        (turned(attended), width),
+        (turned(attend_in), head_columns),
+        (turned(first_saved[1]), width),
+        (turned(first_saved[0]), 2 * hidden_columns),
+        (turned(gated), width),
+        (turned(mixer_in), 3 * width),
+        (picks, COLS),
+    ]
+    (
+        grad_second_down,
+        second_both,
+        grad_attend_output,
+        attend_three,
+        grad_first_down,
+        first_both,
+        grad_mixer_output,
+        grad_mixer_input,
+        sums,
+        token_grad,
+    ) = backward(groups, arrays, resident, row_count, shards, 1)
+
+    def single(value):
+        return value.astype(full)
+
+    share = width // shards
+    vectors = single(
+        lax.dynamic_slice(sums, (0, lax.rem(seq, COLS // share) * share), (7, share))
+    )
+    head_share = HEAD_DIM // shards
+    heads = [
+        single(lax.dynamic_slice(sums, (7, which * lane + seq * head_share), (1, head_share)))[0]
+        for which in range(2)
+    ]
+    key_columns = key_weight.shape[1]
+    return (
+        mixed.astype(low),
+        token_grad.reshape(tokens.shape),
+        vectors[3],
+        single(grad_mixer_input),
+        vectors[4:7],
+        single(grad_mixer_output),
+        vectors[2],
+        single(first_both[:, :hidden_columns]),
+        single(first_both[:, hidden_columns:]),
+        single(grad_first_down),
+        vectors[1],
+        single(attend_three[:, :width]),
+        single(attend_three[:, width : width + key_columns]),
+        single(attend_three[:, width + key_columns :]),
+        heads[0],
+        heads[1],
+        single(grad_attend_output),
+        vectors[0],
+        single(second_both[:, :hidden_columns]),
+        single(second_both[:, hidden_columns:]),
+        single(grad_second_down),
+    )
+
+
+def fused_or_general(*args):
+    tokens = args[0]
+    rows, length, width = tokens.shape
+    row_count, shards = lax.axis_size("row"), lax.axis_size("seq")
+    key_bytes = 2 * rows * length * shards * width
+    if key_bytes <= 4 * 2**20 and shards == 8 and 4 * rows == shards and row_count == 4:
+        return fused_body(*args)
+    return body(*args)
+
+
 def solution(mesh):
     in_specs = (
         P("row", "seq", None),
@@ -868,4 +1798,4 @@
         P("seq", None),
         P("seq", None),
     )
-    return jax.shard_map(body, mesh=mesh, in_specs=in_specs, out_specs=out_specs, check_vma=False)
+    return jax.shard_map(fused_or_general, mesh=mesh, in_specs=in_specs, out_specs=out_specs, check_vma=False)

time: 739 us -> 534 us (0.72); the launches traced: 730 us -> 537 us
  matrix products: 129 us -> 46.2 us
  waiting for transfers between devices: 86.6 us -> 5.89 us
  local copies, waits for them, and re-layouts: 115 us -> 39 us
  Pallas kernels: 320 us -> 385 us
  other arithmetic: 57.4 us -> 43.6 us
    dot_general x21 -> x0, matrix products: 81.3 us -> none  [the longest x12 58.4 us: back_dense(): jnp.einsum('rtf,df->rtd', gradient, matrix, preferred_element_type=jnp.fl...]
    pallas_call x1 -> x2, Pallas kernels: 320 us -> 385 us  [the longest x1 357 us: backward(): pl.pallas_call(kernel, out_shape=[jax.ShapeDtypeStruct((x_count * block_r...]
    unnamed x268 -> x93, local copies, waits for them, and re-layouts: 54 us -> 6.35 us
    unnamed x6 -> x1, waiting for transfers between devices: 47 us -> 0.02 us
    all_gather x2 -> x1, waiting for transfers between devices: 39.5 us -> 5.87 us  [fused_body(): keys_values = lax.all_gather(both, 'seq', axis=1, tiled=True)]
    convert_element_type x15 -> x4, local copies, waits for them, and re-layouts: 19.5 us -> 0.96 us  [the longest x1 0.84 us: fused_body(): values_low = values.astype(low).reshape(keys_low.shape)]
    reduce_sum x4 -> x0, other arithmetic: 8.52 us -> none  [the longest x2 3.97 us: norm_rows(): values * lax.rsqrt(jnp.mean(values * values, axis=-1, keepdims=True) + EPS)]
    slice x14 -> x5, local copies, waits for them, and re-layouts: 12.1 us -> 3.72 us  [the longest x1 2.2 us: fused_body(): projected[..., number * width:(number + 1) * width]]
  transfers between devices with their start and end apart: 6 -> 2, of which waited for: 5 -> 1; matrix products, arithmetic and copies ran while one was open for 12% -> 7% of each run, Pallas kernels for 0% -> 0%
where the time goes in v2:
time: 534 us; the launch traced here: 537 us
  Pallas kernels  385 us (72%)
  matrix products  46.2 us (9%)
  other arithmetic  43.6 us (8%)
  local copies, waits for them, and re-layouts  39 us (7%)
  between operations  15 us (3%)
  waiting for transfers between devices  5.89 us (1%)
    pallas_call x1, Pallas kernels, backward(): pl.pallas_call(kernel, out_shape=[jax.ShapeDtypeStruct((x_count * block_r...  357 us
    dot_general x12, matrix products, dense(): jnp.einsum('rtd,df->rtf', inputs, matrix, preferred_element_type=jnp.floa...  46.2 us
    pallas_call x1, Pallas kernels, attention(): pl.pallas_call(attention_kernel, grid=(rows, width // lane), in_specs=[pl...  27.8 us
    convert_element_type x10, other arithmetic, single(): return value.astype(full)  17.4 us
    reshape x7, local copies, waits for them, and re-layouts, flat(): return value.reshape(token_count, -1)  13.7 us
  transfers between devices with their start and end apart: 2, of which 1 were waited for; matrix products, arithmetic and copies ran while one was open for 7% of the time, Pallas kernels for 0%

profile of v2, /device:TPU:0, one launch (start us, length us, event | category | flops | bytes accessed | tf_op | source)
XLA Modules:
  0.0 537.2 jit_solution(16642412316699406321)
XLA Ops:
  10.4 4.6 fusion.12
  15.0 1.6 copy-done.2
  16.8 2.4 collective-permute-start
  21.5 1.6 fusion.63
  23.2 1.5 multiply_convert_fusion.5
  26.3 6.2 %fusion.10 = f32[2,128,4608]{2,1,0:T(8,128)S(1)} fusion(bf16[2,128,1024]{2,1,0:T(8,128)(2,1)S(1)} %multiply_convert_fusion.4, bf16[1024,4608]{1,0:T(8,128)(2,1)} %refs_39_.1), kind=kOutput, calls=%fused_computation.10 | convolution fusion | flops 2415919104 | bytes 14680064 | tf_op jit(solution)/shard_map/rtd,df->rtf/dot_general | solution.py:65
  32.5 4.6 fusion.66
  37.1 6.2 %multiply_reduce_fusion.2 = (f32[2,128]{1,0:T(2,128)S(1)}, f32[2,128,1024]{2,1,0:T(8,128)S(1)}) fusion(f32[2,128,1024]{2,1,0:T(8,128)S(1)} %get-tuple-element.87, bf16[2,128,4608]{2,1,0:T(8,128)(2,1)S(1)} %get-tuple-element.50, bf16[4608,1024]{1,0:T(8,128)(2,1)} %refs_38_.1), kind=kOutput, calls=%fused_computation.46 | convolution fusion | flops 2416705280 | bytes 13894656 | tf_op jit(solution)/shard_map/rtd,df->rtf/dot_general | solution.py:65
  45.7 2.6 fusion.71
  48.3 2.0 copy.91
  53.7 2.0 copy.95
  66.9 2.2 fusion.68
  69.1 1.3 pad_maximum_fusion.1.refs_24_
  73.9 1.9 fusion.70
  75.8 1.5 copy.89
  80.6 4.5 copy.101
  87.1 2.8 pad_maximum_fusion.refs_23_
  89.8 5.9 %all-gather.2.cloned.1.call-done.both_ref.refs_19_ = bf16[2,1024,1024]{2,1,0:T(8,128)(2,1)} async-done(((bf16[2,128,1024]{2,1,0:T(8,128)(2,1)}), bf16[2,1024,1024]{2,1,0:T(8,128)(2,1)}) %all-gather.2.cloned.1.call-update) | async-done | bytes 4194320 | tf_op jit(solution)/shard_map/all_gather | solution.py:1603
  95.7 2.2 copy-done.1
  97.9 27.8 %shard_map.373 = bf16[256,1024]{1,0:T(8,128)(2,1)S(1)} custom-call(bf16[256,1024]{1,0:T(8,128)(2,1)S(1)} %reshape.523.query_ref.refs_18_, bf16[2,1024,1024]{2,1,0:T(8,128)(2,1)S(1)} %copy-done.1, bf16[2,128,1024]{2,1,0:T(8,128)(2,1)S(1)} %and_convert_fusion.mask_ref), custom_call_target="tpu_custom_call" | custom-call | flops 2147483648 | bytes 8388608 | tf_op jit(solution)/shard_map/pallas_call | solution.py:1500
  126.8 5.8 %fusion.4 = f32[2,128,4608]{2,1,0:T(8,128)S(1)} fusion(bf16[2,128,1024]{2,1,0:T(8,128)(2,1)S(1)} %multiply_convert_fusion.2, bf16[1024,4608]{1,0:T(8,128)(2,1)} %refs_32_.1), kind=kOutput, calls=%fused_computation.4 | convolution fusion | flops 2415919104 | bytes 14680064 | tf_op jit(solution)/shard_map/rtd,df->rtf/dot_general | solution.py:65
  132.7 4.5 fusion.67
  137.2 7.9 %fusion.32 = bf16[2,128,1024]{2,1,0:T(8,128)(2,1)} fusion(f32[2,128,1024]{2,1,0:T(8,128)S(1)} %get-tuple-element.91, bf16[2,128,4608]{2,1,0:T(8,128)(2,1)S(1)} %get-tuple-element.53, bf16[4608,1024]{1,0:T(8,128)(2,1)} %refs_31_.1), kind=kOutput, calls=%fused_computation.29 | convolution fusion | flops 2416443392 | bytes 13369344 | tf_op jit(solution)/shard_map/rtd,df->rtf/dot_general | solution.py:65
  145.1 4.3 copy.97
  152.2 357.3 %shard_map.374 = (bf16[576,1024]{1,0:T(8,128)(2,1)}, bf16[128,9216]{1,0:T(8,128)(2,1)}, bf16[128,1024]{1,0:T(8,128)(2,1)}, bf16[128,2048]{1,0:T(8,128)(2,1)}, bf...) custom-call(bf16[4,2,9,64,256]{4,3,2,1,0:T(8,128)(2,1)} %bitcast.177, ...), custom_call_target="tpu_custom_call" | custom-call | flops 37044092928 | bytes 72351744 | tf_op jit(solution)/shard_map/pallas_call | solution.py:1437
  511.3 1.9 slice_convert_fusion.8
  513.2 1.8 slice_convert_fusion.9
  515.1 2.4 convert_element_type.311
  518.3 2.7 slice_convert_fusion.2
  521.1 1.7 convert_element_type.315
  523.7 2.7 slice_convert_fusion
  526.4 1.7 convert_element_type.322
  (183 shorter events, 42.1 us)
Async XLA Ops:
  7.2 88.5 %all-gather.2.cloned.1.call-start = ((), (), s32[]{:S(2)}) async-start(), calls=%async_computation | async-start | bytes 4718592 | tf_op jit(solution)/shard_map/all_gather | solution.py:1603
  16.6 4.2 copy-start.31
  16.6 4.2 copy-start.38
  16.8 4.6 collective-permute-start
  23.2 9.3 %slice-start = ((s8[9437184]{0:T(1024)(128)(4,1)}), s8[4194304]{0:T(1024)(128)(4,1)S(1)}, s32[]{:S(2)}) async-start(s8[9437184]{0:T(1024)(128)(4,1)} %bitcast.204), calls=%async_computation.1 | async-start | bytes 8388608
  26.1 11.0 %copy-start.6 = (f32[2,128,1024]{2,1,0:T(8,128)}, f32[2,128,1024]{2,1,0:T(8,128)S(1)}, u32[]{:S(2)}) copy-start(f32[2,128,1024]{2,1,0:T(8,128)S(1)} %get-tuple-element.87) | copy-start | bytes 3145732
  26.1 6.4 %slice-start.1 = ((s8[9437184]{0:T(1024)(128)(4,1)}), s8[4194304]{0:T(1024)(128)(4,1)S(1)}, s32[]{:S(2)}) async-start(s8[9437184]{0:T(1024)(128)(4,1)} %bitcast.204), calls=%async_computation.2 | async-start | bytes 8388608
  26.3 6.2 %copy-start.4 = (bf16[2,128,1024]{2,1,0:T(8,128)(2,1)}, bf16[2,128,1024]{2,1,0:T(8,128)(2,1)S(1)}, u32[]{:S(2)}) copy-start(bf16[2,128,1024]{2,1,0:T(8,128)(2,1)S(1)} %multiply_convert_fusion.4) | copy-start | bytes 1572868
  26.3 6.2 %slice-start.2 = ((s8[9437184]{0:T(1024)(128)(4,1)}), s8[1048576]{0:T(1024)(128)(4,1)S(1)}, s32[]{:S(2)}) async-start(s8[9437184]{0:T(1024)(128)(4,1)} %bitcast.204), calls=%async_computation.3 | async-start | bytes 2097152
  37.1 6.2 %copy-start.12 = (bf16[2,128,4608]{2,1,0:T(8,128)(2,1)}, bf16[2,128,4608]{2,1,0:T(8,128)(2,1)S(1)}, u32[]{:S(2)}) copy-start(bf16[2,128,4608]{2,1,0:T(8,128)(2,1)S(1)} %get-tuple-element.50) | copy-start | bytes 7077892
  37.1 7.3 %copy-start.21 = (bf16[1024,512]{1,0:T(8,128)(2,1)S(1)}, bf16[1024,512]{1,0:T(8,128)(2,1)}, u32[]{:S(2)}) copy-start(bf16[1024,512]{1,0:T(8,128)(2,1)} %refs_37_.1) | copy-start | bytes 3145732
  45.7 7.0 %copy-start.22 = (bf16[2,128,512]{1,2,0:T(8,128)(2,1)S(1)}, bf16[2,128,512]{1,2,0:T(8,128)(2,1)}, u32[]{:S(2)}) copy-start(bf16[2,128,512]{1,2,0:T(8,128)(2,1)} %copy.93) | copy-start | bytes 786436
  52.7 8.1 %copy-start.36 = (pred[2,128]{1,0:T(4,128)(4,1)S(1)}, pred[2,128]{1,0:T(4,128)(4,1)}, u32[]{:S(2)}) copy-start(pred[2,128]{1,0:T(4,128)(4,1)} %get-tuple-element.85) | copy-start | bytes 772
  52.8 8.1 %copy-start.35 = (pred[2,128]{1,0:T(4,128)(4,1)S(1)}, pred[2,128]{1,0:T(4,128)(4,1)}, u32[]{:S(2)}) copy-start(pred[2,128]{1,0:T(4,128)(4,1)} %get-tuple-element.46) | copy-start | bytes 772
  52.8 8.7 %copy-start.37 = (bf16[64]{0:T(256)(128)(2,1)S(1)}, bf16[64]{0:T(256)(128)(2,1)}, u32[]{:S(2)}) copy-start(bf16[64]{0:T(256)(128)(2,1)} %param.36) | copy-start | bytes 388
  52.8 8.7 %copy-start.39 = (bf16[64]{0:T(256)(128)(2,1)S(1)}, bf16[64]{0:T(256)(128)(2,1)}, u32[]{:S(2)}) copy-start(bf16[64]{0:T(256)(128)(2,1)} %param.37) | copy-start | bytes 388
  52.8 10.1 %copy-start.29 = (s32[2,2]{1,0:T(2,128)S(1)}, s32[2,2]{1,0:T(2,128)}, u32[]{:S(2)}) copy-start(s32[2,2]{1,0:T(2,128)} %copy-done.28) | copy-start | bytes 52
  52.8 10.2 %copy-start.33 = (f32[32]{0:T(128)S(1)}, f32[32]{0:T(128)}, u32[]{:S(2)}) copy-start(f32[32]{0:T(128)} %copy-done.32) | copy-start | bytes 388
  52.8 12.5 %copy-start.27 = (s32[2,128]{1,0:T(2,128)S(1)}, s32[2,128]{1,0:T(2,128)}, u32[]{:S(2)}) copy-start(s32[2,128]{1,0:T(2,128)} %get-tuple-element.41) | copy-start | bytes 3076
  79.6 16.1 %copy-start = (bf16[256,1024]{1,0:T(8,128)(2,1)}, bf16[256,1024]{1,0:T(8,128)(2,1)S(1)}, u32[]{:S(2)}) copy-start(bf16[256,1024]{1,0:T(8,128)(2,1)S(1)} %reshape.523.query_ref.refs_18_) | copy-start | bytes 1572868
  80.6 4.5 copy-start.5
  80.6 6.5 %copy-start.17 = (bf16[2,128,1024]{2,1,0:T(8,128)(2,1)S(1)}, bf16[2,128,1024]{2,1,0:T(8,128)(2,1)}, u32[]{:S(2)}) copy-start(bf16[2,128,1024]{2,1,0:T(8,128)(2,1)} %get-tuple-element.43) | copy-start | bytes 1572868
  80.6 6.5 %copy-start.18 = (bf16[2,128,1024]{2,1,0:T(8,128)(2,1)S(1)}, bf16[2,128,1024]{2,1,0:T(8,128)(2,1)}, u32[]{:S(2)}) copy-start(bf16[2,128,1024]{2,1,0:T(8,128)(2,1)} %get-tuple-element.62) | copy-start | bytes 1572868
  97.9 27.9 %copy-start.8 = (f32[2,128,1024]{2,1,0:T(8,128)S(1)}, f32[2,128,1024]{2,1,0:T(8,128)}, u32[]{:S(2)}) copy-start(f32[2,128,1024]{2,1,0:T(8,128)} %copy-done.7) | copy-start | bytes 3145732
  97.9 27.9 %copy-start.15 = (bf16[1024,1024]{1,0:T(8,128)(2,1)S(1)}, bf16[1024,1024]{1,0:T(8,128)(2,1)}, u32[]{:S(2)}) copy-start(bf16[1024,1024]{1,0:T(8,128)(2,1)} %refs_34_.1) | copy-start | bytes 6291460
  97.9 34.7 %slice-start.3 = ((s8[9437184]{0:T(1024)(128)(4,1)}), s8[4194304]{0:T(1024)(128)(4,1)S(1)}, s32[]{:S(2)}) async-start(s8[9437184]{0:T(1024)(128)(4,1)} %bitcast.206), calls=%async_computation.4 | async-start | bytes 8388608
  125.8 6.9 %slice-start.4 = ((s8[9437184]{0:T(1024)(128)(4,1)}), s8[4194304]{0:T(1024)(128)(4,1)S(1)}, s32[]{:S(2)}) async-start(s8[9437184]{0:T(1024)(128)(4,1)} %bitcast.206), calls=%async_computation.5 | async-start | bytes 8388608
  126.6 10.6 %copy-start.9 = (f32[2,128,1024]{2,1,0:T(8,128)}, f32[2,128,1024]{2,1,0:T(8,128)S(1)}, u32[]{:S(2)}) copy-start(f32[2,128,1024]{2,1,0:T(8,128)S(1)} %get-tuple-element.91) | copy-start | bytes 3145732
  126.8 5.9 %slice-start.5 = ((s8[9437184]{0:T(1024)(128)(4,1)}), s8[1048576]{0:T(1024)(128)(4,1)S(1)}, s32[]{:S(2)}) async-start(s8[9437184]{0:T(1024)(128)(4,1)} %bitcast.206), calls=%async_computation.6 | async-start | bytes 2097152
  137.2 7.9 %copy-start.13 = (bf16[2,128,4608]{2,1,0:T(8,128)(2,1)}, bf16[2,128,4608]{2,1,0:T(8,128)(2,1)S(1)}, u32[]{:S(2)}) copy-start(bf16[2,128,4608]{2,1,0:T(8,128)(2,1)S(1)} %get-tuple-element.53) | copy-start | bytes 7077892
  509.5 8.0 %copy-start.25 = (bf16[128,1024]{1,0:T(8,128)(2,1)S(1)}, bf16[128,1024]{1,0:T(8,128)(2,1)}, u32[]{:S(2)}) copy-start(bf16[128,1024]{1,0:T(8,128)(2,1)} %get-tuple-element.34) | copy-start | bytes 786436
  511.3 7.0 %copy-start.11 = (bf16[128,9216]{1,0:T(8,128)(2,1)S(1)}, bf16[128,9216]{1,0:T(8,128)(2,1)}, u32[]{:S(2)}) copy-start(bf16[128,9216]{1,0:T(8,128)(2,1)} %get-tuple-element.35) | copy-start | bytes 7077892
  (16 other events, 39.0 us)
Sparse Core Ops, SparseCore 0:
  55.9 39.7 all-gather.1

commit v3 on v2

--- a/solution.py
+++ b/solution.py
@@ -411,13 +411,13 @@
     comm = []
     for steps in seq_steps(bits):
         for _, above, below in steps:
-            comm.append(pltpu.VMEM((SLOTS, above, 2, below) + block, jnp.bfloat16))
+            comm.append(pltpu.VMEM((2, above, 2, below) + block, jnp.bfloat16))
             comm.append(pltpu.VMEM((SLOTS, above, below) + block, jnp.bfloat16))
     z_steps = row_count - 1
     return [
         pltpu.VMEM((shards // 2, 2, x_blocks, block_rows, tokens), jnp.bfloat16),
         pltpu.VMEM((tokens, g_blocks * COLS), jnp.bfloat16),
-        pltpu.VMEM((2, SLOTS, shards // 2) + block, jnp.bfloat16),
+        pltpu.VMEM((2, 2, shards // 2) + block, jnp.bfloat16),
         pltpu.VMEM((2, SLOTS, shards // 2) + block, jnp.bfloat16),
         *comm,
         *[pltpu.VMEM((2, ZSLOTS) + block, jnp.bfloat16) for _ in range(5)],
@@ -490,10 +490,11 @@
     def seq_copy(self, kind, step, slot):
         if step == 0:
             bit = 0
-            source, target = self.send_zero.at[kind, slot], self.recv_zero.at[kind, slot]
+            source = self.send_zero.at[kind, lax.rem(slot, 2)]
+            target = self.recv_zero.at[kind, slot]
         else:
             bit = self.kinds[kind][step - 1][0]
-            source = self.held[kind][step - 1].at[slot, :, 1 - self.value[bit]]
+            source = self.held[kind][step - 1].at[lax.rem(slot, 2), :, 1 - self.value[bit]]
             target = self.received[kind][step - 1].at[slot]
         return pltpu.make_async_remote_copy(
             src_ref=source,
@@ -506,7 +507,7 @@
 
     def seq_sum(self, kind, step, slot):
         bit = self.kinds[kind][step - 2][0]
-        mine = self.held[kind][step - 2][slot, :, self.value[bit]].astype(jnp.float32)
+        mine = self.held[kind][step - 2][lax.rem(slot, 2), :, self.value[bit]].astype(jnp.float32)
         return mine + self.received[kind][step - 2][slot].astype(jnp.float32)
 
     def z_copy(self, kind, step, slot):
@@ -548,7 +549,7 @@
         target = self.send_zero
 
         def put():
-            target[kind, slot] = (
+            target[kind, lax.rem(slot, 2)] = (
                 self.product(kind, index, 1 - self.value[0])
                 .astype(jnp.bfloat16)
                 .reshape(target.shape[2:])
@@ -561,7 +562,7 @@
 
             @pl.when(self.is_local(index))
             def _():
-                target[kind, slot] = self.local.part(kind, index, 1 - self.value[0])
+                target[kind, lax.rem(slot, 2)] = self.local.part(kind, index, 1 - self.value[0])
 
         self.seq_copy(kind, 0, slot).start()
 
@@ -573,7 +574,7 @@
         def put():
             mine = self.product(kind, index, self.value[0])
             total = mine + self.recv_zero[kind, slot].astype(jnp.float32).reshape(mine.shape)
-            target[slot] = total.astype(jnp.bfloat16).reshape(target.shape[1:])
+            target[lax.rem(slot, 2)] = total.astype(jnp.bfloat16).reshape(target.shape[1:])
 
         if self.local is None:
             put()
@@ -584,7 +585,7 @@
             def _():
                 mine = self.local.part(kind, index, self.value[0]).astype(jnp.float32)
                 total = mine + self.recv_zero[kind, slot].astype(jnp.float32)
-                target[slot] = total.astype(jnp.bfloat16).reshape(target.shape[1:])
+                target[lax.rem(slot, 2)] = total.astype(jnp.bfloat16).reshape(target.shape[1:])
 
         self.seq_copy(kind, 1, slot).start()
 
@@ -594,7 +595,7 @@
             self.seq_copy(kind, step - 1, slot).wait()
             total = self.seq_sum(kind, step, slot)
             target = self.held[kind][step - 1]
-            target[slot] = total.astype(jnp.bfloat16).reshape(target.shape[1:])
+            target[lax.rem(slot, 2)] = total.astype(jnp.bfloat16).reshape(target.shape[1:])
             self.seq_copy(kind, step, slot).start()
 
         return run
@@ -940,24 +941,24 @@
 
 BACKWARD_STARTS = {
     "second": 0,
-    "attend_output": 9,
-    "attention": 11,
-    "queries": 19,
-    "keys": 24,
-    "first": 25,
-    "mixer_output": 34,
-    "halo": 36,
-    "mixer_input": 37,
-    "close": 40,
+    "attend_output": 8,
+    "attention": 10,
+    "queries": 26,
+    "keys": 31,
+    "first": 32,
+    "mixer_output": 41,
+    "halo": 43,
+    "mixer_input": 44,
+    "close": 47,
 }
-LOCAL_PAIRS = (15, 16, 19, 20)
+LOCAL_PAIRS = (18, 19, 26, 27)
 
 
 def backward_kernel(names, entries, row_count, shards, *refs):
     at = types.SimpleNamespace(**dict(zip(names, refs)))
     outs = refs[len(names) : len(names) + len(entries)]
-    token_out = refs[len(names) + len(entries)]
-    scratch = refs[len(names) + len(entries) + 1 :]
+    token_out, mixed_out = refs[len(names) + len(entries) : len(names) + len(entries) + 2]
+    scratch = refs[len(names) + len(entries) + 2 :]
     (
         tiles_a,
         tiles_b,
@@ -993,7 +994,7 @@
     hidden_blocks = at.first_gate.shape[1] // COLS
     blocks = width // COLS
     g_at = [entry[2] * COLS for entry in entries]
-    second_down, second_wide, output_at, heads_at, first_down, first_wide = g_at[:6]
+    second_wide, second_down, output_at, heads_at, first_down, first_wide = g_at[:6]
     mixer_out_at, mixer_in_at, small_at = g_at[6:]
     starts = BACKWARD_STARTS
 
@@ -1009,25 +1010,26 @@
 
     def take(kind, index, total):
         row_at, columns = local_place(kind, index)
-        key_sums[row_at, kind, :, columns] = total
+        key_sums[row_at, kind, :, columns] = total.astype(jnp.bfloat16)
 
     local.part, local.take = part, take
 
     def tile_copies(name, j, slot):
         columns = pl.ds(pl.multiple_of(j * COLS, COLS), COLS)
         a, b, c = tiles_a.at[slot], tiles_b.at[slot], tiles_c.at[slot]
-        if name in ("second", "first"):
-            down, gate, up, gate_value, up_value = (
-                (at.second_down, at.second_gate, at.second_up, at.gate_two, at.up_two)
-                if name == "second"
-                else (at.first_down, at.first_gate, at.first_up, at.gate_one, at.up_one)
-            )
+        if name == "second":
             moves = [
-                (down.at[columns], a),
-                (gate.at[:, columns], b),
-                (up.at[:, columns], c),
-                (gate_value.at[:, columns], saved.at[slot, 0]),
-                (up_value.at[:, columns], saved.at[slot, 1]),
+                (at.second_gate.at[:, columns], b),
+                (at.second_up.at[:, columns], c),
+                (at.second_down.at[columns], a),
+            ]
+        elif name == "first":
+            moves = [
+                (at.first_down.at[columns], a),
+                (at.first_gate.at[:, columns], b),
+                (at.first_up.at[:, columns], c),
+                (at.gate_one.at[:, columns], saved.at[slot, 0]),
+                (at.up_one.at[:, columns], saved.at[slot, 1]),
             ]
         elif name == "attend_output":
             moves = [(at.attend_output.at[columns], a)]
@@ -1069,7 +1071,7 @@
     numbers = dict(steps)
 
     def tile_step(name, j):
-        slot = lax.rem(first_step[name] + j, 2)
+        slot = (first_step[name] + j) % 2 if isinstance(j, int) else lax.rem(first_step[name] + j, 2)
         for copy in tile_copies(name, j, slot):
             copy.wait()
 
@@ -1093,17 +1095,19 @@
 
     count = len(entries)
     x_loads = [
-        load(number, at.xs[number], x_all.at[:, :, pl.ds(x_first, x_count)])
+        load(number, at.xs[number - 2], x_all.at[:, :, pl.ds(x_first, x_count)])
         for number, (x_first, x_count, _, _, _) in enumerate(entries)
+        if number >= 2
     ]
     cotangent_load = load(count, at.cotangent, g_all.at[:, pl.ds(second_down, width)])
     middle_loads = [
         load(count + 1, at.queries_low, queries),
         load(count + 2, at.keys_values, keys_values),
         load(count + 3, at.mask, mask),
-        load(count + 4, at.queries_raw, queries_raw),
         load(count + 5, at.keys_raw, keys_raw),
     ]
+    raw_load = load(count + 4, at.queries_raw, queries_raw)
+    staged = queries_raw
     late_loads = [
         load(count + 6, at.mixer_saved, keys_values.at[0]),
         load(count + 7, at.projected, keys_values.at[1, pl.ds(0, 3 * tokens)]),
@@ -1112,19 +1116,31 @@
         load(count + 8, source, hidden)
         for source in (at.hidden_three, at.hidden_two, at.hidden_one, at.hidden_zero)
     ]
-    out_copy = load(count + 9, attended_grad, token_out)
-
-    x_loads[0].start()
+    out_copy = load(count + 9, staged, token_out)
+    mixed_copy = load(count + 9, staged, mixed_out)
+
+    hidden_loads[0].start()
     cotangent_load.start()
     for copy in tile_copies("second", 0, 0):
         copy.start()
-    for copy in x_loads[1:] + middle_loads + hidden_loads[:1]:
+    for copy in middle_loads + x_loads:
         copy.start()
     normed_grad[...] = jnp.zeros_like(normed_grad)
     small[...] = jnp.zeros_like(small)
     g_all[:, pl.ds(small_at, COLS)] = jnp.zeros((tokens, COLS), jnp.bfloat16)
-    exchange.meet()
-    x_loads[0].wait()
+    wide[...] = jnp.zeros_like(wide)
+    hidden_loads[0].wait()
+    normed = attended_grad
+    x_two = entries[0][0]
+    for first in range(0, tokens, 128):
+        span = pl.ds(first, 128)
+        value = hidden[span]
+        inverse = lax.rsqrt(jnp.mean(value * value, axis=-1, keepdims=True) + EPS)
+        value = value * inverse * at.gains[0:1, :]
+        normed[span] = value.astype(jnp.bfloat16)
+        turned = value.T.astype(jnp.bfloat16)
+        shape = x_all.shape[:2] + (2,) + x_all.shape[3:4] + (128,)
+        x_all[:, :, x_two : x_two + 2, :, pl.ds(first, 128)] = turned.reshape(shape)
     cotangent_load.wait()
     gradient[...] = g_all[:, pl.ds(second_down, width)].astype(jnp.float32)
 
@@ -1132,7 +1148,8 @@
         g_all[:, pl.ds(place, width)] = gradient[...].astype(jnp.bfloat16)
 
     def norm_back(number):
-        hidden_loads[number].wait()
+        if number > 0:
+            hidden_loads[number].wait()
         gain = at.gains[number : number + 1, :]
         sums = jnp.zeros((1, width), jnp.float32)
         piece = 64
@@ -1156,9 +1173,26 @@
         slot = tile_step(name, j)
         low = g_all[:, pl.ds(gradient_at, width)]
         active_grad = dot_nt(low, tiles_a[slot])
-        gate_value = saved[slot, 0].astype(jnp.float32)
-        up_value = saved[slot, 1].astype(jnp.float32)
+        if name == "second":
+            gate_value = jnp.dot(normed[...], tiles_b[slot], preferred_element_type=jnp.float32)
+            up_value = jnp.dot(normed[...], tiles_c[slot], preferred_element_type=jnp.float32)
+        else:
+            gate_value = saved[slot, 0].astype(jnp.float32)
+            up_value = saved[slot, 1].astype(jnp.float32)
         share = 1.0 / (1.0 + jnp.exp(-gate_value))
+        if name == "second":
+            active = gate_value * share * up_value
+            wide[...] += jnp.dot(
+                active.astype(jnp.bfloat16), tiles_a[slot], preferred_element_type=jnp.float32
+            )
+            turned = active.T.astype(jnp.bfloat16)
+            x_down, x_count = entries[1][:2]
+            block_rows = x_all.shape[3]
+            for block in range(COLS // block_rows):
+                place = j * (COLS // block_rows) + block
+                shard = place // x_count
+                part = turned[block * block_rows : (block + 1) * block_rows]
+                x_all[shard // 2, lax.rem(shard, 2), x_down + lax.rem(place, x_count)] = part
         up_grad = (active_grad * gate_value * share).astype(jnp.bfloat16)
         gate_grad = active_grad * up_value * share * (1.0 + gate_value * (1.0 - share))
         gate_grad = gate_grad.astype(jnp.bfloat16)
@@ -1180,7 +1214,8 @@
         query = two_heads(queries[span, columns], True)
         upper = two_heads(attended_grad[span, columns], False)
         both = keys_values[row_at, :, columns]
-        weights = jnp.exp(dot_nt(both, query)) * mask[row_at].astype(jnp.float32)
+        allowed = mask[row_at].astype(jnp.float32)
+        weights = jnp.exp(dot_nt(both, query)) * jnp.concatenate([allowed, allowed], axis=1)
         weights = weights * (1.0 / jnp.sum(weights, axis=0, keepdims=True))
         weight_grad_value = dot_nt(both, upper)
         delta = jnp.sum(weights * weight_grad_value, axis=0, keepdims=True)
@@ -1237,7 +1272,9 @@
         first = lanes_below((tokens, lane), HEAD_DIM, lane)
         for pair in range(width // lane // 2):
             even, odd = [
-                key_sums[:, :, :, pl.ds((2 * pair + which) * lane, lane)].reshape(tokens, lane)
+                key_sums[:, :, :, pl.ds((2 * pair + which) * lane, lane)]
+                .astype(jnp.float32)
+                .reshape(tokens, lane)
                 for which in range(2)
             ]
             key_value = jnp.where(first, even, pltpu.roll(odd, HEAD_DIM, 1))
@@ -1333,15 +1370,22 @@
             def _():
                 run(j)
 
-        when("second", lambda j: feed_tile("second", j, second_down, second_wide), 0, hidden_blocks)
+        when(
+            "second",
+            lambda j: feed_tile("second", j + 1, second_down, second_wide),
+            0,
+            hidden_blocks - 1,
+        )
 
         def waits(j):
-            for copy in x_loads[1:] + middle_loads:
+            for copy in middle_loads + x_loads:
                 copy.wait()
 
-        when("second", waits, hidden_blocks - 1)
+        when("attend_output", waits)
 
         def to_attended(j):
+            staged[...] = (hidden[...] + wide[...]).astype(jnp.bfloat16)
+            mixed_copy.start()
             norm_back(0)
             low_gradient(output_at)
             output_tile("attend_output", 0, output_at, attended_grad)
@@ -1349,14 +1393,19 @@
         when("attend_output", to_attended)
         when("attend_output", lambda j: output_tile("attend_output", 1, output_at, attended_grad), 1)
 
+        def staged_free(j):
+            mixed_copy.wait()
+            raw_load.start()
+
+        when("attention", staged_free)
+
         def attention(j):
-            pairs = KV_HEADS // 2
-            for which in range(2):
-                attention_head(j // pairs, 2 * lax.rem(j, pairs) + which)
-
-        when("attention", attention, 0, rows * KV_HEADS // 2)
+            attention_head(j // KV_HEADS, lax.rem(j, KV_HEADS))
+
+        when("attention", attention, 0, rows * KV_HEADS)
 
         def to_queries(j):
+            raw_load.wait()
             for copy in late_loads:
                 copy.start()
             query_heads()
@@ -1397,22 +1446,24 @@
 
         def close(j):
             norm_back(3)
-            attended_grad[...] = gradient[...].astype(jnp.bfloat16)
+            staged[...] = gradient[...].astype(jnp.bfloat16)
             out_copy.start()
             g_all[pl.ds(0, small.shape[0]), pl.ds(small_at, COLS)] = small[...].astype(jnp.bfloat16)
 
         when("close", close)
         when("close", lambda j: out_copy.wait(), 1)
 
+    exchange.meet()
+    feed_tile("second", 0, second_down, second_wide)
     exchange.run(task)
 
 
 def backward(groups, arrays, resident, row_count, shards, collective_id):
-    xs = [x for x, _ in groups]
+    xs = [x for x, _ in groups if not isinstance(x, int)]
     block_rows, tokens = xs[0].shape[3:]
     width = arrays["cotangent"].shape[1]
     entries, x_blocks, g_blocks, chunks = reduce_entries(
-        [(x.shape[2], columns // COLS) for x, columns in groups]
+        [(x if isinstance(x, int) else x.shape[2], columns // COLS) for x, columns in groups]
     )
     names = ["xs_%d" % number for number in range(len(xs))] + list(arrays)
     values = list(xs) + list(arrays.values())
@@ -1440,9 +1491,9 @@
             jax.ShapeDtypeStruct((x_count * block_rows, g_count * COLS), low)
             for _, x_count, _, g_count, _ in entries
         ]
-        + [jax.ShapeDtypeStruct((tokens, width), low)],
+        + [jax.ShapeDtypeStruct((tokens, width), low)] * 2,
         in_specs=[vmem_space if name in resident else any_space for name in names],
-        out_specs=[any_space] * (len(entries) + 1),
+        out_specs=[any_space] * (len(entries) + 2),
         scratch_shapes=[
             pltpu.VMEM((2, COLS, width), low),
             pltpu.VMEM((2, width, COLS), low),
@@ -1450,11 +1501,11 @@
             pltpu.VMEM((2, 2, tokens, COLS), low),
             pltpu.VMEM((rows, total_length, width), low),
             pltpu.VMEM((rows, shards // 2, 2, key_blocks, block_rows, width), low),
-            pltpu.VMEM((rows, key_blocks, block_rows, width), full),
+            pltpu.VMEM((rows, key_blocks, block_rows, width), low),
             pltpu.VMEM((tokens, width), low),
             pltpu.VMEM((tokens, width), low),
             pltpu.VMEM((tokens, width), full),
-            pltpu.VMEM((rows, total_length, 2 * tokens // rows), low),
+            pltpu.VMEM((rows, total_length, tokens // rows), low),
             pltpu.VMEM((tokens, width), low),
             pltpu.VMEM((tokens, width // 2), low),
             pltpu.VMEM((tokens, width), full),
@@ -1610,10 +1661,8 @@
     allowed_turned = (segment[:, None, :] == key_segment[:, :, None]) & (
         positions[None, None, :] >= key_positions[None, :, None]
     )
-    mask_turned = jnp.concatenate([allowed_turned, allowed_turned], axis=-1).astype(low)
     attended = attention(queries_low, keys_values, allowed.astype(low))
     hidden_three = hidden_two + dense(attended.reshape(tokens.shape), attend_output)
-    mixed, second_saved = feed(hidden_three, second_gain, second_gate, second_up, second_down)
 
     half = HEAD_DIM // 2
     inverse = THETA ** (-2.0 * jnp.arange(half, dtype=full) / HEAD_DIM)
@@ -1639,8 +1688,6 @@
     lane = 2 * HEAD_DIM
     arrays = dict(
         cotangent=flat(cotangent),
-        gate_two=second_saved[2],
-        up_two=second_saved[3],
         gate_one=first_saved[2],
         up_one=first_saved[3],
         hidden_three=flat(hidden_three),
@@ -1649,7 +1696,7 @@
         hidden_zero=flat(hidden_zero),
         queries_low=queries_low,
         keys_values=keys_values,
-        mask=mask_turned,
+        mask=allowed_turned.astype(low),
         queries_raw=flat(queries_raw).astype(low),
         keys_raw=flat(keys_raw).astype(low),
         mixer_saved=mixer_saved,
@@ -1679,8 +1726,8 @@
     hidden_columns = first_gate.shape[1]
     head_columns = width + 2 * key_weight.shape[1]
     groups = [
-        (turned(second_saved[1]), width),
-        (turned(second_saved[0]), 2 * hidden_columns),
+        (width // shards // block_rows, 2 * hidden_columns),
+        (hidden_columns // shards // block_rows, width),
         (turned(attended), width),
         (turned(attend_in), head_columns),
         (turned(first_saved[1]), width),
@@ -1690,8 +1737,8 @@
         (picks, COLS),
     ]
     (
+        second_both,
         grad_second_down,
-        second_both,
         grad_attend_output,
         attend_three,
         grad_first_down,
@@ -1700,6 +1747,7 @@
         grad_mixer_input,
         sums,
         token_grad,
+        mixed,
     ) = backward(groups, arrays, resident, row_count, shards, 1)
 
     def single(value):
@@ -1716,7 +1764,7 @@
     ]
     key_columns = key_weight.shape[1]
     return (
-        mixed.astype(low),
+        mixed.reshape(tokens.shape),
         token_grad.reshape(tokens.shape),
         vectors[3],
         single(grad_mixer_input),

time: 534 us -> 505 us (0.946)
  matrix products: 46.2 us -> 30.3 us
  Pallas kernels: 385 us -> 372 us
  local copies, waits for them, and re-layouts: 39 us -> 31.7 us
    dot_general x12 -> x9, matrix products: 46.2 us -> 30.3 us  [dense(): jnp.einsum('rtd,df->rtf', inputs, matrix, preferred_element_type=jnp.floa...]
    pallas_call x1, Pallas kernels: 27.8 us -> 12.5 us  [attention(): pl.pallas_call(attention_kernel, grid=(rows, width // lane), in_specs=[pl...]
    reshape x7 -> x5, local copies, waits for them, and re-layouts: 13.7 us -> 8.49 us  [flat(): return value.reshape(token_count, -1)]
  transfers between devices with their start and end apart: 2 -> 2, of which waited for: 1 -> 1; matrix products, arithmetic and copies ran while one was open for 7% -> 6% of each run, Pallas kernels for 0% -> 0%
where the time goes in v3:
time: 505 us; the launch traced here: 504 us
  Pallas kernels  372 us (74%)
  other arithmetic  43.1 us (9%)
  local copies, waits for them, and re-layouts  31.7 us (6%)
  matrix products  30.3 us (6%)
  between operations  14.8 us (3%)
  waiting for transfers between devices  10.4 us (2%)
    pallas_call x1, Pallas kernels, backward(): pl.pallas_call(kernel, out_shape=[jax.ShapeDtypeStruct((x_count * block_r...  359 us
    dot_general x9, matrix products, dense(): jnp.einsum('rtd,df->rtf', inputs, matrix, preferred_element_type=jnp.floa...  30.3 us
    convert_element_type x10, other arithmetic, single(): return value.astype(full)  17.9 us
    pallas_call x1, Pallas kernels, attention(): pl.pallas_call(attention_kernel, grid=(rows, width // lane), in_specs=[pl...  12.5 us
    all_gather x1, waiting for transfers between devices, fused_body(): keys_values = lax.all_gather(both, 'seq', axis=1, tiled=True)  10.4 us
  transfers between devices with their start and end apart: 2, of which 1 were waited for; matrix products, arithmetic and copies ran while one was open for 6% of the time, Pallas kernels for 0%

profile of v3, /device:TPU:0, one launch (start us, length us, event | category | flops | bytes accessed | tf_op | source)
XLA Modules:
  0.0 504.5 jit_solution(7403743881318004855)
XLA Ops:
  9.2 1.2 multiply_convert_fusion.5
  10.4 4.6 fusion.6
  15.0 1.6 copy-done.2
  16.8 2.4 collective-permute-start
  21.6 1.6 fusion.51
  23.2 1.5 multiply_convert_fusion.3
  26.3 6.1 %fusion.4 = f32[2,128,4608]{2,1,0:T(8,128)S(1)} fusion(bf16[2,128,1024]{2,1,0:T(8,128)(2,1)S(1)} %multiply_convert_fusion.2, bf16[1024,4608]{1,0:T(8,128)(2,1)} %refs_35_.1), kind=kOutput, calls=%fused_computation.4 | convolution fusion | flops 2415919104 | bytes 14680064 | tf_op jit(solution)/shard_map/rtd,df->rtf/dot_general | solution.py:65
  32.4 4.5 fusion.54
  37.0 6.2 %multiply_reduce_fusion.1 = (f32[2,128]{1,0:T(2,128)S(1)}, f32[2,128,1024]{2,1,0:T(8,128)S(1)}) fusion(f32[2,128,1024]{2,1,0:T(8,128)S(1)} %get-tuple-element.86, bf16[2,128,4608]{2,1,0:T(8,128)(2,1)S(1)} %get-tuple-element.52, bf16[4608,1024]{1,0:T(8,128)(2,1)} %refs_34_.1), kind=kOutput, calls=%fused_computation.34 | convolution fusion | flops 2416705280 | bytes 13894656 | tf_op jit(solution)/shard_map/rtd,df->rtf/dot_general | solution.py:65
  44.3 1.3 fusion.58
  45.6 2.0 copy.85
  48.8 1.7 convolution_convert_fusion
  54.6 2.0 copy.89
  62.1 2.1 fusion.55
  64.3 1.3 pad_maximum_fusion.1.refs_20_
  70.3 1.9 fusion.57
  72.2 1.5 copy.83
  76.0 4.5 copy.93
  83.5 2.7 pad_maximum_fusion.refs_19_
  86.2 10.4 %all-gather.2.cloned.1.call-done.both_ref.refs_15_ = bf16[2,1024,1024]{2,1,0:T(8,128)(2,1)} async-done(((bf16[2,128,1024]{2,1,0:T(8,128)(2,1)}), bf16[2,1024,1024]{2,1,0:T(8,128)(2,1)}) %all-gather.2.cloned.1.call-update) | async-done | bytes 4194320 | tf_op jit(solution)/shard_map/all_gather | solution.py:1654
  96.6 2.2 copy-done.1
  98.8 12.5 %shard_map.373 = bf16[256,1024]{1,0:T(8,128)(2,1)S(1)} custom-call(bf16[256,1024]{1,0:T(8,128)(2,1)S(1)} %reshape.491.query_ref.refs_14_, bf16[2,1024,1024]{2,1,0:T(8,128)(2,1)S(1)} %copy-done.1, bf16[2,128,1024]{2,1,0:T(8,128)(2,1)S(1)} %and_convert_fusion.1.mask_ref), custom_call_target="tpu_custom_call" | custom-call | flops 2147483648 | bytes 8388608 | tf_op jit(solution)/shard_map/pallas_call | solution.py:1551
  112.3 3.3 fusion.17
  116.4 359.3 %shard_map.374 = (bf16[128,9216]{1,0:T(8,128)(2,1)}, bf16[576,1024]{1,0:T(8,128)(2,1)}, bf16[128,1024]{1,0:T(8,128)(2,1)}, bf16[128,2048]{1,0:T(8,128)(2,1)}, bf...) custom-call(bf16[4,2,2,64,256]{4,3,2,1,0:T(8,128)(2,1)} %bitcast.162, ...), custom_call_target="tpu_custom_call" | custom-call | flops 37044092928 | bytes 72351744 | tf_op jit(solution)/shard_map/pallas_call | solution.py:1488
  475.7 1.8 slice_convert_fusion.9
  477.5 1.8 slice_convert_fusion.8
  481.1 4.5 slice_convert_fusion.2
  485.6 2.7 slice_convert_fusion
  488.4 1.7 convert_element_type.291
  490.1 1.7 convert_element_type.298
  491.8 1.3 convert_element_type.287
  494.8 1.3 bitcast_convert_fusion
  (178 shorter events, 34.5 us)
Async XLA Ops:
  7.2 89.4 %all-gather.2.cloned.1.call-start = ((), (), s32[]{:S(2)}) async-start(), calls=%async_computation | async-start | bytes 4718592 | tf_op jit(solution)/shard_map/all_gather | solution.py:1654
  16.6 4.2 copy-start.33
  16.6 4.2 copy-start.31
  16.6 4.3 copy-start.43
  16.8 4.6 collective-permute-start
  19.4 3.8 copy-start.29
  23.2 9.2 %slice-start = ((s8[9437184]{0:T(1024)(128)(4,1)}), s8[4194304]{0:T(1024)(128)(4,1)S(1)}, s32[]{:S(2)}) async-start(s8[9437184]{0:T(1024)(128)(4,1)} %bitcast.172), calls=%async_computation.1 | async-start | bytes 8388608
  26.1 10.9 %copy-start.6 = (f32[2,128,1024]{2,1,0:T(8,128)}, f32[2,128,1024]{2,1,0:T(8,128)S(1)}, u32[]{:S(2)}) copy-start(f32[2,128,1024]{2,1,0:T(8,128)S(1)} %get-tuple-element.86) | copy-start | bytes 3145732
  26.1 6.3 %slice-start.1 = ((s8[9437184]{0:T(1024)(128)(4,1)}), s8[4194304]{0:T(1024)(128)(4,1)S(1)}, s32[]{:S(2)}) async-start(s8[9437184]{0:T(1024)(128)(4,1)} %bitcast.172), calls=%async_computation.2 | async-start | bytes 8388608
  26.3 6.1 %copy-start.4 = (bf16[2,128,1024]{2,1,0:T(8,128)(2,1)}, bf16[2,128,1024]{2,1,0:T(8,128)(2,1)S(1)}, u32[]{:S(2)}) copy-start(bf16[2,128,1024]{2,1,0:T(8,128)(2,1)S(1)} %multiply_convert_fusion.2) | copy-start | bytes 1572868
  26.3 6.1 %slice-start.2 = ((s8[9437184]{0:T(1024)(128)(4,1)}), s8[1048576]{0:T(1024)(128)(4,1)S(1)}, s32[]{:S(2)}) async-start(s8[9437184]{0:T(1024)(128)(4,1)} %bitcast.172), calls=%async_computation.3 | async-start | bytes 2097152
  37.0 6.2 %copy-start.10 = (bf16[2,128,4608]{2,1,0:T(8,128)(2,1)}, bf16[2,128,4608]{2,1,0:T(8,128)(2,1)S(1)}, u32[]{:S(2)}) copy-start(bf16[2,128,4608]{2,1,0:T(8,128)(2,1)S(1)} %get-tuple-element.52) | copy-start | bytes 7077892
  37.0 7.3 %copy-start.17 = (bf16[1024,512]{1,0:T(8,128)(2,1)S(1)}, bf16[1024,512]{1,0:T(8,128)(2,1)}, u32[]{:S(2)}) copy-start(bf16[1024,512]{1,0:T(8,128)(2,1)} %refs_32_.1) | copy-start | bytes 3145732
  52.5 4.2 copy-start.32
  52.5 4.2 copy-start.34
  52.5 4.2 copy-start.35
  52.5 4.2 copy-start.42
  52.5 4.2 copy-start.41
  52.5 4.2 copy-start.40
  52.6 5.2 %copy-start.38 = (bf16[1024]{0:T(1024)(128)(2,1)S(1)}, bf16[1024]{0:T(1024)(128)(2,1)}, u32[]{:S(2)}) copy-start(bf16[1024]{0:T(1024)(128)(2,1)} %param.39) | copy-start | bytes 6148
  52.6 5.8 %copy-start.44 = (bf16[64]{0:T(256)(128)(2,1)S(1)}, bf16[64]{0:T(256)(128)(2,1)}, u32[]{:S(2)}) copy-start(bf16[64]{0:T(256)(128)(2,1)} %param.37) | copy-start | bytes 388
  52.6 7.2 %copy-start.30 = (s32[2,2]{1,0:T(2,128)S(1)}, s32[2,2]{1,0:T(2,128)}, u32[]{:S(2)}) copy-start(s32[2,2]{1,0:T(2,128)} %copy-done.29) | copy-start | bytes 52
  52.7 7.2 %copy-start.25 = (s32[2,128]{1,0:T(2,128)S(1)}, s32[2,128]{1,0:T(2,128)}, u32[]{:S(2)}) copy-start(s32[2,128]{1,0:T(2,128)} %copy-done.24) | copy-start | bytes 3076
  52.7 7.2 %copy-start.27 = (s32[128]{0:T(128)S(1)}, s32[128]{0:T(128)}, u32[]{:S(2)}) copy-start(s32[128]{0:T(128)} %copy-done.26) | copy-start | bytes 1540
  52.7 7.3 %copy-start.37 = (f32[32]{0:T(128)S(1)}, f32[32]{0:T(128)}, u32[]{:S(2)}) copy-start(f32[32]{0:T(128)} %copy-done.36) | copy-start | bytes 388
  65.5 4.8 copy-start.12
  76.0 20.6 %copy-start = (bf16[256,1024]{1,0:T(8,128)(2,1)}, bf16[256,1024]{1,0:T(8,128)(2,1)S(1)}, u32[]{:S(2)}) copy-start(bf16[256,1024]{1,0:T(8,128)(2,1)S(1)} %reshape.491.query_ref.refs_14_) | copy-start | bytes 1572868
  76.0 5.5 %copy-start.5 = (bf16[2,128,1024]{2,1,0:T(8,128)(2,1)S(1)}, bf16[2,128,1024]{2,1,0:T(8,128)(2,1)}, u32[]{:S(2)}) copy-start(bf16[2,128,1024]{2,1,0:T(8,128)(2,1)} %copy-done.4) | copy-start | bytes 1572868
  98.8 13.5 %copy-start.8 = (f32[2,128,1024]{2,1,0:T(8,128)S(1)}, f32[2,128,1024]{2,1,0:T(8,128)}, u32[]{:S(2)}) copy-start(f32[2,128,1024]{2,1,0:T(8,128)} %copy-done.7) | copy-start | bytes 3145732
  481.1 4.5 copy-start.9
  491.8 4.3 copy-start.20
  491.8 5.1 %copy-start.19 = (bf16[256,1024]{1,0:T(8,128)(2,1)S(1)}, bf16[256,1024]{1,0:T(8,128)(2,1)}, u32[]{:S(2)}) copy-start(bf16[256,1024]{1,0:T(8,128)(2,1)} %get-tuple-element.33) | copy-start | bytes 1572868
  (18 other events, 35.7 us)
Sparse Core Ops, SparseCore 0:
  56.7 39.7 all-gather.1

commit v4 on v3

--- a/solution.py
+++ b/solution.py
@@ -939,6 +939,487 @@
     return jnp.concatenate(parts, axis=0).astype(jnp.bfloat16)
 
 
+def head_tools(lane):
+    head_of = lax.broadcasted_iota(jnp.int32, (lane, lane), 0) // HEAD_DIM
+    ones = head_of == lax.broadcasted_iota(jnp.int32, (lane, lane), 1) // HEAD_DIM
+    ones = ones.astype(jnp.float32).astype(jnp.bfloat16)
+
+    def head_mean(value):
+        total = jnp.dot(value.astype(jnp.bfloat16), ones, preferred_element_type=jnp.float32)
+        return total * (1.0 / HEAD_DIM)
+
+    def turn(value):
+        half = HEAD_DIM // 2
+        first = lanes_below(value.shape, half, HEAD_DIM)
+        return jnp.where(first, pltpu.roll(value, lane - half, 1), pltpu.roll(value, half, 1))
+
+    return head_mean, turn
+
+
+def forward_kernel(names, out_names, scratch_names, shards, *refs):
+    at = types.SimpleNamespace(**dict(zip(names + out_names + scratch_names, refs)))
+    row, seq = lax.axis_index("row"), lax.axis_index("seq")
+    tokens, width = at.low_one.shape
+    rows, total_length = at.both.shape[:2]
+    length = tokens // rows
+    lane = 2 * HEAD_DIM
+    blocks = width // COLS
+    hidden_blocks = at.first_gate.shape[1] // COLS
+    bits = [lax.rem(seq // (1 << bit), 2) for bit in range(3)]
+    partner = [seq + (1 << bit) * (1 - 2 * bits[bit]) for bit in range(3)]
+    head_mean, turn = head_tools(lane)
+
+    def tile_copies(step, slot):
+        name, j = step
+        b, c = at.tiles_b.at[slot], at.tiles_c.at[slot]
+
+        def columns(block):
+            return pl.ds(block * COLS if isinstance(block, int) else pl.multiple_of(block * COLS, COLS), COLS)
+
+        if name == "mixer_input":
+            first, second = ((0, 4), (1, 5), (2, 3))[j]
+            moves = [
+                (at.mixer_input.at[:, columns(first)], b),
+                (at.mixer_input.at[:, columns(second)], c),
+            ]
+        elif name == "keys":
+            moves = [(at.key_weight, b), (at.value_weight, c)]
+        elif name == "first":
+            moves = [
+                (at.first_gate.at[:, columns(j)], b),
+                (at.first_up.at[:, columns(j)], c),
+                (at.first_down.at[columns(j)], at.tiles_a.at[slot]),
+            ]
+        else:
+            matrix = {
+                "mixer_output": at.mixer_output,
+                "queries": at.query_weight,
+                "attend_output": at.attend_output,
+            }[name]
+            moves = [(matrix.at[:, columns(0)], b), (matrix.at[:, columns(1)], c)]
+        return [
+            pltpu.make_async_copy(source, target, at.tile_sem.at[slot, place])
+            for place, (source, target) in enumerate(moves)
+        ]
+
+    steps = [("mixer_input", 0), ("mixer_input", 1), ("mixer_input", 2), ("mixer_output", 0)]
+    first_at = len(steps)
+    steps += [("first", j) for j in range(hidden_blocks)]
+    steps += [("keys", 0), ("queries", 0), ("attend_output", 0)]
+
+    def begin(number):
+        for copy in tile_copies(steps[number], number % 2):
+            copy.wait()
+        if number + 1 < len(steps):
+            for copy in tile_copies(steps[number + 1], (number + 1) % 2):
+                copy.start()
+        return number % 2
+
+    saves = []
+
+    def save(source, target):
+        copy = pltpu.make_async_copy(source, target, at.save_sem.at[len(saves)])
+        copy.start()
+        saves.append(copy)
+
+    def normed(hidden, number, target):
+        for first in range(0, tokens, 64):
+            span = pl.ds(first, 64)
+            value = hidden[span]
+            inverse = lax.rsqrt(jnp.mean(value * value, axis=-1, keepdims=True) + EPS)
+            value = value * inverse * at.vectors[number : number + 1, :]
+            target[span] = value.astype(jnp.bfloat16)
+
+    def times(left, tile):
+        return jnp.dot(left[...], tile, preferred_element_type=jnp.float32)
+
+    for copy in tile_copies(steps[0], 0):
+        copy.start()
+    token_load = pltpu.make_async_copy(at.tokens, at.attended, at.load_sem.at[0])
+    token_load.start()
+    at.halo_in[...] = jnp.zeros_like(at.halo_in)
+    barrier = pltpu.get_barrier_semaphore()
+    others = partner + [lax.rem(seq + step, shards) for step in (1, shards - 1)]
+    for other in others:
+        pl.semaphore_signal(barrier, inc=1, device_id=(row, other), device_id_type=MESH)
+    token_load.wait()
+    at.hidden_a[...] = at.attended[...].astype(jnp.float32)
+    save(at.hidden_a, at.hidden_zero)
+    normed(at.hidden_a, 3, at.low_one)
+    pl.semaphore_wait(barrier, len(others))
+
+    for number, (first, second) in enumerate(((0, 4), (1, 5))):
+        slot = begin(number)
+        entry = times(at.low_one, at.tiles_b[slot])
+        carrier = times(at.low_one, at.tiles_c[slot])
+        columns = pl.ds(number * COLS, COLS)
+        product = (entry * carrier).astype(jnp.bfloat16)
+        at.mixed_low[pl.ds(3 * tokens, tokens), columns] = product
+        product = product.astype(jnp.float32)
+        at.gates_low[pl.ds(0, tokens), columns] = entry.astype(jnp.bfloat16)
+        at.gates_low[pl.ds(2 * tokens, tokens), columns] = carrier.astype(jnp.bfloat16)
+        for which in range(rows):
+            last = product[(which + 1) * length - 8 : (which + 1) * length]
+            at.halo_out[which, :, columns] = last
+    halo = pltpu.make_async_remote_copy(
+        src_ref=at.halo_out,
+        dst_ref=at.halo_in,
+        send_sem=at.halo_sem.at[0],
+        recv_sem=at.halo_sem.at[1],
+        device_id=(row, jnp.minimum(seq + 1, shards - 1)),
+        device_id_type=MESH,
+    )
+
+    @pl.when(seq < shards - 1)
+    def _():
+        halo.start()
+
+    slot = begin(2)
+    for block, tile in enumerate((at.tiles_b, at.tiles_c)):
+        at.work[:, pl.ds(block * COLS, COLS)] = times(at.low_one, tile[slot])
+
+    @pl.when(seq > 0)
+    def _():
+        halo.wait_recv()
+
+    @pl.when(seq < shards - 1)
+    def _():
+        halo.wait_send()
+
+    position = lax.rem(lax.broadcasted_iota(jnp.int32, (tokens, lane), 0), length) + seq * length
+    keep_one = position - 1 >= at.seg_start[...]
+    keep_two = position - 2 >= at.seg_start[...]
+    edge = lax.broadcasted_iota(jnp.int32, (8, lane), 0)
+    for part_at in range(0, width, lane):
+        columns = pl.ds(part_at, lane)
+        current = at.mixed_low[pl.ds(3 * tokens, tokens), columns].astype(jnp.float32)
+        shifted = []
+        for steps_back, keep in ((1, keep_one), (2, keep_two)):
+            back = pltpu.roll(current, steps_back, 0)
+            pieces = []
+            for which in range(rows):
+                before = pltpu.roll(at.halo_in[which, :, columns], steps_back, 0)
+                start = which * length
+                pieces.append(jnp.where(edge < steps_back, before, back[start : start + 8]))
+                pieces.append(back[start + 8 : start + length])
+            back = jnp.concatenate(pieces, axis=0)
+            shifted.append(jnp.where(keep, back, 0.0))
+        one, two = shifted
+        convolved = at.vectors[6:7, columns] * current + at.vectors[5:6, columns] * one
+        convolved += at.vectors[4:5, columns] * two
+        exit_gate = at.work[:, columns]
+        at.mixed_low[pl.ds(0, tokens), columns] = convolved.astype(jnp.bfloat16)
+        at.mixed_low[pl.ds(tokens, tokens), columns] = two.astype(jnp.bfloat16)
+        at.mixed_low[pl.ds(2 * tokens, tokens), columns] = one.astype(jnp.bfloat16)
+        at.gates_low[pl.ds(tokens, tokens), columns] = exit_gate.astype(jnp.bfloat16)
+        at.low_two[:, columns] = (exit_gate * convolved).astype(jnp.bfloat16)
+    save(at.mixed_low, at.mixer_saved)
+    save(at.gates_low, at.projected)
+
+    def add_output(number, left, before, after):
+        slot = begin(number)
+        for block, tile in enumerate((at.tiles_b, at.tiles_c)):
+            columns = pl.ds(block * COLS, COLS)
+            after[:, columns] = before[:, columns] + times(left, tile[slot])
+
+    add_output(3, at.low_two, at.hidden_a, at.hidden_b)
+    save(at.hidden_b, at.hidden_one)
+    normed(at.hidden_b, 2, at.low_three)
+    at.hidden_c[...] = at.hidden_b[...]
+
+    def feed_tile(j, carried):
+        slot = lax.rem(first_at + j, 2)
+        for copy in tile_copies(("first", j), slot):
+            copy.wait()
+
+        @pl.when(j + 1 < hidden_blocks)
+        def _():
+            for copy in tile_copies(("first", j + 1), 1 - slot):
+                copy.start()
+
+        @pl.when(j + 1 == hidden_blocks)
+        def _():
+            for copy in tile_copies(("keys", 0), 1 - slot):
+                copy.start()
+
+        gate_value = times(at.low_three, at.tiles_b[slot])
+        up_value = times(at.low_three, at.tiles_c[slot])
+        columns = pl.ds(pl.multiple_of(j * COLS, COLS), COLS)
+        at.gate_low[:, columns] = gate_value.astype(jnp.bfloat16)
+        at.up_low[:, columns] = up_value.astype(jnp.bfloat16)
+        active = gate_value / (1.0 + jnp.exp(-gate_value)) * up_value
+        active = active.astype(jnp.bfloat16)
+        at.active_low[:, columns] = active
+        at.hidden_c[...] += jnp.dot(
+            active, at.tiles_a[slot], preferred_element_type=jnp.float32
+        )
+        return carried
+
+    lax.fori_loop(0, hidden_blocks, feed_tile, 0)
+    save(at.hidden_c, at.hidden_two)
+    save(at.gate_low, at.gate_one)
+    save(at.up_low, at.up_one)
+    normed(at.hidden_c, 1, at.low_four)
+
+    def head_path(raw, gain):
+        value = raw * lax.rsqrt(head_mean(raw * raw) + EPS) * gain
+        return value * at.cosine[...] + turn(value) * at.sine[...]
+
+    keys_at = first_at + hidden_blocks
+    slot = begin(keys_at)
+    at.work[:, pl.ds(0, width // 2)] = times(at.low_four, at.tiles_b[slot])
+    at.work[:, pl.ds(width // 2, width // 2)] = times(at.low_four, at.tiles_c[slot])
+    at.keys_low[...] = at.work[:, pl.ds(0, width // 2)].astype(jnp.bfloat16)
+    save(at.keys_low, at.keys_raw)
+    first = lanes_below((tokens, lane), HEAD_DIM, lane)
+    own = pl.ds(pl.multiple_of(seq * length, length), length)
+    for pair in range(width // lane // 2):
+        keys = head_path(at.work[:, pl.ds(pair * lane, lane)], at.vectors[8:9, pl.ds(0, lane)])
+        values = at.work[:, pl.ds(width // 2 + pair * lane, lane)]
+        even = jnp.where(first, keys, pltpu.roll(values, HEAD_DIM, 1)).astype(jnp.bfloat16)
+        odd = jnp.where(first, pltpu.roll(keys, HEAD_DIM, 1), values).astype(jnp.bfloat16)
+        for which, value in enumerate((even, odd)):
+            columns = pl.ds((2 * pair + which) * lane, lane)
+            at.both[:, own, columns] = value.reshape(rows, length, lane)
+
+    def piece(owner, which=None):
+        span = pl.ds(pl.multiple_of(owner * length, length), length)
+        return at.both.at[:, span] if which is None else at.both.at[which, span]
+
+    def send(number, part, bit):
+        return pltpu.make_async_remote_copy(
+            src_ref=part,
+            dst_ref=part,
+            send_sem=at.gather_send.at[number],
+            recv_sem=at.gather_recv.at[number],
+            device_id=(row, partner[bit]),
+            device_id_type=MESH,
+        )
+
+    def flip(owner, bit):
+        value = lax.rem(owner // (1 << bit), 2)
+        return owner + (1 << bit) * (1 - 2 * value)
+
+    across, along = partner[1], partner[2]
+    corner = flip(across, 2)
+    near_zero, far_one = send(0, piece(seq, 0), 1), send(1, piece(seq, 1), 2)
+    near_one, far_zero = send(2, piece(seq, 1), 1), send(3, piece(seq, 0), 2)
+    twin = send(4, piece(seq), 0)
+    for copy in (near_zero, far_one, near_one, far_zero, twin):
+        copy.start()
+
+    slot = begin(keys_at + 1)
+    for block, tile in enumerate((at.tiles_b, at.tiles_c)):
+        at.work[:, pl.ds(block * COLS, COLS)] = times(at.low_four, tile[slot])
+    at.queries_low[...] = at.work[...].astype(jnp.bfloat16)
+    save(at.queries_low, at.queries_raw)
+    for head in range(width // lane):
+        columns = pl.ds(head * lane, lane)
+        query = head_path(at.work[:, columns], at.vectors[7:8, pl.ds(0, lane)]).astype(jnp.bfloat16)
+        query = query * jnp.bfloat16(HEAD_DIM**-0.5)
+        at.scaled[:, columns] = query
+        for which in range(rows):
+            at.paired[which * (width // lane) + head] = two_heads(
+                query[which * length : (which + 1) * length], True
+            )
+    save(at.scaled, at.queries_out)
+
+    def transposed(low, target):
+        for first in range(0, tokens, lane):
+            span = pl.ds(first, lane)
+            value = low[span].astype(jnp.float32).T.astype(jnp.bfloat16)
+            target[:, :, :, :, span] = value.reshape(target.shape[:-1] + (lane,))
+
+    transposed(at.low_one, at.turned_one)
+    save(at.turned_one, at.mixer_in_x)
+    near_zero.wait()
+    far_one.wait()
+    near_forward = send(5, piece(across, 0), 2)
+    far_forward = send(6, piece(along, 1), 1)
+    near_forward.start()
+    far_forward.start()
+    transposed(at.low_two, at.turned_two)
+    save(at.turned_two, at.gated_x)
+
+    at.sums[...] = jnp.zeros_like(at.sums)
+    pairs_of = width // lane
+    chip = seq // 2
+
+    def attend(other):
+        @pl.when(other <= chip)
+        def _():
+            span = pl.ds(pl.multiple_of(other * 2 * length, 2 * length), 2 * length)
+            shape = (length, 2 * length)
+            key_at = lax.broadcasted_iota(jnp.int32, shape, 1) + other * 2 * length
+            query_at = lax.broadcasted_iota(jnp.int32, shape, 0) + seq * length
+            first = lanes_below((2 * length, lane), HEAD_DIM, lane)
+            for which in range(rows):
+                start = at.seg_start[pl.ds(which * length, length)]
+                start = jnp.concatenate([start, start], axis=1)
+                allowed = jnp.logical_and(key_at >= start, key_at <= query_at)
+                allowed = jnp.concatenate([allowed, allowed], axis=0)
+
+                def one(head, carried):
+                    columns = pl.ds(pl.multiple_of(head * lane, lane), lane)
+                    both = at.both[which, span, columns]
+                    place = which * pairs_of + head
+                    weights = jnp.exp(dot_nt(at.paired[place], both))
+                    weights = jnp.where(allowed, weights, 0.0).astype(jnp.bfloat16)
+                    right = jnp.where(first, 1.0, both.astype(jnp.float32)).astype(jnp.bfloat16)
+                    at.sums[place] += jnp.dot(
+                        weights, right, preferred_element_type=jnp.float32
+                    )
+                    return carried
+
+                lax.fori_loop(0, pairs_of, one, 0)
+
+    twin.wait()
+    attend(chip)
+    near_one.wait()
+    near_share = send(7, piece(across), 0)
+    near_share.start()
+    far_zero.wait()
+    far_share = send(8, piece(along), 0)
+    far_share.start()
+    transposed(at.low_three, at.turned_three)
+    save(at.turned_three, at.first_in_x)
+    near_share.wait()
+    attend(across // 2)
+    transposed(at.low_four, at.turned_four)
+    save(at.turned_four, at.attend_in_x)
+    far_share.wait()
+    attend(along // 2)
+
+    block_rows = at.turned_active.shape[3]
+    x_count = at.turned_active.shape[2]
+    for j in range(hidden_blocks):
+        for first in range(0, tokens, lane):
+            span = pl.ds(first, lane)
+            value = at.active_low[span, pl.ds(j * COLS, COLS)].astype(jnp.float32).T
+            value = value.astype(jnp.bfloat16)
+            for block in range(COLS // block_rows):
+                place = j * (COLS // block_rows) + block
+                shard = place // x_count
+                at.turned_active[shard // 2, shard % 2, place % x_count, :, span] = value[
+                    block * block_rows : (block + 1) * block_rows
+                ]
+    save(at.turned_active, at.active_x)
+    near_forward.wait()
+    far_forward.wait()
+    corner_share = send(9, piece(corner), 0)
+    corner_share.start()
+    corner_share.wait()
+    save(at.both, at.keys_values)
+    attend(corner // 2)
+
+    first = lanes_below((length, lane), HEAD_DIM, lane)
+    for which in range(rows):
+        span = pl.ds(which * length, length)
+        for head in range(pairs_of):
+            value = at.sums[which * pairs_of + head]
+            value = value * (1.0 / pltpu.roll(value, HEAD_DIM, 1))
+            value = jnp.where(first, pltpu.roll(value[:length], HEAD_DIM, 1), value[length:])
+            at.attended[span, pl.ds(head * lane, lane)] = value.astype(jnp.bfloat16)
+    add_output(keys_at + 2, at.attended, at.hidden_c, at.hidden_d)
+    save(at.hidden_d, at.hidden_three)
+    transposed(at.attended, at.turned_five)
+    save(at.turned_five, at.attended_x)
+    for copy in saves:
+        copy.wait()
+
+
+def forward(arrays, resident, rows, shards, collective_id):
+    tokens, width = arrays["tokens"].shape
+    hidden_columns = arrays["first_gate"].shape[1]
+    length = tokens // rows
+    total_length = length * shards
+    block_rows = math.gcd(width // shards, hidden_columns // shards)
+    low, full = jnp.bfloat16, jnp.float32
+
+    def x_shape(columns):
+        return (shards // 2, 2, columns // shards // block_rows, block_rows, tokens)
+
+    outs = dict(
+        hidden_zero=((tokens, width), full),
+        hidden_one=((tokens, width), full),
+        hidden_two=((tokens, width), full),
+        hidden_three=((tokens, width), full),
+        gate_one=((tokens, hidden_columns), low),
+        up_one=((tokens, hidden_columns), low),
+        queries_out=((tokens, width), low),
+        queries_raw=((tokens, width), low),
+        keys_raw=((tokens, width // 2), low),
+        keys_values=((rows, total_length, width), low),
+        mixer_saved=((4 * tokens, width), low),
+        projected=((3 * tokens, width), low),
+        mixer_in_x=(x_shape(width), low),
+        gated_x=(x_shape(width), low),
+        first_in_x=(x_shape(width), low),
+        attend_in_x=(x_shape(width), low),
+        attended_x=(x_shape(width), low),
+        active_x=(x_shape(hidden_columns), low),
+    )
+    pairs = rows * width // (2 * HEAD_DIM)
+    dma = pltpu.SemaphoreType.DMA
+    scratch = dict(
+        tiles_a=pltpu.VMEM((2, COLS, width), low),
+        tiles_b=pltpu.VMEM((2, width, COLS), low),
+        tiles_c=pltpu.VMEM((2, width, COLS), low),
+        hidden_a=pltpu.VMEM((tokens, width), full),
+        hidden_b=pltpu.VMEM((tokens, width), full),
+        hidden_c=pltpu.VMEM((tokens, width), full),
+        hidden_d=pltpu.VMEM((tokens, width), full),
+        low_one=pltpu.VMEM((tokens, width), low),
+        low_two=pltpu.VMEM((tokens, width), low),
+        low_three=pltpu.VMEM((tokens, width), low),
+        low_four=pltpu.VMEM((tokens, width), low),
+        attended=pltpu.VMEM((tokens, width), low),
+        work=pltpu.VMEM((tokens, width), full),
+        mixed_low=pltpu.VMEM((4 * tokens, width), low),
+        gates_low=pltpu.VMEM((3 * tokens, width), low),
+        gate_low=pltpu.VMEM((tokens, hidden_columns), low),
+        up_low=pltpu.VMEM((tokens, hidden_columns), low),
+        active_low=pltpu.VMEM((tokens, hidden_columns), low),
+        keys_low=pltpu.VMEM((tokens, width // 2), low),
+        queries_low=pltpu.VMEM((tokens, width), low),
+        scaled=pltpu.VMEM((tokens, width), low),
+        both=pltpu.VMEM((rows, total_length, width), low),
+        paired=pltpu.VMEM((pairs, 2 * length, 2 * HEAD_DIM), low),
+        sums=pltpu.VMEM((pairs, 2 * length, 2 * HEAD_DIM), full),
+        turned_one=pltpu.VMEM(x_shape(width), low),
+        turned_two=pltpu.VMEM(x_shape(width), low),
+        turned_three=pltpu.VMEM(x_shape(width), low),
+        turned_four=pltpu.VMEM(x_shape(width), low),
+        turned_five=pltpu.VMEM(x_shape(width), low),
+        turned_active=pltpu.VMEM(x_shape(hidden_columns), low),
+        halo_out=pltpu.VMEM((rows, 8, width), full),
+        halo_in=pltpu.VMEM((rows, 8, width), full),
+        tile_sem=dma((2, 3)),
+        load_sem=dma((1,)),
+        save_sem=dma((len(outs),)),
+        halo_sem=dma((2,)),
+        gather_send=dma((10,)),
+        gather_recv=dma((10,)),
+    )
+    any_space = pl.BlockSpec(memory_space=pl.ANY)
+    vmem_space = pl.BlockSpec(memory_space=pltpu.VMEM)
+    weights = sum(value.size for value in arrays.values())
+    results = pl.pallas_call(
+        functools.partial(forward_kernel, list(arrays), list(outs), list(scratch), shards),
+        out_shape=[jax.ShapeDtypeStruct(shape, kind) for shape, kind in outs.values()],
+        in_specs=[vmem_space if name in resident else any_space for name in arrays],
+        out_specs=[any_space] * len(outs),
+        scratch_shapes=list(scratch.values()),
+        compiler_params=pltpu.CompilerParams(
+            collective_id=collective_id, has_side_effects=True, vmem_limit_bytes=60 * 2**20
+        ),
+        cost_estimate=pl.CostEstimate(
+            flops=2 * weights * tokens, bytes_accessed=2 * weights, transcendentals=0
+        ),
+    )(*arrays.values())
+    return dict(zip(outs, results))
+
+
 BACKWARD_STARTS = {
     "second": 0,
     "attend_output": 8,
@@ -970,7 +1451,6 @@
         queries,
         attended_grad,
         wide,
-        mask,
         queries_raw,
         keys_raw,
         gradient,
@@ -1097,13 +1577,12 @@
     x_loads = [
         load(number, at.xs[number - 2], x_all.at[:, :, pl.ds(x_first, x_count)])
         for number, (x_first, x_count, _, _, _) in enumerate(entries)
-        if number >= 2
+        if 2 <= number < count - 1
     ]
     cotangent_load = load(count, at.cotangent, g_all.at[:, pl.ds(second_down, width)])
     middle_loads = [
-        load(count + 1, at.queries_low, queries),
+        load(count + 1, at.queries_out, queries),
         load(count + 2, at.keys_values, keys_values),
-        load(count + 3, at.mask, mask),
         load(count + 5, at.keys_raw, keys_raw),
     ]
     raw_load = load(count + 4, at.queries_raw, queries_raw)
@@ -1136,7 +1615,7 @@
         span = pl.ds(first, 128)
         value = hidden[span]
         inverse = lax.rsqrt(jnp.mean(value * value, axis=-1, keepdims=True) + EPS)
-        value = value * inverse * at.gains[0:1, :]
+        value = value * inverse * at.vectors[0:1, :]
         normed[span] = value.astype(jnp.bfloat16)
         turned = value.T.astype(jnp.bfloat16)
         shape = x_all.shape[:2] + (2,) + x_all.shape[3:4] + (128,)
@@ -1150,7 +1629,7 @@
     def norm_back(number):
         if number > 0:
             hidden_loads[number].wait()
-        gain = at.gains[number : number + 1, :]
+        gain = at.vectors[number : number + 1, :]
         sums = jnp.zeros((1, width), jnp.float32)
         piece = 64
         for first in range(0, tokens, piece):
@@ -1214,8 +1693,11 @@
         query = two_heads(queries[span, columns], True)
         upper = two_heads(attended_grad[span, columns], False)
         both = keys_values[row_at, :, columns]
-        allowed = mask[row_at].astype(jnp.float32)
-        weights = jnp.exp(dot_nt(both, query)) * jnp.concatenate([allowed, allowed], axis=1)
+        key_at = lax.broadcasted_iota(jnp.int32, (both.shape[0], length), 0)
+        query_at = lax.broadcasted_iota(jnp.int32, (both.shape[0], length), 1) + seq * length
+        allowed = jnp.logical_and(key_at >= at.starts[row_at, 0:1], key_at <= query_at)
+        weights = jnp.exp(dot_nt(both, query))
+        weights = jnp.where(jnp.concatenate([allowed, allowed], axis=1), weights, 0.0)
         weights = weights * (1.0 / jnp.sum(weights, axis=0, keepdims=True))
         weight_grad_value = dot_nt(both, upper)
         delta = jnp.sum(weights * weight_grad_value, axis=0, keepdims=True)
@@ -1233,19 +1715,10 @@
         )
 
     lane = 2 * HEAD_DIM
-    head_of = lax.broadcasted_iota(jnp.int32, (lane, lane), 0) // HEAD_DIM
-    ones = head_of == lax.broadcasted_iota(jnp.int32, (lane, lane), 1) // HEAD_DIM
-    ones = ones.astype(jnp.float32).astype(jnp.bfloat16)
-
-    def head_mean(value):
-        total = jnp.dot(value.astype(jnp.bfloat16), ones, preferred_element_type=jnp.float32)
-        return total * (1.0 / HEAD_DIM)
+    head_mean, turn = head_tools(lane)
 
     def head_back(value, raw, gain):
-        half = HEAD_DIM // 2
-        first = lanes_below(value.shape, half, HEAD_DIM)
-        turned = jnp.where(first, pltpu.roll(value, lane - half, 1), pltpu.roll(value, half, 1))
-        value = value * at.cosine[...] - turned * at.sine[...]
+        value = value * at.cosine[...] - turn(value) * at.sine[...]
         raw = raw.astype(jnp.float32)
         inverse = lax.rsqrt(head_mean(raw * raw) + EPS)
         raw = raw * inverse
@@ -1262,7 +1735,7 @@
         sums = jnp.zeros((8, lane), jnp.float32)
         for part_at in range(0, width, lane):
             columns = pl.ds(part_at, lane)
-            value, more = head_back(wide[:, columns], queries_raw[:, columns], at.head_gains[0:1])
+            value, more = head_back(wide[:, columns], queries_raw[:, columns], at.vectors[7:8, pl.ds(0, lane)])
             g_all[:, pl.ds(heads_at + part_at, lane)] = value.astype(jnp.bfloat16)
             sums = sums + more
         small[head_row : head_row + 1, 0:lane] = both_halves(sums)[0:1]
@@ -1280,7 +1753,7 @@
             key_value = jnp.where(first, even, pltpu.roll(odd, HEAD_DIM, 1))
             value_value = jnp.where(first, pltpu.roll(even, HEAD_DIM, 1), odd)
             columns = pl.ds(pair * lane, lane)
-            value, more = head_back(key_value, keys_raw[:, columns], at.head_gains[1:2])
+            value, more = head_back(key_value, keys_raw[:, columns], at.vectors[8:9, pl.ds(0, lane)])
             place = heads_at + width + pair * lane
             g_all[:, pl.ds(place, lane)] = value.astype(jnp.bfloat16)
             place += width // 2
@@ -1312,6 +1785,9 @@
 
     def convolution_back():
         within = lax.rem(lax.broadcasted_iota(jnp.int32, (tokens, lane), 0), length)
+        position = within + seq * length
+        keep_one = position - 1 >= at.seg_start[...]
+        keep_two = position - 2 >= at.seg_start[...]
         edge = lax.broadcasted_iota(jnp.int32, (8, lane), 0)
         for part_at in range(0, width, lane):
             columns = pl.ds(part_at, lane)
@@ -1325,9 +1801,9 @@
                 sums = jnp.sum(conv_grad * saved_part(1 + tap, columns), axis=0, keepdims=True)
                 place = blocks * (4 + tap) + block
                 small[place : place + 1, inside : inside + lane] = sums
-            two = at.taps[0:1, columns] * at.keep[1] * conv_grad
-            one = at.taps[1:2, columns] * at.keep[0] * conv_grad
-            here = at.taps[2:3, columns] * conv_grad
+            two = jnp.where(keep_two, at.vectors[4:5, columns] * conv_grad, 0.0)
+            one = jnp.where(keep_one, at.vectors[5:6, columns] * conv_grad, 0.0)
+            here = at.vectors[6:7, columns] * conv_grad
             here += jnp.where(within < length - 1, pltpu.roll(one, tokens - 1, 0), 0.0)
             here += jnp.where(within < length - 2, pltpu.roll(two, tokens - 2, 0), 0.0)
             normed_grad[:, columns] = here
@@ -1411,6 +1887,19 @@
             query_heads()
 
         when("queries", to_queries)
+        def pick_rows(j):
+            block_rows = x_all.shape[3]
+            shape = (shards * 2 * block_rows, tokens)
+            place = lax.broadcasted_iota(jnp.int32, shape, 0)
+            vector, shard = lax.rem(place, 2 * block_rows), place // (2 * block_rows)
+            wanted = blocks * vector + jnp.where(vector < 7, shard * blocks // shards, 0)
+            found = lax.broadcasted_iota(jnp.int32, shape, 1) == wanted
+            found = jnp.logical_and(found, vector < 8).astype(jnp.float32).astype(jnp.bfloat16)
+            x_first = entries[-1][0]
+            target = x_all.shape[:2] + (2, block_rows, tokens)
+            x_all[:, :, x_first : x_first + 2] = found.reshape(target)
+
+        when("queries", pick_rows, 2)
         when("queries", lambda j: project_back("queries", 0, heads_at, heads_at + COLS), 1)
 
         def to_keys(j):
@@ -1505,7 +1994,6 @@
             pltpu.VMEM((tokens, width), low),
             pltpu.VMEM((tokens, width), low),
             pltpu.VMEM((tokens, width), full),
-            pltpu.VMEM((rows, total_length, tokens // rows), low),
             pltpu.VMEM((tokens, width), low),
             pltpu.VMEM((tokens, width // 2), low),
             pltpu.VMEM((tokens, width), full),
@@ -1528,43 +2016,6 @@
             transcendentals=0,
         ),
     )(*values)
-
-
-def attention_kernel(query_ref, both_ref, mask_ref, out_ref):
-    query = two_heads(query_ref[...], True)
-    both = both_ref[0]
-    allowed = mask_ref[0].astype(jnp.float32)
-    weights = jnp.exp(dot_nt(query, both)) * jnp.concatenate([allowed, allowed], axis=0)
-    weights = weights * (1.0 / jnp.sum(weights, axis=-1, keepdims=True))
-    value = jnp.dot(weights.astype(jnp.bfloat16), both, preferred_element_type=jnp.float32)
-    length = out_ref.shape[0]
-    first = lanes_below((length, 2 * HEAD_DIM), HEAD_DIM, 2 * HEAD_DIM)
-    out_ref[...] = jnp.where(
-        first, pltpu.roll(value[:length], HEAD_DIM, 1), value[length:]
-    ).astype(out_ref.dtype)
-
-
-def attention(queries, keys_values, mask):
-    rows, total_length, width = keys_values.shape
-    length = queries.shape[0] // rows
-    lane = 2 * HEAD_DIM
-    return pl.pallas_call(
-        attention_kernel,
-        grid=(rows, width // lane),
-        in_specs=[
-            pl.BlockSpec((length, lane), lambda r, h: (r, h)),
-            pl.BlockSpec((1, total_length, lane), lambda r, h: (r, 0, h)),
-            pl.BlockSpec((1, length, total_length), lambda r, h: (r, 0, 0)),
-        ],
-        out_specs=pl.BlockSpec((length, lane), lambda r, h: (r, h)),
-        out_shape=jax.ShapeDtypeStruct(queries.shape, jnp.bfloat16),
-        compiler_params=pltpu.CompilerParams(vmem_limit_bytes=32 * 2**20),
-        cost_estimate=pl.CostEstimate(
-            flops=8 * queries.shape[0] * total_length * width,
-            bytes_accessed=4 * keys_values.size,
-            transcendentals=2 * queries.shape[0] * total_length * KV_HEADS,
-        ),
-    )(queries, keys_values, mask)
 
 
 def fused_body(
@@ -1594,121 +2045,46 @@
     full, low = jnp.float32, jnp.bfloat16
     rows, length, width = tokens.shape
     token_count = rows * length
+    lane = 2 * HEAD_DIM
     row_count, shards = lax.axis_size("row"), lax.axis_size("seq")
     seq = lax.axis_index("seq")
     positions = seq * length + jnp.arange(length, dtype=jnp.int32)
-    segment, seg_start = segment_info(lengths, positions)
+    _, seg_start = segment_info(lengths, positions)
     offsets = positions[None, :] - seg_start
-
-    def flat(value):
-        return value.reshape(token_count, -1)
-
-    hidden_zero = tokens.astype(full)
-    mixer_in = norm_rows(hidden_zero, mixer_gain.astype(full)).astype(low)
-    projected = dense(mixer_in, mixer_input)
-    entry, exit_gate, carrier = [
-        projected[..., number * width : (number + 1) * width] for number in range(3)
-    ]
-    product = (entry * carrier).astype(low)
-    previous = passed_along(product[:, length - 2 :, :], "seq", 1)
-    extended = jnp.concatenate([previous, product], axis=1).astype(full)
-    keep_one = (positions[None, :] - 1 >= seg_start).astype(full)[..., None]
-    keep_two = (positions[None, :] - 2 >= seg_start).astype(full)[..., None]
-    taps = mixer_kernel.astype(full)
-    two_back = keep_two * extended[:, :length]
-    one_back = keep_one * extended[:, 1 : length + 1]
-    current = extended[:, 2:]
-    convolved = taps[2] * current + taps[1] * one_back + taps[0] * two_back
-    gated = (exit_gate * convolved).astype(low)
-    hidden_one = hidden_zero + dense(gated, mixer_output)
-    mixer_saved = jnp.concatenate(
-        [flat(part).astype(low) for part in (convolved, two_back, one_back, current)]
-    )
-    projected_saved = jnp.concatenate(
-        [flat(part).astype(low) for part in (entry, exit_gate, carrier)]
-    )
-
-    def feed(hidden, gain, gate_matrix, up_matrix, down_matrix):
-        normed = norm_rows(hidden, gain.astype(full)).astype(low)
-        gate_value, upward = dense(normed, gate_matrix), dense(normed, up_matrix)
-        active = swiglu(gate_value, upward).astype(low)
-        saved = (normed, active, flat(gate_value.astype(low)), flat(upward.astype(low)))
-        return hidden + dense(active, down_matrix), saved
-
-    hidden_two, first_saved = feed(hidden_one, first_gain, first_gate, first_up, first_down)
-
-    attend_in = norm_rows(hidden_two, attend_gain.astype(full)).astype(low)
-    queries_raw, keys_raw = dense(attend_in, query_weight), dense(attend_in, key_weight)
-    values = dense(attend_in, value_weight)
-
-    def head_path(value, heads, gain):
-        value = value.reshape(rows, length, heads, HEAD_DIM)
-        return rotate(norm_rows(value, gain.astype(full)), offsets)
-
-    queries_low = flat(
-        (head_path(queries_raw, HEADS, query_gain).astype(low) * low(HEAD_DIM**-0.5))
-    )
-    keys_low = head_path(keys_raw, KV_HEADS, key_gain).astype(low)
-    values_low = values.astype(low).reshape(keys_low.shape)
-    both = jnp.stack([keys_low, values_low], axis=3).reshape(rows, length, width)
-    keys_values = lax.all_gather(both, "seq", axis=1, tiled=True)
-    total_length = keys_values.shape[1]
-    key_positions = jnp.arange(total_length, dtype=jnp.int32)
-    key_segment, _ = segment_info(lengths, key_positions)
-    allowed = (segment[:, :, None] == key_segment[:, None, :]) & (
-        positions[None, :, None] >= key_positions[None, None, :]
-    )
-    allowed_turned = (segment[:, None, :] == key_segment[:, :, None]) & (
-        positions[None, None, :] >= key_positions[None, :, None]
-    )
-    attended = attention(queries_low, keys_values, allowed.astype(low))
-    hidden_three = hidden_two + dense(attended.reshape(tokens.shape), attend_output)
-
     half = HEAD_DIM // 2
     inverse = THETA ** (-2.0 * jnp.arange(half, dtype=full) / HEAD_DIM)
-    angles = offsets.astype(full).reshape(token_count, 1) * inverse
-    cosine, sine = jnp.cos(angles), jnp.sin(angles)
-    block_rows = math.gcd(width // shards, first_down.shape[0] // shards)
-
-    def turned(inputs):
-        inputs = flat(inputs).T
-        blocks = inputs.shape[0] // shards // block_rows
-        return inputs.reshape(shards // 2, 2, blocks, block_rows, token_count)
-
-    blocks = width // COLS
-    shape = (shards, 2 * block_rows, token_count)
-    shard_at, row_at, token_at = [lax.broadcasted_iota(jnp.int32, shape, dim) for dim in range(3)]
-    wanted = blocks * row_at + jnp.where(row_at < 7, shard_at * blocks // shards, 0)
-    picks = ((row_at < 8) & (token_at == wanted)).astype(low)
-    picks = picks.reshape(shards // 2, 2, 2, block_rows, token_count)
-
-    def padded(value):
-        return jnp.pad(value.astype(full), ((0, 8 - value.shape[0]), (0, 0)))
-
-    lane = 2 * HEAD_DIM
+    angles = offsets.astype(full).reshape(token_count, 1) * jnp.tile(inverse, 4)
+    sign = jnp.tile(jnp.concatenate([-jnp.ones(half, full), jnp.ones(half, full)]), 2)
+    vectors = jnp.concatenate(
+        [
+            jnp.stack([second_gain, attend_gain, first_gain, mixer_gain]),
+            mixer_kernel,
+            jnp.stack([jnp.tile(gain, width // HEAD_DIM) for gain in (query_gain, key_gain)]),
+            jnp.zeros((7, width), low),
+        ]
+    ).astype(full)
+    tables = dict(
+        cosine=jnp.cos(angles),
+        sine=jnp.sin(angles) * sign,
+        seg_start=jnp.broadcast_to(seg_start.reshape(token_count, 1), (token_count, lane)),
+        vectors=vectors,
+    )
     arrays = dict(
-        cotangent=flat(cotangent),
-        gate_one=first_saved[2],
-        up_one=first_saved[3],
-        hidden_three=flat(hidden_three),
-        hidden_two=flat(hidden_two),
-        hidden_one=flat(hidden_one),
-        hidden_zero=flat(hidden_zero),
-        queries_low=queries_low,
-        keys_values=keys_values,
-        mask=allowed_turned.astype(low),
-        queries_raw=flat(queries_raw).astype(low),
-        keys_raw=flat(keys_raw).astype(low),
-        mixer_saved=mixer_saved,
-        projected=projected_saved,
-        cosine=jnp.concatenate([cosine] * 4, axis=1),
-        sine=jnp.concatenate([-sine, sine] * 2, axis=1),
-        keep=jnp.broadcast_to(
-            jnp.stack([keep_one, keep_two]).reshape(2, token_count, 1), (2, token_count, lane)
-        ),
-        gains=padded(jnp.stack([second_gain, attend_gain, first_gain, mixer_gain])),
-        taps=padded(mixer_kernel),
-        head_gains=padded(jnp.tile(jnp.stack([query_gain, key_gain]), (1, 2))),
+        tokens=tokens.reshape(token_count, width),
+        mixer_input=mixer_input,
+        mixer_output=mixer_output,
+        first_gate=first_gate,
+        first_up=first_up,
+        first_down=first_down,
+        query_weight=query_weight,
+        key_weight=key_weight,
+        value_weight=value_weight,
+        attend_output=attend_output,
+        **tables,
+    )
+    saved = forward(arrays, tuple(tables), rows, shards, 2)
+    block_rows = saved["attended_x"].shape[3]
+    weights = dict(
         second_down=second_down,
         second_gate=second_gate,
         second_up=second_up,
@@ -1722,19 +2098,28 @@
         mixer_output=mixer_output,
         mixer_input=mixer_input,
     )
-    resident = ("cosine", "sine", "keep", "gains", "taps", "head_gains")
+    names = ["gate_one", "up_one", "hidden_three", "hidden_two", "hidden_one", "hidden_zero"]
+    names += ["queries_out", "keys_values", "queries_raw", "keys_raw", "mixer_saved", "projected"]
+    starts = jnp.broadcast_to(seg_start[:, None, :], (rows, 8, length))
+    arrays = dict(
+        cotangent=cotangent.reshape(token_count, width),
+        **{name: saved[name] for name in names},
+        **tables,
+        starts=starts,
+        **weights,
+    )
     hidden_columns = first_gate.shape[1]
     head_columns = width + 2 * key_weight.shape[1]
     groups = [
         (width // shards // block_rows, 2 * hidden_columns),
         (hidden_columns // shards // block_rows, width),
-        (turned(attended), width),
-        (turned(attend_in), head_columns),
-        (turned(first_saved[1]), width),
-        (turned(first_saved[0]), 2 * hidden_columns),
-        (turned(gated), width),
-        (turned(mixer_in), 3 * width),
-        (picks, COLS),
+        (saved["attended_x"], width),
+        (saved["attend_in_x"], head_columns),
+        (saved["active_x"], width),
+        (saved["first_in_x"], 2 * hidden_columns),
+        (saved["gated_x"], width),
+        (saved["mixer_in_x"], 3 * width),
+        (2, COLS),
     ]
     (
         second_both,
@@ -1748,7 +2133,7 @@
         sums,
         token_grad,
         mixed,
-    ) = backward(groups, arrays, resident, row_count, shards, 1)
+    ) = backward(groups, arrays, tuple(tables) + ("starts",), row_count, shards, 1)
 
     def single(value):
         return value.astype(full)

time: 505 us -> 464 us (0.919)
  Pallas kernels: 372 us -> 433 us
  matrix products: 30.3 us -> 0 us
  other arithmetic: 43.1 us -> 19.2 us
  local copies, waits for them, and re-layouts: 31.7 us -> 9.9 us
  between operations: 14.8 us -> 0.73 us
  waiting for transfers between devices: 10.4 us -> 0 us
    pallas_call x1, Pallas kernels: 12.5 us -> 54.9 us  [forward(): pl.pallas_call(functools.partial(forward_kernel, list(arrays), list(outs)...]
    dot_general x9 -> x0, matrix products: 30.3 us -> none  [dense(): jnp.einsum('rtd,df->rtf', inputs, matrix, preferred_element_type=jnp.floa...]
    pallas_call x1, Pallas kernels: 359 us -> 378 us  [backward(): pl.pallas_call(kernel, out_shape=[jax.ShapeDtypeStruct((x_count * block_r...]
    reshape x6 -> x0, local copies, waits for them, and re-layouts: 10.5 us -> none  [the longest x5 8.49 us: flat(): return value.reshape(token_count, -1)]
    all_gather x1 -> x0, waiting for transfers between devices: 10.4 us -> none  [fused_body(): keys_values = lax.all_gather(both, 'seq', axis=1, tiled=True)]
    convert_element_type x19 -> x2, other arithmetic: 9.24 us -> 0.64 us  [the longest x1 0.64 us: fused_body(): vectors = jnp.concatenate([jnp.stack([second_gain, attend_gain, first_gai...]
    concatenate x5 -> x0, other arithmetic: 5.69 us -> none  [the longest x1 2.69 us: fused_body(): jnp.concatenate([flat(part).astype(low) for part in (convolved, two_back,...]
    unnamed x98 -> x18, local copies, waits for them, and re-layouts: 7.1 us -> 1.62 us
  transfers between devices with their start and end apart: 2 -> 0, of which waited for: 1 -> 0; matrix products, arithmetic and copies ran while one was open for 6% -> 0% of each run, Pallas kernels for 0% -> 0%
where the time goes in v4:
time: 464 us; the launch traced here: 463 us
  Pallas kernels  433 us (93%)
  other arithmetic  19.2 us (4%)
  local copies, waits for them, and re-layouts  9.9 us (2%)
    pallas_call x1, Pallas kernels, backward(): pl.pallas_call(kernel, out_shape=[jax.ShapeDtypeStruct((x_count * block_r...  378 us
    pallas_call x1, Pallas kernels, forward(): pl.pallas_call(functools.partial(forward_kernel, list(arrays), list(outs)...  54.9 us
    convert_element_type x9, other arithmetic, single(): return value.astype(full)  15.1 us

profile of v4, /device:TPU:0, one launch (start us, length us, event | category | flops | bytes accessed | tf_op | source)
XLA Modules:
  0.0 463.1 jit_solution(7980211302930505476)
XLA Ops:
  0.7 0.8 reduce_window_sum.11
  1.5 0.1 fusion.1
  1.7 0.7 tile.9
  2.5 1.2 fusion
  3.7 0.8 broadcast_in_dim.17.refs_12_.refs_21_
  4.5 0.7 tile.10
  5.1 0.1 stack_tile.6
  5.2 0.7 tile.11
  5.9 0.1 stack_tile.7
  6.0 0.7 stack.12
  6.6 0.7 stack.13
  7.3 0.7 stack.14
  8.0 0.7 stack.15
  8.7 0.8 concatenate.3
  9.5 0.6 convert_element_type.52.refs_13_.refs_22_
  10.1 54.9 %shard_map.373 = (f32[256,1024]{1,0:T(8,128)}, f32[256,1024]{1,0:T(8,128)}, f32[256,1024]{1,0:T(8,128)}, f32[256,1024]{1,0:T(8,128)}, bf16[256,4608]{1,0:T(8,128...) custom-call(bf16[256,1024]{1,0:T(8,128)(2,1)} %bitcast.28, ...), custom_call_target="tpu_custom_call" | custom-call | flops 11198791680 | bytes 43745280 | tf_op jit(solution)/shard_map/pallas_call | solution.py:1407
  65.0 0.6 broadcast_in_dim.19.refs_23_
  65.6 378.3 %shard_map.374 = (bf16[128,9216]{1,0:T(8,128)(2,1)}, bf16[576,1024]{1,0:T(8,128)(2,1)}, bf16[128,1024]{1,0:T(8,128)(2,1)}, bf16[128,2048]{1,0:T(8,128)(2,1)}, bf...) custom-call(bf16[4,2,2,64,256]{4,3,2,1,0:T(8,128)(2,1)} %get-tuple-e, ...), custom_call_target="tpu_custom_call" | custom-call | flops 37044092928 | bytes 72351744 | tf_op jit(solution)/shard_map/pallas_call | solution.py:1977
  444.0 6.4 %slice_convert_fusion = (f32[128,4608]{1,0:T(8,128)}, f32[128,4608]{1,0:T(8,128)}, f32[128,4608]{1,0:T(8,128)}, f32[128,4608]{1,0:T(8,128)}) fusion(bf16[128,9216]{1,0:T(8,128)(2,1)} %get-tuple-element.77, bf16[128,9216]{1,0:T(8,128)(2,1)} %get-tuple-element.73), kind=kLoop, calls=%fused_computation | loop fusion | flops 2359296 | bytes 14155776 | tf_op jit(solution)/shard_map/convert_element_type | solution.py:2139
  450.4 1.7 convert_element_type.58
  452.1 1.7 convert_element_type.65
  453.8 1.3 convert_element_type.54
  455.1 0.8 slice_convert_fusion.5
  456.0 0.8 convert_element_type.55
  456.8 0.8 convert_element_type.62
  457.7 0.8 slice_convert_fusion.4
  458.5 0.6 dynamic-slice_convert_fusion
  459.1 0.5 slice_bitcast_fusion
  459.7 0.6 slice.37
  460.2 1.3 fusion.6
  461.5 0.8 copy.45
  462.3 0.8 copy.46
  (23 shorter events, 0.2 us)
Async XLA Ops:
  444.0 6.5 %copy-start.1 = (bf16[576,1024]{1,0:T(8,128)(2,1)S(1)}, bf16[576,1024]{1,0:T(8,128)(2,1)}, u32[]{:S(2)}) copy-start(bf16[576,1024]{1,0:T(8,128)(2,1)} %get-tuple-element.74) | copy-start | bytes 3538948
  450.4 1.7 copy-start
  452.1 1.7 copy-start.2
  452.1 3.0 copy-start.3
  453.8 2.2 copy-start.7
  453.8 3.0 copy-start.6
  453.8 7.7 %copy-start.5 = (bf16[256,1024]{1,0:T(8,128)(2,1)S(1)}, bf16[256,1024]{1,0:T(8,128)(2,1)}, u32[]{:S(2)}) copy-start(bf16[256,1024]{1,0:T(8,128)(2,1)} %get-tuple-element.68) | copy-start | bytes 1572868
  455.1 7.2 %copy-start.4 = (bf16[256,1024]{1,0:T(8,128)(2,1)S(1)}, bf16[256,1024]{1,0:T(8,128)(2,1)}, u32[]{:S(2)}) copy-start(bf16[256,1024]{1,0:T(8,128)(2,1)} %get-tuple-element.69) | copy-start | bytes 1572868

commit v5 on v4

--- a/solution.py
+++ b/solution.py
@@ -939,6 +939,19 @@
     return jnp.concatenate(parts, axis=0).astype(jnp.bfloat16)
 
 
+def segment_start(lengths, which, place):
+    end, start = jnp.int32(0), jnp.zeros(place.shape, jnp.int32)
+    for number in range(lengths.shape[1]):
+        end = end + lengths[which, number]
+        start = jnp.where(place >= end, end, start)
+    return start
+
+
+def both_halves(value):
+    value = jnp.broadcast_to(value, (8,) + value.shape[1:])
+    return (value + pltpu.roll(value, HEAD_DIM, 1))[0:1]
+
+
 def head_tools(lane):
     head_of = lax.broadcasted_iota(jnp.int32, (lane, lane), 0) // HEAD_DIM
     ones = head_of == lax.broadcasted_iota(jnp.int32, (lane, lane), 1) // HEAD_DIM
@@ -969,6 +982,8 @@
     partner = [seq + (1 << bit) * (1 - 2 * bits[bit]) for bit in range(3)]
     head_mean, turn = head_tools(lane)
 
+    ahead = at.tiles_a.shape[0]
+
     def tile_copies(step, slot):
         name, j = step
         b, c = at.tiles_b.at[slot], at.tiles_c.at[slot]
@@ -976,15 +991,15 @@
         def columns(block):
             return pl.ds(block * COLS if isinstance(block, int) else pl.multiple_of(block * COLS, COLS), COLS)
 
-        if name == "mixer_input":
+        if name == MIXER_INPUT:
             first, second = ((0, 4), (1, 5), (2, 3))[j]
             moves = [
                 (at.mixer_input.at[:, columns(first)], b),
                 (at.mixer_input.at[:, columns(second)], c),
             ]
-        elif name == "keys":
+        elif name == KEYS:
             moves = [(at.key_weight, b), (at.value_weight, c)]
-        elif name == "first":
+        elif name == FIRST:
             moves = [
                 (at.first_gate.at[:, columns(j)], b),
                 (at.first_up.at[:, columns(j)], c),
@@ -992,9 +1007,9 @@
             ]
         else:
             matrix = {
-                "mixer_output": at.mixer_output,
-                "queries": at.query_weight,
-                "attend_output": at.attend_output,
+                MIXER_OUTPUT: at.mixer_output,
+                QUERIES: at.query_weight,
+                ATTEND_OUTPUT: at.attend_output,
             }[name]
             moves = [(matrix.at[:, columns(0)], b), (matrix.at[:, columns(1)], c)]
         return [
@@ -1002,18 +1017,19 @@
             for place, (source, target) in enumerate(moves)
         ]
 
-    steps = [("mixer_input", 0), ("mixer_input", 1), ("mixer_input", 2), ("mixer_output", 0)]
+    steps = [(MIXER_INPUT, 0), (MIXER_INPUT, 1), (MIXER_INPUT, 2), (MIXER_OUTPUT, 0)]
     first_at = len(steps)
-    steps += [("first", j) for j in range(hidden_blocks)]
-    steps += [("keys", 0), ("queries", 0), ("attend_output", 0)]
+    steps += [(FIRST, j) for j in range(hidden_blocks)]
+    steps += [(KEYS, 0), (QUERIES, 0), (ATTEND_OUTPUT, 0)]
 
     def begin(number):
-        for copy in tile_copies(steps[number], number % 2):
+        for copy in tile_copies(steps[number], number % ahead):
             copy.wait()
-        if number + 1 < len(steps):
-            for copy in tile_copies(steps[number + 1], (number + 1) % 2):
+        later = number + ahead - 1
+        if later < len(steps):
+            for copy in tile_copies(steps[later], later % ahead):
                 copy.start()
-        return number % 2
+        return number % ahead
 
     saves = []
 
@@ -1033,15 +1049,41 @@
     def times(left, tile):
         return jnp.dot(left[...], tile, preferred_element_type=jnp.float32)
 
-    for copy in tile_copies(steps[0], 0):
-        copy.start()
     token_load = pltpu.make_async_copy(at.tokens, at.attended, at.load_sem.at[0])
     token_load.start()
+    for number in range(ahead - 1):
+        for copy in tile_copies(steps[number], number):
+            copy.start()
     at.halo_in[...] = jnp.zeros_like(at.halo_in)
     barrier = pltpu.get_barrier_semaphore()
     others = partner + [lax.rem(seq + step, shards) for step in (1, shards - 1)]
     for other in others:
         pl.semaphore_signal(barrier, inc=1, device_id=(row, other), device_id_type=MESH)
+    at.vectors[...] = jnp.zeros_like(at.vectors)
+    gains = [at.second_gain, at.attend_gain, at.first_gain, at.mixer_gain]
+    for number, gain in enumerate(gains):
+        at.vectors[number : number + 1, :] = gain[...].astype(jnp.float32).reshape(1, width)
+    at.vectors[4:7, :] = at.mixer_kernel[...].astype(jnp.float32)
+    for number, gain in enumerate((at.query_gain, at.key_gain)):
+        at.vectors[7 + number : 8 + number, 0:HEAD_DIM] = (
+            gain[...].astype(jnp.float32).reshape(1, HEAD_DIM)
+        )
+    half = HEAD_DIM // 2
+    lane_at = lax.broadcasted_iota(jnp.int32, (length, lane), 1)
+    power = lax.rem(lane_at, half).astype(jnp.float32) * (-2.0 * math.log(THETA) / HEAD_DIM)
+    inverse = jnp.exp(power)
+    side = jnp.where(lanes_below((length, lane), half, HEAD_DIM), -1.0, 1.0)
+    place = lax.broadcasted_iota(jnp.int32, (length, lane), 0) + seq * length
+    for which in range(rows):
+        start = segment_start(at.lengths, which, place)
+        angle = (place - start).astype(jnp.float32) * inverse
+        span = pl.ds(which * length, length)
+        at.seg_start[span] = start
+        at.cosine[span] = jnp.cos(angle)
+        at.sine[span] = jnp.sin(angle) * side
+    save(at.vectors, at.vectors_out)
+    save(at.cosine, at.cosine_out)
+    save(at.sine, at.sine_out)
     token_load.wait()
     at.hidden_a[...] = at.attended[...].astype(jnp.float32)
     save(at.hidden_a, at.hidden_zero)
@@ -1128,19 +1170,23 @@
     at.hidden_c[...] = at.hidden_b[...]
 
     def feed_tile(j, carried):
-        slot = lax.rem(first_at + j, 2)
-        for copy in tile_copies(("first", j), slot):
+        slot = lax.rem(first_at + j, ahead)
+        for copy in tile_copies((FIRST, j), slot):
             copy.wait()
-
-        @pl.when(j + 1 < hidden_blocks)
+        later = j + ahead - 1
+        later_slot = lax.rem(first_at + later, ahead)
+
+        @pl.when(later < hidden_blocks)
         def _():
-            for copy in tile_copies(("first", j + 1), 1 - slot):
+            for copy in tile_copies((FIRST, later), later_slot):
                 copy.start()
 
-        @pl.when(j + 1 == hidden_blocks)
-        def _():
-            for copy in tile_copies(("keys", 0), 1 - slot):
-                copy.start()
+        for past, step in enumerate(steps[first_at + hidden_blocks :][: ahead - 1]):
+
+            @pl.when(later == hidden_blocks + past)
+            def _():
+                for copy in tile_copies(step, later_slot):
+                    copy.start()
 
         gate_value = times(at.low_three, at.tiles_b[slot])
         up_value = times(at.low_three, at.tiles_c[slot])
@@ -1174,7 +1220,7 @@
     first = lanes_below((tokens, lane), HEAD_DIM, lane)
     own = pl.ds(pl.multiple_of(seq * length, length), length)
     for pair in range(width // lane // 2):
-        keys = head_path(at.work[:, pl.ds(pair * lane, lane)], at.vectors[8:9, pl.ds(0, lane)])
+        keys = head_path(at.work[:, pl.ds(pair * lane, lane)], both_halves(at.vectors[8:9, pl.ds(0, lane)]))
         values = at.work[:, pl.ds(width // 2 + pair * lane, lane)]
         even = jnp.where(first, keys, pltpu.roll(values, HEAD_DIM, 1)).astype(jnp.bfloat16)
         odd = jnp.where(first, pltpu.roll(keys, HEAD_DIM, 1), values).astype(jnp.bfloat16)
@@ -1215,7 +1261,7 @@
     save(at.queries_low, at.queries_raw)
     for head in range(width // lane):
         columns = pl.ds(head * lane, lane)
-        query = head_path(at.work[:, columns], at.vectors[7:8, pl.ds(0, lane)]).astype(jnp.bfloat16)
+        query = head_path(at.work[:, columns], both_halves(at.vectors[7:8, pl.ds(0, lane)])).astype(jnp.bfloat16)
         query = query * jnp.bfloat16(HEAD_DIM**-0.5)
         at.scaled[:, columns] = query
         for which in range(rows):
@@ -1243,6 +1289,7 @@
 
     at.sums[...] = jnp.zeros_like(at.sums)
     pairs_of = width // lane
+    together = 4
     chip = seq // 2
 
     def attend(other):
@@ -1259,19 +1306,25 @@
                 allowed = jnp.logical_and(key_at >= start, key_at <= query_at)
                 allowed = jnp.concatenate([allowed, allowed], axis=0)
 
-                def one(head, carried):
-                    columns = pl.ds(pl.multiple_of(head * lane, lane), lane)
-                    both = at.both[which, span, columns]
-                    place = which * pairs_of + head
-                    weights = jnp.exp(dot_nt(at.paired[place], both))
-                    weights = jnp.where(allowed, weights, 0.0).astype(jnp.bfloat16)
-                    right = jnp.where(first, 1.0, both.astype(jnp.float32)).astype(jnp.bfloat16)
-                    at.sums[place] += jnp.dot(
-                        weights, right, preferred_element_type=jnp.float32
-                    )
+                def some(group, carried):
+                    heads = [group * together + head for head in range(together)]
+                    boths = [
+                        at.both[which, span, pl.ds(pl.multiple_of(head * lane, lane), lane)]
+                        for head in heads
+                    ]
+                    places = [which * pairs_of + head for head in heads]
+                    scores = [
+                        dot_nt(at.paired[place], both) for place, both in zip(places, boths)
+                    ]
+                    for place, score, both in zip(places, scores, boths):
+                        weights = jnp.where(allowed, jnp.exp(score), 0.0).astype(jnp.bfloat16)
+                        right = jnp.where(first, 1.0, both.astype(jnp.float32))
+                        at.sums[place] += jnp.dot(
+                            weights, right.astype(jnp.bfloat16), preferred_element_type=jnp.float32
+                        )
                     return carried
 
-                lax.fori_loop(0, pairs_of, one, 0)
+                lax.fori_loop(0, pairs_of // together, some, 0)
 
     twin.wait()
     attend(chip)
@@ -1358,13 +1411,16 @@
         attend_in_x=(x_shape(width), low),
         attended_x=(x_shape(width), low),
         active_x=(x_shape(hidden_columns), low),
+        vectors_out=((16, width), full),
+        cosine_out=((tokens, 2 * HEAD_DIM), full),
+        sine_out=((tokens, 2 * HEAD_DIM), full),
     )
     pairs = rows * width // (2 * HEAD_DIM)
     dma = pltpu.SemaphoreType.DMA
     scratch = dict(
-        tiles_a=pltpu.VMEM((2, COLS, width), low),
-        tiles_b=pltpu.VMEM((2, width, COLS), low),
-        tiles_c=pltpu.VMEM((2, width, COLS), low),
+        tiles_a=pltpu.VMEM((4, COLS, width), low),
+        tiles_b=pltpu.VMEM((4, width, COLS), low),
+        tiles_c=pltpu.VMEM((4, width, COLS), low),
         hidden_a=pltpu.VMEM((tokens, width), full),
         hidden_b=pltpu.VMEM((tokens, width), full),
         hidden_c=pltpu.VMEM((tokens, width), full),
@@ -1392,22 +1448,27 @@
         turned_four=pltpu.VMEM(x_shape(width), low),
         turned_five=pltpu.VMEM(x_shape(width), low),
         turned_active=pltpu.VMEM(x_shape(hidden_columns), low),
+        vectors=pltpu.VMEM((16, width), full),
+        cosine=pltpu.VMEM((tokens, 2 * HEAD_DIM), full),
+        sine=pltpu.VMEM((tokens, 2 * HEAD_DIM), full),
+        seg_start=pltpu.VMEM((tokens, 2 * HEAD_DIM), jnp.int32),
         halo_out=pltpu.VMEM((rows, 8, width), full),
         halo_in=pltpu.VMEM((rows, 8, width), full),
-        tile_sem=dma((2, 3)),
+        tile_sem=dma((4, 3)),
         load_sem=dma((1,)),
         save_sem=dma((len(outs),)),
         halo_sem=dma((2,)),
         gather_send=dma((10,)),
         gather_recv=dma((10,)),
     )
+    spaces = dict.fromkeys(resident, pltpu.VMEM)
+    spaces["lengths"] = pltpu.SMEM
     any_space = pl.BlockSpec(memory_space=pl.ANY)
-    vmem_space = pl.BlockSpec(memory_space=pltpu.VMEM)
     weights = sum(value.size for value in arrays.values())
     results = pl.pallas_call(
         functools.partial(forward_kernel, list(arrays), list(outs), list(scratch), shards),
         out_shape=[jax.ShapeDtypeStruct(shape, kind) for shape, kind in outs.values()],
-        in_specs=[vmem_space if name in resident else any_space for name in arrays],
+        in_specs=[pl.BlockSpec(memory_space=spaces.get(name, pl.ANY)) for name in arrays],
         out_specs=[any_space] * len(outs),
         scratch_shapes=list(scratch.values()),
         compiler_params=pltpu.CompilerParams(
@@ -1420,17 +1481,18 @@
     return dict(zip(outs, results))
 
 
+SECOND, ATTEND_OUTPUT, ATTENTION, QUERIES, KEYS, FIRST, MIXER_OUTPUT, HALO, MIXER_INPUT, CLOSE = range(10)
 BACKWARD_STARTS = {
-    "second": 0,
-    "attend_output": 8,
-    "attention": 10,
-    "queries": 26,
-    "keys": 31,
-    "first": 32,
-    "mixer_output": 41,
-    "halo": 43,
-    "mixer_input": 44,
-    "close": 47,
+    SECOND: 0,
+    ATTEND_OUTPUT: 8,
+    ATTENTION: 10,
+    QUERIES: 26,
+    KEYS: 31,
+    FIRST: 32,
+    MIXER_OUTPUT: 41,
+    HALO: 43,
+    MIXER_INPUT: 44,
+    CLOSE: 47,
 }
 LOCAL_PAIRS = (18, 19, 26, 27)
 
@@ -1497,13 +1559,13 @@
     def tile_copies(name, j, slot):
         columns = pl.ds(pl.multiple_of(j * COLS, COLS), COLS)
         a, b, c = tiles_a.at[slot], tiles_b.at[slot], tiles_c.at[slot]
-        if name == "second":
+        if name == SECOND:
             moves = [
                 (at.second_gate.at[:, columns], b),
                 (at.second_up.at[:, columns], c),
                 (at.second_down.at[columns], a),
             ]
-        elif name == "first":
+        elif name == FIRST:
             moves = [
                 (at.first_down.at[columns], a),
                 (at.first_gate.at[:, columns], b),
@@ -1511,16 +1573,16 @@
                 (at.gate_one.at[:, columns], saved.at[slot, 0]),
                 (at.up_one.at[:, columns], saved.at[slot, 1]),
             ]
-        elif name == "attend_output":
+        elif name == ATTEND_OUTPUT:
             moves = [(at.attend_output.at[columns], a)]
-        elif name == "mixer_output":
+        elif name == MIXER_OUTPUT:
             moves = [(at.mixer_output.at[columns], a)]
-        elif name == "queries":
+        elif name == QUERIES:
             moves = [
                 (at.query_weight.at[:, pl.ds(0, COLS)], b),
                 (at.query_weight.at[:, pl.ds(COLS, COLS)], c),
             ]
-        elif name == "keys":
+        elif name == KEYS:
             moves = [(at.key_weight, b), (at.value_weight, c)]
         else:
             even = pl.multiple_of(2 * j * COLS, COLS)
@@ -1535,13 +1597,13 @@
         ]
 
     steps = [
-        ("second", hidden_blocks),
-        ("attend_output", blocks),
-        ("queries", 1),
-        ("keys", 1),
-        ("first", hidden_blocks),
-        ("mixer_output", blocks),
-        ("mixer_input", 3 * blocks // 2),
+        (SECOND, hidden_blocks),
+        (ATTEND_OUTPUT, blocks),
+        (QUERIES, 1),
+        (KEYS, 1),
+        (FIRST, hidden_blocks),
+        (MIXER_OUTPUT, blocks),
+        (MIXER_INPUT, 3 * blocks // 2),
     ]
     first_step, total = {}, 0
     for name, number in steps:
@@ -1600,7 +1662,7 @@
 
     hidden_loads[0].start()
     cotangent_load.start()
-    for copy in tile_copies("second", 0, 0):
+    for copy in tile_copies(SECOND, 0, 0):
         copy.start()
     for copy in middle_loads + x_loads:
         copy.start()
@@ -1652,14 +1714,14 @@
         slot = tile_step(name, j)
         low = g_all[:, pl.ds(gradient_at, width)]
         active_grad = dot_nt(low, tiles_a[slot])
-        if name == "second":
+        if name == SECOND:
             gate_value = jnp.dot(normed[...], tiles_b[slot], preferred_element_type=jnp.float32)
             up_value = jnp.dot(normed[...], tiles_c[slot], preferred_element_type=jnp.float32)
         else:
             gate_value = saved[slot, 0].astype(jnp.float32)
             up_value = saved[slot, 1].astype(jnp.float32)
         share = 1.0 / (1.0 + jnp.exp(-gate_value))
-        if name == "second":
+        if name == SECOND:
             active = gate_value * share * up_value
             wide[...] += jnp.dot(
                 active.astype(jnp.bfloat16), tiles_a[slot], preferred_element_type=jnp.float32
@@ -1695,7 +1757,8 @@
         both = keys_values[row_at, :, columns]
         key_at = lax.broadcasted_iota(jnp.int32, (both.shape[0], length), 0)
         query_at = lax.broadcasted_iota(jnp.int32, (both.shape[0], length), 1) + seq * length
-        allowed = jnp.logical_and(key_at >= at.starts[row_at, 0:1], key_at <= query_at)
+        start = segment_start(at.lengths, row_at, query_at[0:8])[0:1]
+        allowed = jnp.logical_and(key_at >= start, key_at <= query_at)
         weights = jnp.exp(dot_nt(both, query))
         weights = jnp.where(jnp.concatenate([allowed, allowed], axis=1), weights, 0.0)
         weights = weights * (1.0 / jnp.sum(weights, axis=0, keepdims=True))
@@ -1726,22 +1789,19 @@
         value = value * gain
         return inverse * (value - raw * head_mean(value * raw)), sums
 
-    def both_halves(sums):
-        return sums + pltpu.roll(sums, HEAD_DIM, 1)
-
     head_row = 7 * blocks
 
     def query_heads():
-        sums = jnp.zeros((8, lane), jnp.float32)
+        sums = jnp.zeros((1, lane), jnp.float32)
         for part_at in range(0, width, lane):
             columns = pl.ds(part_at, lane)
-            value, more = head_back(wide[:, columns], queries_raw[:, columns], at.vectors[7:8, pl.ds(0, lane)])
+            value, more = head_back(wide[:, columns], queries_raw[:, columns], both_halves(at.vectors[7:8, pl.ds(0, lane)]))
             g_all[:, pl.ds(heads_at + part_at, lane)] = value.astype(jnp.bfloat16)
             sums = sums + more
-        small[head_row : head_row + 1, 0:lane] = both_halves(sums)[0:1]
+        small[head_row : head_row + 1, 0:lane] = both_halves(sums)
 
     def key_heads():
-        sums = jnp.zeros((8, lane), jnp.float32)
+        sums = jnp.zeros((1, lane), jnp.float32)
         first = lanes_below((tokens, lane), HEAD_DIM, lane)
         for pair in range(width // lane // 2):
             even, odd = [
@@ -1753,13 +1813,13 @@
             key_value = jnp.where(first, even, pltpu.roll(odd, HEAD_DIM, 1))
             value_value = jnp.where(first, pltpu.roll(even, HEAD_DIM, 1), odd)
             columns = pl.ds(pair * lane, lane)
-            value, more = head_back(key_value, keys_raw[:, columns], at.vectors[8:9, pl.ds(0, lane)])
+            value, more = head_back(key_value, keys_raw[:, columns], both_halves(at.vectors[8:9, pl.ds(0, lane)]))
             place = heads_at + width + pair * lane
             g_all[:, pl.ds(place, lane)] = value.astype(jnp.bfloat16)
             place += width // 2
             g_all[:, pl.ds(place, lane)] = value_value.astype(jnp.bfloat16)
             sums = sums + more
-        small[head_row : head_row + 1, lane : 2 * lane] = both_halves(sums)[0:1]
+        small[head_row : head_row + 1, lane : 2 * lane] = both_halves(sums)
 
     def project_back(name, j, even_at, odd_at):
         slot = tile_step(name, j)
@@ -1786,8 +1846,13 @@
     def convolution_back():
         within = lax.rem(lax.broadcasted_iota(jnp.int32, (tokens, lane), 0), length)
         position = within + seq * length
-        keep_one = position - 1 >= at.seg_start[...]
-        keep_two = position - 2 >= at.seg_start[...]
+        start = [
+            segment_start(at.lengths, which, position[which * length : (which + 1) * length])
+            for which in range(rows)
+        ]
+        start = jnp.concatenate(start, axis=0)
+        keep_one = position - 1 >= start
+        keep_two = position - 2 >= start
         edge = lax.broadcasted_iota(jnp.int32, (8, lane), 0)
         for part_at in range(0, width, lane):
             columns = pl.ds(part_at, lane)
@@ -1847,8 +1912,8 @@
                 run(j)
 
         when(
-            "second",
-            lambda j: feed_tile("second", j + 1, second_down, second_wide),
+            SECOND,
+            lambda j: feed_tile(SECOND, j + 1, second_down, second_wide),
             0,
             hidden_blocks - 1,
         )
@@ -1857,28 +1922,28 @@
             for copy in middle_loads + x_loads:
                 copy.wait()
 
-        when("attend_output", waits)
+        when(ATTEND_OUTPUT, waits)
 
         def to_attended(j):
             staged[...] = (hidden[...] + wide[...]).astype(jnp.bfloat16)
             mixed_copy.start()
             norm_back(0)
             low_gradient(output_at)
-            output_tile("attend_output", 0, output_at, attended_grad)
-
-        when("attend_output", to_attended)
-        when("attend_output", lambda j: output_tile("attend_output", 1, output_at, attended_grad), 1)
+            output_tile(ATTEND_OUTPUT, 0, output_at, attended_grad)
+
+        when(ATTEND_OUTPUT, to_attended)
+        when(ATTEND_OUTPUT, lambda j: output_tile(ATTEND_OUTPUT, 1, output_at, attended_grad), 1)
 
         def staged_free(j):
             mixed_copy.wait()
             raw_load.start()
 
-        when("attention", staged_free)
+        when(ATTENTION, staged_free)
 
         def attention(j):
             attention_head(j // KV_HEADS, lax.rem(j, KV_HEADS))
 
-        when("attention", attention, 0, rows * KV_HEADS)
+        when(ATTENTION, attention, 0, rows * KV_HEADS)
 
         def to_queries(j):
             raw_load.wait()
@@ -1886,7 +1951,7 @@
                 copy.start()
             query_heads()
 
-        when("queries", to_queries)
+        when(QUERIES, to_queries)
         def pick_rows(j):
             block_rows = x_all.shape[3]
             shape = (shards * 2 * block_rows, tokens)
@@ -1899,39 +1964,39 @@
             target = x_all.shape[:2] + (2, block_rows, tokens)
             x_all[:, :, x_first : x_first + 2] = found.reshape(target)
 
-        when("queries", pick_rows, 2)
-        when("queries", lambda j: project_back("queries", 0, heads_at, heads_at + COLS), 1)
+        when(QUERIES, pick_rows, 2)
+        when(QUERIES, lambda j: project_back(QUERIES, 0, heads_at, heads_at + COLS), 1)
 
         def to_keys(j):
             key_heads()
-            project_back("keys", 0, heads_at + width, heads_at + width + COLS)
+            project_back(KEYS, 0, heads_at + width, heads_at + width + COLS)
             norm_back(1)
             low_gradient(first_down)
 
-        when("keys", to_keys)
-        when("first", lambda j: feed_tile("first", j, first_down, first_wide), 0, hidden_blocks)
+        when(KEYS, to_keys)
+        when(FIRST, lambda j: feed_tile(FIRST, j, first_down, first_wide), 0, hidden_blocks)
 
         def to_gated(j):
             norm_back(2)
             low_gradient(mixer_out_at)
-            output_tile("mixer_output", 0, mixer_out_at, wide)
+            output_tile(MIXER_OUTPUT, 0, mixer_out_at, wide)
             for copy in late_loads:
                 copy.wait()
 
-        when("mixer_output", to_gated)
+        when(MIXER_OUTPUT, to_gated)
 
         def to_convolved(j):
-            output_tile("mixer_output", 1, mixer_out_at, wide)
+            output_tile(MIXER_OUTPUT, 1, mixer_out_at, wide)
             convolution_back()
 
-        when("mixer_output", to_convolved, 1)
-        when("halo", lambda j: product_back())
+        when(MIXER_OUTPUT, to_convolved, 1)
+        when(HALO, lambda j: product_back())
 
         def mixer_tile(j):
             even = pl.multiple_of(mixer_in_at + 2 * j * COLS, COLS)
-            project_back("mixer_input", j, even, pl.multiple_of(even + COLS, COLS))
-
-        when("mixer_input", mixer_tile, 0, numbers["mixer_input"])
+            project_back(MIXER_INPUT, j, even, pl.multiple_of(even + COLS, COLS))
+
+        when(MIXER_INPUT, mixer_tile, 0, numbers[MIXER_INPUT])
 
         def close(j):
             norm_back(3)
@@ -1939,11 +2004,11 @@
             out_copy.start()
             g_all[pl.ds(0, small.shape[0]), pl.ds(small_at, COLS)] = small[...].astype(jnp.bfloat16)
 
-        when("close", close)
-        when("close", lambda j: out_copy.wait(), 1)
+        when(CLOSE, close)
+        when(CLOSE, lambda j: out_copy.wait(), 1)
 
     exchange.meet()
-    feed_tile("second", 0, second_down, second_wide)
+    feed_tile(SECOND, 0, second_down, second_wide)
     exchange.run(task)
 
 
@@ -1958,7 +2023,8 @@
     values = list(xs) + list(arrays.values())
     rows, total_length = arrays["keys_values"].shape[:2]
     any_space = pl.BlockSpec(memory_space=pl.ANY)
-    vmem_space = pl.BlockSpec(memory_space=pltpu.VMEM)
+    spaces = dict.fromkeys(resident, pltpu.VMEM)
+    spaces["lengths"] = pltpu.SMEM
     key_blocks = total_length // shards // block_rows
 
     def kernel(*refs):
@@ -1981,7 +2047,7 @@
             for _, x_count, _, g_count, _ in entries
         ]
         + [jax.ShapeDtypeStruct((tokens, width), low)] * 2,
-        in_specs=[vmem_space if name in resident else any_space for name in names],
+        in_specs=[pl.BlockSpec(memory_space=spaces.get(name, pl.ANY)) for name in names],
         out_specs=[any_space] * (len(entries) + 2),
         scratch_shapes=[
             pltpu.VMEM((2, COLS, width), low),
@@ -2048,26 +2114,15 @@
     lane = 2 * HEAD_DIM
     row_count, shards = lax.axis_size("row"), lax.axis_size("seq")
     seq = lax.axis_index("seq")
-    positions = seq * length + jnp.arange(length, dtype=jnp.int32)
-    _, seg_start = segment_info(lengths, positions)
-    offsets = positions[None, :] - seg_start
-    half = HEAD_DIM // 2
-    inverse = THETA ** (-2.0 * jnp.arange(half, dtype=full) / HEAD_DIM)
-    angles = offsets.astype(full).reshape(token_count, 1) * jnp.tile(inverse, 4)
-    sign = jnp.tile(jnp.concatenate([-jnp.ones(half, full), jnp.ones(half, full)]), 2)
-    vectors = jnp.concatenate(
-        [
-            jnp.stack([second_gain, attend_gain, first_gain, mixer_gain]),
-            mixer_kernel,
-            jnp.stack([jnp.tile(gain, width // HEAD_DIM) for gain in (query_gain, key_gain)]),
-            jnp.zeros((7, width), low),
-        ]
-    ).astype(full)
     tables = dict(
-        cosine=jnp.cos(angles),
-        sine=jnp.sin(angles) * sign,
-        seg_start=jnp.broadcast_to(seg_start.reshape(token_count, 1), (token_count, lane)),
-        vectors=vectors,
+        lengths=lengths,
+        mixer_kernel=mixer_kernel,
+        mixer_gain=mixer_gain,
+        first_gain=first_gain,
+        attend_gain=attend_gain,
+        second_gain=second_gain,
+        query_gain=query_gain,
+        key_gain=key_gain,
     )
     arrays = dict(
         tokens=tokens.reshape(token_count, width),
@@ -2082,8 +2137,8 @@
         attend_output=attend_output,
         **tables,
     )
-    saved = forward(arrays, tuple(tables), rows, shards, 2)
-    block_rows = saved["attended_x"].shape[3]
+    saved = types.SimpleNamespace(**forward(arrays, tuple(tables), rows, shards, 2))
+    block_rows = saved.attended_x.shape[3]
     weights = dict(
         second_down=second_down,
         second_gate=second_gate,
@@ -2098,14 +2153,23 @@
         mixer_output=mixer_output,
         mixer_input=mixer_input,
     )
-    names = ["gate_one", "up_one", "hidden_three", "hidden_two", "hidden_one", "hidden_zero"]
-    names += ["queries_out", "keys_values", "queries_raw", "keys_raw", "mixer_saved", "projected"]
-    starts = jnp.broadcast_to(seg_start[:, None, :], (rows, 8, length))
+    tables = dict(vectors=saved.vectors_out, cosine=saved.cosine_out, sine=saved.sine_out)
     arrays = dict(
+        lengths=lengths,
         cotangent=cotangent.reshape(token_count, width),
-        **{name: saved[name] for name in names},
+        gate_one=saved.gate_one,
+        up_one=saved.up_one,
+        hidden_three=saved.hidden_three,
+        hidden_two=saved.hidden_two,
+        hidden_one=saved.hidden_one,
+        hidden_zero=saved.hidden_zero,
+        queries_out=saved.queries_out,
+        keys_values=saved.keys_values,
+        queries_raw=saved.queries_raw,
+        keys_raw=saved.keys_raw,
+        mixer_saved=saved.mixer_saved,
+        projected=saved.projected,
         **tables,
-        starts=starts,
         **weights,
     )
     hidden_columns = first_gate.shape[1]
@@ -2113,12 +2177,12 @@
     groups = [
         (width // shards // block_rows, 2 * hidden_columns),
         (hidden_columns // shards // block_rows, width),
-        (saved["attended_x"], width),
-        (saved["attend_in_x"], head_columns),
-        (saved["active_x"], width),
-        (saved["first_in_x"], 2 * hidden_columns),
-        (saved["gated_x"], width),
-        (saved["mixer_in_x"], 3 * width),
+        (saved.attended_x, width),
+        (saved.attend_in_x, head_columns),
+        (saved.active_x, width),
+        (saved.first_in_x, 2 * hidden_columns),
+        (saved.gated_x, width),
+        (saved.mixer_in_x, 3 * width),
         (2, COLS),
     ]
     (
@@ -2133,7 +2197,7 @@
         sums,
         token_grad,
         mixed,
-    ) = backward(groups, arrays, tuple(tables) + ("starts",), row_count, shards, 1)
+    ) = backward(groups, arrays, tuple(tables), row_count, shards, 1)
 
     def single(value):
         return value.astype(full)

time: 464 us -> 433 us (0.933)
  Pallas kernels: 433 us -> 413 us
  local copies, waits for them, and re-layouts: 9.9 us -> 2.72 us
    pallas_call x1, Pallas kernels: 378 us -> 367 us  [backward(): pl.pallas_call(kernel, out_shape=[jax.ShapeDtypeStruct((x_count * block_r...]
    pallas_call x1, Pallas kernels: 54.9 us -> 46 us  [forward(): pl.pallas_call(functools.partial(forward_kernel, list(arrays), list(outs)...]
    another operation x10 -> x0, local copies, waits for them, and re-layouts: 4.89 us -> none  [the longest x4 2.74 us: fused_body(): jnp.stack([second_gain, attend_gain, first_gain, mixer_gain])]
where the time goes in v5:
time: 433 us
  Pallas kernels  413 us (95%)
  other arithmetic  16.4 us (4%)
    pallas_call x1, Pallas kernels, backward(): pl.pallas_call(kernel, out_shape=[jax.ShapeDtypeStruct((x_count * block_r...  367 us
    pallas_call x1, Pallas kernels, forward(): pl.pallas_call(functools.partial(forward_kernel, list(arrays), list(outs)...  46 us
    convert_element_type x9, other arithmetic, single(): return value.astype(full)  15.1 us

profile of v5, /device:TPU:0, one launch (start us, length us, event | category | flops | bytes accessed | tf_op | source)
XLA Modules:
  0.0 432.9 jit_solution(2749173727221847014)
XLA Ops:
  0.7 46.0 %shard_map.373 = (f32[256,1024]{1,0:T(8,128)}, f32[256,1024]{1,0:T(8,128)}, f32[256,1024]{1,0:T(8,128)}, f32[256,1024]{1,0:T(8,128)}, bf16[256,4608]{1,0:T(8,128...) custom-call(bf16[256,1024]{1,0:T(8,128)(2,1)} %bitcast.22, ...), custom_call_target="tpu_custom_call" | custom-call | flops 11143809024 | bytes 43530504 | tf_op jit(solution)/shard_map/pallas_call | solution.py:1468
  46.6 367.1 %shard_map.374 = (bf16[128,9216]{1,0:T(8,128)(2,1)}, bf16[576,1024]{1,0:T(8,128)(2,1)}, bf16[128,1024]{1,0:T(8,128)(2,1)}, bf16[128,2048]{1,0:T(8,128)(2,1)}, bf...) custom-call(bf16[4,2,2,64,256]{4,3,2,1,0:T(8,128)(2,1)} %get-tuple-e, ...), custom_call_target="tpu_custom_call" | custom-call | flops 37044092928 | bytes 72351744 | tf_op jit(solution)/shard_map/pallas_call | solution.py:2043
  413.8 0.0 copy-start.1
  413.8 6.4 %slice_convert_fusion = (f32[128,4608]{1,0:T(8,128)}, f32[128,4608]{1,0:T(8,128)}, f32[128,4608]{1,0:T(8,128)}, f32[128,4608]{1,0:T(8,128)}) fusion(bf16[128,9216]{1,0:T(8,128)(2,1)} %get-tuple-element.83, bf16[128,9216]{1,0:T(8,128)(2,1)} %get-tuple-element.79), kind=kLoop, calls=%fused_computation | loop fusion | flops 2359296 | bytes 14155776 | tf_op jit(solution)/shard_map/convert_element_type | solution.py:2203
  420.2 0.0 copy-start
  420.2 0.0 copy-done.1
  420.2 1.7 convert_element_type.46
  421.9 0.0 copy-start.2
  421.9 0.0 copy-done
  421.9 0.0 copy-start.3
  421.9 1.7 convert_element_type.53
  423.6 0.0 copy-start.7
  423.6 0.0 copy-start.6
  423.6 0.0 copy-done.2
  423.6 0.0 copy-start.5
  423.6 1.3 convert_element_type.42
  424.9 0.0 copy-start.4
  424.9 0.0 copy-done.3
  424.9 0.8 slice_convert_fusion.5
  425.8 0.0 copy-done.7
  425.8 0.8 convert_element_type.43
  426.6 0.0 copy-done.6
  426.6 0.8 convert_element_type.50
  427.5 0.8 slice_convert_fusion.4
  428.3 0.6 dynamic-slice_convert_fusion
  429.0 0.5 slice_bitcast_fusion
  429.5 0.6 slice.37
  430.1 1.3 fusion.3
  431.3 0.0 copy-done.5
  431.3 0.8 copy.45
  432.1 0.0 copy-done.4
  432.1 0.8 copy.46
Async XLA Ops:
  413.8 6.5 %copy-start.1 = (bf16[576,1024]{1,0:T(8,128)(2,1)S(1)}, bf16[576,1024]{1,0:T(8,128)(2,1)}, u32[]{:S(2)}) copy-start(bf16[576,1024]{1,0:T(8,128)(2,1)} %get-tuple-element.80) | copy-start | bytes 3538948
  420.2 1.7 copy-start
  421.9 1.7 copy-start.2
  421.9 3.0 copy-start.3
  423.6 2.2 copy-start.7
  423.6 3.0 copy-start.6
  423.6 7.7 %copy-start.5 = (bf16[256,1024]{1,0:T(8,128)(2,1)S(1)}, bf16[256,1024]{1,0:T(8,128)(2,1)}, u32[]{:S(2)}) copy-start(bf16[256,1024]{1,0:T(8,128)(2,1)} %get-tuple-element.74) | copy-start | bytes 1572868
  424.9 7.2 %copy-start.4 = (bf16[256,1024]{1,0:T(8,128)(2,1)S(1)}, bf16[256,1024]{1,0:T(8,128)(2,1)}, u32[]{:S(2)}) copy-start(bf16[256,1024]{1,0:T(8,128)(2,1)} %get-tuple-element.75) | copy-start | bytes 1572868

commit v6 on v5

--- a/solution.py
+++ b/solution.py
@@ -431,6 +431,7 @@
 
 class Exchange:
     def __init__(self, entries, row_count, shards, outs, scratch, locals_at=(), local=None):
+        self.last_rows = None
         self.entries, self.outs = entries, outs
         self.locals_at, self.local = locals_at, local
         self.bits = bits = shards.bit_length() - 1
@@ -487,15 +488,42 @@
             preferred_element_type=jnp.float32,
         )
 
-    def seq_copy(self, kind, step, slot):
+    def sized(self, kind, index, act):
+        if self.last_rows is None or kind == 1:
+            act(None)
+        else:
+            pl.when(index < self.pairs - 1)(lambda: act(None))
+            pl.when(index == self.pairs - 1)(lambda: act(self.last_rows))
+
+    def seq_start(self, kind, step, slot, index):
+        self.sized(kind, index, lambda rows: self.seq_copy(kind, step, slot, rows).start())
+
+    def seq_wait(self, kind, step, slot, index):
+        self.sized(kind, index, lambda rows: self.seq_copy(kind, step, slot, rows).wait())
+
+    def z_start(self, kind, step, slot, index):
+        self.sized(kind, index, lambda rows: self.z_copy(kind, step, slot, rows).start())
+
+    def z_wait(self, kind, step, slot, index):
+        self.sized(kind, index, lambda rows: self.z_copy(kind, step, slot, rows).wait())
+
+    def z_wait_recv(self, kind, step, slot, index):
+        self.sized(kind, index, lambda rows: self.z_copy(kind, step, slot, rows).wait_recv())
+
+    def z_wait_send(self, kind, step, slot, index):
+        self.sized(kind, index, lambda rows: self.z_copy(kind, step, slot, rows).wait_send())
+
+    def seq_copy(self, kind, step, slot, rows):
+        some = pl.ds(0, self.z_own.shape[2] if rows is None else rows)
         if step == 0:
             bit = 0
-            source = self.send_zero.at[kind, lax.rem(slot, 2)]
-            target = self.recv_zero.at[kind, slot]
+            source = self.send_zero.at[kind, lax.rem(slot, 2), :, some]
+            target = self.recv_zero.at[kind, slot, :, some]
         else:
             bit = self.kinds[kind][step - 1][0]
-            source = self.held[kind][step - 1].at[lax.rem(slot, 2), :, 1 - self.value[bit]]
-            target = self.received[kind][step - 1].at[slot]
+            away = 1 - self.value[bit]
+            source = self.held[kind][step - 1].at[lax.rem(slot, 2), :, away, :, some]
+            target = self.received[kind][step - 1].at[slot, :, :, some]
         return pltpu.make_async_remote_copy(
             src_ref=source,
             dst_ref=target,
@@ -510,7 +538,8 @@
         mine = self.held[kind][step - 2][lax.rem(slot, 2), :, self.value[bit]].astype(jnp.float32)
         return mine + self.received[kind][step - 2][slot].astype(jnp.float32)
 
-    def z_copy(self, kind, step, slot):
+    def z_copy(self, kind, step, slot, rows):
+        some = pl.ds(0, self.z_own.shape[2] if rows is None else rows)
         if step < self.depth:
             source = self.z_own if step == 0 else self.z_part
             target, where = self.z_in, self.toward
@@ -520,8 +549,8 @@
         else:
             source, target, where = self.z_total, self.z_total, self.away
         return pltpu.make_async_remote_copy(
-            src_ref=source.at[kind, slot],
-            dst_ref=target.at[kind, slot],
+            src_ref=source.at[kind, slot, some],
+            dst_ref=target.at[kind, slot, some],
             send_sem=self.z_send.at[kind, step, slot],
             recv_sem=self.z_recv.at[kind, step, slot],
             device_id=(where, self.seq),
@@ -564,11 +593,11 @@
             def _():
                 target[kind, lax.rem(slot, 2)] = self.local.part(kind, index, 1 - self.value[0])
 
-        self.seq_copy(kind, 0, slot).start()
+        self.seq_start(kind, 0, slot, index)
 
     def second(self, kind, index):
         slot = lax.rem(index, SLOTS)
-        self.seq_copy(kind, 0, slot).wait()
+        self.seq_wait(kind, 0, slot, index)
         target = self.held[kind][0]
 
         def put():
@@ -587,22 +616,22 @@
                 total = mine + self.recv_zero[kind, slot].astype(jnp.float32)
                 target[lax.rem(slot, 2)] = total.astype(jnp.bfloat16).reshape(target.shape[1:])
 
-        self.seq_copy(kind, 1, slot).start()
+        self.seq_start(kind, 1, slot, index)
 
     def middle(self, step):
         def run(kind, index):
             slot = lax.rem(index, SLOTS)
-            self.seq_copy(kind, step - 1, slot).wait()
+            self.seq_wait(kind, step - 1, slot, index)
             total = self.seq_sum(kind, step, slot)
             target = self.held[kind][step - 1]
             target[lax.rem(slot, 2)] = total.astype(jnp.bfloat16).reshape(target.shape[1:])
-            self.seq_copy(kind, step, slot).start()
+            self.seq_start(kind, step, slot, index)
 
         return run
 
     def last(self, kind, index):
         slot, z_slot = lax.rem(index, SLOTS), lax.rem(index, ZSLOTS)
-        self.seq_copy(kind, self.bits - 1, slot).wait()
+        self.seq_wait(kind, self.bits - 1, slot, index)
         total = self.seq_sum(kind, self.bits, slot).reshape(self.z_own.shape[2:])
 
         def put():
@@ -610,7 +639,7 @@
 
             @pl.when(self.level == 0)
             def _():
-                self.z_copy(kind, 0, z_slot).start()
+                self.z_start(kind, 0, z_slot, index)
 
         if self.local is None:
             put()
@@ -630,29 +659,29 @@
 
                 @pl.when(level == step)
                 def _():
-                    self.z_copy(kind, step - 1, slot).wait_recv()
+                    self.z_wait_recv(kind, step - 1, slot, index)
                     self.z_part[kind, slot] = (
                         self.z_own[kind, slot].astype(jnp.float32)
                         + self.z_in[kind, slot].astype(jnp.float32)
                     ).astype(jnp.bfloat16)
-                    self.z_copy(kind, step, slot).start()
+                    self.z_start(kind, step, slot, index)
 
                 @pl.when(level == step - 1)
                 def _():
-                    self.z_copy(kind, step - 1, slot).wait_send()
+                    self.z_wait_send(kind, step - 1, slot, index)
 
             elif step == depth + 1:
 
                 @pl.when(level == depth)
                 def _():
-                    self.z_copy(kind, depth, slot).wait()
+                    self.z_wait(kind, depth, slot, index)
                     own = self.z_own if depth == 0 else self.z_part
                     self.z_total[kind, slot] = (
                         own[kind, slot].astype(jnp.float32)
                         + self.z_cross[kind, slot].astype(jnp.float32)
                     ).astype(jnp.bfloat16)
                     if depth > 0:
-                        self.z_copy(kind, step, slot).start()
+                        self.z_start(kind, step, slot, index)
                     self.start_out(kind, slot, index)
 
             else:
@@ -660,14 +689,14 @@
 
                 @pl.when(level == receiver)
                 def _():
-                    self.z_copy(kind, step - 1, slot).wait_recv()
+                    self.z_wait_recv(kind, step - 1, slot, index)
                     if receiver > 0:
-                        self.z_copy(kind, step, slot).start()
+                        self.z_start(kind, step, slot, index)
                     self.start_out(kind, slot, index)
 
                 @pl.when(level == receiver + 1)
                 def _():
-                    self.z_copy(kind, step - 1, slot).wait_send()
+                    self.z_wait_send(kind, step - 1, slot, index)
 
         return run
 
@@ -696,8 +725,15 @@
 
                 @pl.when(here)
                 def _():
-                    for kind in range(2):
-                        stage(kind, index)
+                    stage(0, index)
+                    if self.last_rows is None:
+                        stage(1, index)
+
+                if self.last_rows is not None:
+
+                    @pl.when(jnp.logical_and(here, index < self.pairs - 1))
+                    def _():
+                        stage(1, index)
 
             if task is not None:
                 task(i)
@@ -912,6 +948,105 @@
     )
 
 
+def finish_kernel(cuts, count, shards, *refs):
+    passed, sums_in, refs = refs[:2], refs[2], refs[3:]
+    ins, outs = refs[:count], refs[count : count + len(cuts)]
+    refs = refs[count + len(cuts) :]
+    passed_out, vectors, taps_out, heads, refs = refs[:2], refs[2:6], refs[6], refs[7:9], refs[9:]
+    lows, fulls = refs[:count], refs[count : count + len(cuts)]
+    held, sums, load_sem, save_sem, pass_sem = refs[count + len(cuts) :]
+    moves = [
+        pltpu.make_async_copy(source, held.at[number], pass_sem.at[number])
+        for number, source in enumerate(passed)
+    ]
+    moves.append(pltpu.make_async_copy(sums_in, sums, pass_sem.at[2]))
+    loads = [
+        pltpu.make_async_copy(ins[number], lows[number], load_sem.at[number])
+        for number in range(count)
+    ]
+    for load in loads + moves:
+        load.start()
+    saves, waited = [], set()
+    for number, (source, first, columns) in enumerate(cuts):
+        if source not in waited:
+            loads[source].wait()
+            waited.add(source)
+        low, full = lows[source], fulls[number]
+        rows = low.shape[0]
+        piece = 64 if rows % 64 == 0 else rows
+
+        def convert(at, carried):
+            span = pl.ds(pl.multiple_of(at * 16, 16), 16)
+            full[span] = low[span, pl.ds(first, columns)].astype(jnp.float32)
+            return carried
+
+        for start in range(0, rows, piece):
+            lax.fori_loop(start // 16, (start + piece) // 16, convert, 0)
+            span = pl.ds(start, piece)
+            save = pltpu.make_async_copy(
+                full.at[span], outs[number].at[span], save_sem.at[len(saves)]
+            )
+            save.start()
+            saves.append(save)
+    for move in moves:
+        move.wait()
+    for number, target in enumerate(passed_out):
+        save = pltpu.make_async_copy(held.at[number], target, pass_sem.at[number])
+        save.start()
+        saves.append(save)
+    seq = lax.axis_index("seq")
+    share = vectors[0].shape[0]
+    value = sums[pl.ds(0, 16)].astype(jnp.float32)
+    chosen = jnp.zeros((16, share), jnp.float32)
+    for place in range(COLS // share):
+        here = lax.rem(seq, COLS // share) == place
+        chosen = jnp.where(here, value[:, place * share : (place + 1) * share], chosen)
+    for number, vector in enumerate(vectors):
+        vector[...] = chosen[number : number + 1].reshape(share)
+    taps_out[...] = chosen[4:7]
+    lane = 2 * HEAD_DIM
+    for number, head in enumerate(heads):
+        line = value[0:8, number * lane : (number + 1) * lane]
+        part = head.shape[0]
+        chosen = jnp.zeros((1, part), jnp.float32)
+        for place in range(shards):
+            chosen = jnp.where(seq == place, line[7:8, place * part : (place + 1) * part], chosen)
+        head[...] = chosen.reshape(part)
+    for save in saves:
+        save.wait()
+
+
+def to_full(passed, sums, lows, cuts, shards):
+    any_space = pl.BlockSpec(memory_space=pl.ANY)
+    shapes = [(lows[source].shape[0], columns) for source, _, columns in cuts]
+    pieces = sum(rows // 64 if rows % 64 == 0 else 1 for rows, _ in shapes)
+    size = sum(low.size for low in lows)
+    width = passed[0].shape[1]
+    small = [(width // shards,)] * 4 + [(3, width // shards)] + [(HEAD_DIM // shards,)] * 2
+    results = pl.pallas_call(
+        functools.partial(finish_kernel, cuts, len(lows), shards),
+        out_shape=[jax.ShapeDtypeStruct(shape, jnp.float32) for shape in shapes]
+        + [jax.ShapeDtypeStruct(value.shape, value.dtype) for value in passed]
+        + [jax.ShapeDtypeStruct(shape, jnp.float32) for shape in small],
+        in_specs=[any_space] * (3 + len(lows)),
+        out_specs=[any_space] * (len(cuts) + 2)
+        + [pl.BlockSpec(memory_space=pltpu.VMEM)] * len(small),
+        scratch_shapes=[
+            *[pltpu.VMEM(low.shape, low.dtype) for low in lows],
+            *[pltpu.VMEM(shape, jnp.float32) for shape in shapes],
+            pltpu.VMEM((2,) + passed[0].shape, passed[0].dtype),
+            pltpu.VMEM(sums.shape, sums.dtype),
+            pltpu.SemaphoreType.DMA((len(lows),)),
+            pltpu.SemaphoreType.DMA((pieces,)),
+            pltpu.SemaphoreType.DMA((3,)),
+        ],
+        compiler_params=pltpu.CompilerParams(vmem_limit_bytes=62 * 2**20),
+        cost_estimate=pl.CostEstimate(flops=size, bytes_accessed=6 * size, transcendentals=0),
+    )(*passed, sums, *lows)
+    cut_count = len(cuts)
+    return results[:cut_count], results[cut_count : cut_count + 2], results[cut_count + 2 :]
+
+
 def dot_nt(left, right):
     return lax.dot_general(
         left, right, (((1,), (1,)), ((), ())), preferred_element_type=jnp.float32
@@ -1033,9 +1168,12 @@
 
     saves = []
 
+    streaming = [True]
+
     def save(source, target):
         copy = pltpu.make_async_copy(source, target, at.save_sem.at[len(saves)])
-        copy.start()
+        if not streaming[0]:
+            copy.start()
         saves.append(copy)
 
     def normed(hidden, number, target):
@@ -1252,6 +1390,9 @@
     near_one, far_zero = send(2, piece(seq, 1), 1), send(3, piece(seq, 0), 2)
     twin = send(4, piece(seq), 0)
     for copy in (near_zero, far_one, near_one, far_zero, twin):
+        copy.start()
+    streaming[0] = False
+    for copy in saves:
         copy.start()
 
     slot = begin(keys_at + 1)
@@ -1528,6 +1669,7 @@
     ) = scratch
     local = types.SimpleNamespace()
     exchange = Exchange(entries, row_count, shards, outs, scratch, LOCAL_PAIRS, local)
+    exchange.last_rows = 16
     x_all, g_all = exchange.x_all, exchange.g_all
     seq, row = exchange.seq, exchange.row
     tokens, width = gradient.shape
@@ -2199,41 +2341,65 @@
         mixed,
     ) = backward(groups, arrays, tuple(tables), row_count, shards, 1)
 
-    def single(value):
-        return value.astype(full)
-
-    share = width // shards
-    vectors = single(
-        lax.dynamic_slice(sums, (0, lax.rem(seq, COLS // share) * share), (7, share))
-    )
-    head_share = HEAD_DIM // shards
-    heads = [
-        single(lax.dynamic_slice(sums, (7, which * lane + seq * head_share), (1, head_share)))[0]
-        for which in range(2)
-    ]
     key_columns = key_weight.shape[1]
+    lows = [second_both, first_both, grad_second_down, grad_first_down]
+    lows += [attend_three, grad_attend_output, grad_mixer_output, grad_mixer_input]
+    fulls, (mixed, token_grad), small = to_full(
+        (mixed, token_grad),
+        sums,
+        lows,
+        (
+            (0, 0, hidden_columns),
+            (0, hidden_columns, hidden_columns),
+            (1, 0, hidden_columns),
+            (1, hidden_columns, hidden_columns),
+            (2, 0, width),
+            (3, 0, width),
+            (4, 0, width),
+            (4, width, key_columns),
+            (4, width + key_columns, key_columns),
+            (5, 0, width),
+            (6, 0, width),
+            (7, 0, 3 * width),
+        ),
+        shards,
+    )
+    (
+        second_gate_full,
+        second_up_full,
+        first_gate_full,
+        first_up_full,
+        second_down_full,
+        first_down_full,
+        query_full,
+        key_full,
+        value_full,
+        attend_output_full,
+        mixer_output_full,
+        mixer_input_full,
+    ) = fulls
     return (
         mixed.reshape(tokens.shape),
         token_grad.reshape(tokens.shape),
-        vectors[3],
-        single(grad_mixer_input),
-        vectors[4:7],
-        single(grad_mixer_output),
-        vectors[2],
-        single(first_both[:, :hidden_columns]),
-        single(first_both[:, hidden_columns:]),
-        single(grad_first_down),
-        vectors[1],
-        single(attend_three[:, :width]),
-        single(attend_three[:, width : width + key_columns]),
-        single(attend_three[:, width + key_columns :]),
-        heads[0],
-        heads[1],
-        single(grad_attend_output),
-        vectors[0],
-        single(second_both[:, :hidden_columns]),
-        single(second_both[:, hidden_columns:]),
-        single(grad_second_down),
+        small[3],
+        mixer_input_full,
+        small[4],
+        mixer_output_full,
+        small[2],
+        first_gate_full,
+        first_up_full,
+        first_down_full,
+        small[1],
+        query_full,
+        key_full,
+        value_full,
+        small[5],
+        small[6],
+        attend_output_full,
+        small[0],
+        second_gate_full,
+        second_up_full,
+        second_down_full,
     )
 
 

time: 433 us -> 423 us (0.977)
  other arithmetic: 16.4 us -> 0 us
  Pallas kernels: 413 us -> 422 us
    convert_element_type x9 -> x0, other arithmetic: 15.1 us -> none  [single(): return value.astype(full)]
    pallas_call x0 -> x1, Pallas kernels: none -> 10.1 us  [to_full(): pl.pallas_call(functools.partial(finish_kernel, cuts, len(lows), shards),...]
where the time goes in v6:
time: 423 us
  Pallas kernels  422 us (100%)
    pallas_call x1, Pallas kernels, backward(): pl.pallas_call(kernel, out_shape=[jax.ShapeDtypeStruct((x_count * block_r...  366 us
    pallas_call x1, Pallas kernels, forward(): pl.pallas_call(functools.partial(forward_kernel, list(arrays), list(outs)...  45.5 us
    pallas_call x1, Pallas kernels, to_full(): pl.pallas_call(functools.partial(finish_kernel, cuts, len(lows), shards),...  10.1 us

profile of v6, /device:TPU:0, one launch (start us, length us, event | category | flops | bytes accessed | tf_op | source)
XLA Modules:
  0.0 422.8 jit_solution(11034022304763225954)
XLA Ops:
  0.7 45.5 %shard_map.373 = (f32[256,1024]{1,0:T(8,128)}, f32[256,1024]{1,0:T(8,128)}, f32[256,1024]{1,0:T(8,128)}, f32[256,1024]{1,0:T(8,128)}, bf16[256,4608]{1,0:T(8,128...) custom-call(bf16[256,1024]{1,0:T(8,128)(2,1)} %bitcast.4, ...), custom_call_target="tpu_custom_call" | custom-call | flops 11143809024 | bytes 43530504 | tf_op jit(solution)/shard_map/pallas_call | solution.py:1609
  46.2 366.3 %shard_map.374 = (bf16[128,9216]{1,0:T(8,128)(2,1)}, bf16[576,1024]{1,0:T(8,128)(2,1)}, bf16[128,1024]{1,0:T(8,128)(2,1)}, bf16[128,2048]{1,0:T(8,128)(2,1)}, bf...) custom-call(bf16[4,2,2,64,256]{4,3,2,1,0:T(8,128)(2,1)} %get-tuple-e, ...), custom_call_target="tpu_custom_call" | custom-call | flops 37044092928 | bytes 72351744 | tf_op jit(solution)/shard_map/pallas_call | solution.py:2185
  412.5 10.1 %shard_map.375 = (f32[128,4608]{1,0:T(8,128)}, f32[128,4608]{1,0:T(8,128)}, f32[128,4608]{1,0:T(8,128)}, f32[128,4608]{1,0:T(8,128)}, f32[576,1024]{1,0:T(8,128)...) custom-call(bf16[256,1024]{1,0:T(8,128)(2,1)} %get-tuple-element.95., ...), custom_call_target="tpu_custom_call" | custom-call | flops 4456448 | bytes 26738688 | tf_op jit(solution)/shard_map/pallas_call | solution.py:1026

commit v7 on v6

--- a/solution.py
+++ b/solution.py
@@ -414,13 +414,17 @@
             comm.append(pltpu.VMEM((2, above, 2, below) + block, jnp.bfloat16))
             comm.append(pltpu.VMEM((SLOTS, above, below) + block, jnp.bfloat16))
     z_steps = row_count - 1
+    own_slots = 3 if row_count <= 4 else ZSLOTS
     return [
         pltpu.VMEM((shards // 2, 2, x_blocks, block_rows, tokens), jnp.bfloat16),
         pltpu.VMEM((tokens, g_blocks * COLS), jnp.bfloat16),
         pltpu.VMEM((2, 2, shards // 2) + block, jnp.bfloat16),
         pltpu.VMEM((2, SLOTS, shards // 2) + block, jnp.bfloat16),
         *comm,
-        *[pltpu.VMEM((2, ZSLOTS) + block, jnp.bfloat16) for _ in range(5)],
+        *[
+            pltpu.VMEM((2, count) + block, jnp.bfloat16)
+            for count in (own_slots, ZSLOTS, own_slots, ZSLOTS, ZSLOTS)
+        ],
         pltpu.SemaphoreType.DMA((2, bits, SLOTS)),
         pltpu.SemaphoreType.DMA((2, bits, SLOTS)),
         pltpu.SemaphoreType.DMA((2, z_steps, ZSLOTS)),
@@ -431,7 +435,7 @@
 
 class Exchange:
     def __init__(self, entries, row_count, shards, outs, scratch, locals_at=(), local=None):
-        self.last_rows = None
+        self.last_rows, self.fold = None, None
         self.entries, self.outs = entries, outs
         self.locals_at, self.local = locals_at, local
         self.bits = bits = shards.bit_length() - 1
@@ -464,6 +468,8 @@
             others.append((lax.rem(self.row + step, self.row_count), self.seq))
         for step in (1, self.shards - 1):
             others.append((self.row, lax.rem(self.seq + step, self.shards)))
+        if self.fold is not None:
+            others.append((self.fold.far, self.seq))
         for other in others:
             pl.semaphore_signal(barrier, inc=1, device_id=other, device_id_type=MESH)
         pl.semaphore_wait(barrier, len(others))
@@ -494,6 +500,9 @@
         else:
             pl.when(index < self.pairs - 1)(lambda: act(None))
             pl.when(index == self.pairs - 1)(lambda: act(self.last_rows))
+
+    def own_slot(self, slot):
+        return lax.rem(slot, self.z_own.shape[1])
 
     def seq_start(self, kind, step, slot, index):
         self.sized(kind, index, lambda rows: self.seq_copy(kind, step, slot, rows).start())
@@ -549,7 +558,7 @@
         else:
             source, target, where = self.z_total, self.z_total, self.away
         return pltpu.make_async_remote_copy(
-            src_ref=source.at[kind, slot, some],
+            src_ref=source.at[kind, slot if source is self.z_total else self.own_slot(slot), some],
             dst_ref=target.at[kind, slot, some],
             send_sem=self.z_send.at[kind, step, slot],
             recv_sem=self.z_recv.at[kind, step, slot],
@@ -635,7 +644,7 @@
         total = self.seq_sum(kind, self.bits, slot).reshape(self.z_own.shape[2:])
 
         def put():
-            self.z_own[kind, z_slot] = total.astype(jnp.bfloat16)
+            self.z_own[kind, self.own_slot(z_slot)] = total.astype(jnp.bfloat16)
 
             @pl.when(self.level == 0)
             def _():
@@ -660,8 +669,8 @@
                 @pl.when(level == step)
                 def _():
                     self.z_wait_recv(kind, step - 1, slot, index)
-                    self.z_part[kind, slot] = (
-                        self.z_own[kind, slot].astype(jnp.float32)
+                    self.z_part[kind, self.own_slot(slot)] = (
+                        self.z_own[kind, self.own_slot(slot)].astype(jnp.float32)
                         + self.z_in[kind, slot].astype(jnp.float32)
                     ).astype(jnp.bfloat16)
                     self.z_start(kind, step, slot, index)
@@ -677,7 +686,7 @@
                     self.z_wait(kind, depth, slot, index)
                     own = self.z_own if depth == 0 else self.z_part
                     self.z_total[kind, slot] = (
-                        own[kind, slot].astype(jnp.float32)
+                        own[kind, self.own_slot(slot)].astype(jnp.float32)
                         + self.z_cross[kind, slot].astype(jnp.float32)
                     ).astype(jnp.bfloat16)
                     if depth > 0:
@@ -735,11 +744,204 @@
                     def _():
                         stage(1, index)
 
+            if self.fold is not None:
+                self.fold.advance(i)
             if task is not None:
                 task(i)
             return carried
 
-        lax.fori_loop(0, self.pairs + len(stages) - 1, iteration, 0)
+        total = self.pairs + len(stages) - 1
+        if self.fold is not None:
+            total = max(total, self.fold.end)
+        lax.fori_loop(0, total, iteration, 0)
+
+
+FOLD_START, FOLD_PERIOD = 8, 3
+
+
+def fold_scratch(shards, block_rows):
+    half = (block_rows // 2, COLS)
+    low = jnp.bfloat16
+    orders = []
+    for steps in seq_steps(shards.bit_length() - 1):
+        for _, above, below in steps:
+            orders.append(pltpu.VMEM((above, 2, below) + half, low))
+            orders.append(pltpu.VMEM((2, above, below) + half, low))
+    return [
+        pltpu.VMEM((shards // 2, block_rows, COLS), low),
+        pltpu.VMEM((2, shards // 2, block_rows, COLS), low),
+        pltpu.VMEM((shards // 2, 2) + half, low),
+        pltpu.VMEM((2, shards // 2) + half, low),
+        *orders,
+        pltpu.VMEM(half, low),
+        pltpu.VMEM((3,) + half, low),
+        pltpu.VMEM((3, 2) + half, low),
+        pltpu.SemaphoreType.DMA((6, 3)),
+        pltpu.SemaphoreType.DMA((6, 3)),
+        pltpu.SemaphoreType.DMA((2, 3)),
+    ]
+
+
+class Fold:
+    def __init__(self, exchange, entry, out, scratch):
+        self.exchange, self.entry, self.out = exchange, entry, out
+        (self.send, self.received, self.halves, self.half_in, *rest) = scratch
+        self.held, self.held_in = [[], []], [[], []]
+        for order in range(2):
+            for _ in exchange.kinds[order]:
+                self.held[order].append(rest.pop(0))
+                self.held_in[order].append(rest.pop(0))
+        self.own, self.cross, self.total, self.send_sem, self.recv_sem, self.out_sem = rest
+        row = exchange.row
+        self.bit = lax.rem(row, 2)
+        self.near, self.far = row + 1 - 2 * self.bit, lax.rem(row + 2, 4)
+        self.count = entry[1] * entry[3]
+        self.stages = [
+            (0, self.first),
+            (1, self.second),
+            (3, self.third),
+            (4, self.fourth),
+            (5, self.fifth),
+            (7, self.sixth),
+            (9, self.seventh),
+            (10, self.finish),
+        ]
+        self.end = FOLD_START + FOLD_PERIOD * (self.count - 1) + 11
+
+    def advance(self, i):
+        for offset, run in self.stages:
+            since = i - (FOLD_START + offset)
+            number = jnp.maximum(since, 0) // FOLD_PERIOD
+            here = jnp.logical_and(since >= 0, lax.rem(jnp.maximum(since, 0), FOLD_PERIOD) == 0)
+            here = jnp.logical_and(here, number < self.count)
+
+            @pl.when(here)
+            def _():
+                run(number)
+
+    def copy(self, step, number, order=0):
+        exchange = self.exchange
+        row, seq, two, three = exchange.row, exchange.seq, lax.rem(number, 2), lax.rem(number, 3)
+        if step == 0:
+            source, target = self.send, self.received.at[two]
+            device = (row, exchange.partner[0])
+        elif step == 1:
+            source, target = self.halves.at[:, 1 - self.bit], self.half_in.at[two]
+            device = (self.near, seq)
+        elif step < 4:
+            bit = exchange.kinds[order][step - 2][0]
+            source = self.held[order][step - 2].at[:, 1 - exchange.value[bit]]
+            target = self.held_in[order][step - 2].at[lax.rem(number // 2, 2)]
+            device = (row, exchange.partner[bit])
+        elif step == 4:
+            source, target = self.own, self.cross.at[three]
+            device = (self.far, seq)
+        else:
+            source = target = self.total.at[three, self.bit]
+            device = (self.near, seq)
+        return pltpu.make_async_remote_copy(
+            src_ref=source,
+            dst_ref=target,
+            send_sem=self.send_sem.at[step, three],
+            recv_sem=self.recv_sem.at[step, three],
+            device_id=device,
+            device_id_type=MESH,
+        )
+
+    def product(self, number, side):
+        x_first, x_count, g_first = self.entry[:3]
+        left = self.exchange.x_all[:, side, x_first + lax.rem(number, x_count)]
+        columns = pl.ds(pl.multiple_of((g_first + number // x_count) * COLS, COLS), COLS)
+        return jnp.dot(
+            left.reshape(left.shape[0] * left.shape[1], left.shape[2]),
+            self.exchange.g_all[:, columns],
+            preferred_element_type=jnp.float32,
+        )
+
+    def first(self, number):
+        value = self.product(number, 1 - self.exchange.value[0]).astype(jnp.bfloat16)
+        self.send[...] = value.reshape(self.send.shape)
+        self.copy(0, number).start()
+
+    def second(self, number):
+        self.copy(0, number).wait()
+        mine = self.product(number, self.exchange.value[0])
+        other = self.received[lax.rem(number, 2)].astype(jnp.float32)
+        total = mine + other.reshape(mine.shape)
+        self.halves[...] = total.astype(jnp.bfloat16).reshape(self.halves.shape)
+        self.copy(1, number).start()
+
+    def by_order(self, number, run):
+        for order in range(2):
+            pl.when(lax.rem(number, 2) == order)(functools.partial(run, order))
+
+    def third(self, number):
+        self.copy(1, number).wait()
+        total = self.halves[:, self.bit].astype(jnp.float32)
+        total = total + self.half_in[lax.rem(number, 2)].astype(jnp.float32)
+        total = total.astype(jnp.bfloat16)
+
+        def go(order):
+            target = self.held[order][0]
+            target[...] = total.reshape(target.shape)
+            self.copy(2, number, order).start()
+
+        self.by_order(number, go)
+
+    def summed(self, number, order, step):
+        bit = self.exchange.kinds[order][step][0]
+        mine = self.held[order][step][:, self.exchange.value[bit]].astype(jnp.float32)
+        other = self.held_in[order][step][lax.rem(number // 2, 2)].astype(jnp.float32)
+        return (mine + other).astype(jnp.bfloat16)
+
+    def fourth(self, number):
+        def go(order):
+            self.copy(2, number, order).wait()
+            target = self.held[order][1]
+            target[...] = self.summed(number, order, 0).reshape(target.shape)
+            self.copy(3, number, order).start()
+
+        self.by_order(number, go)
+
+    def fifth(self, number):
+        def go(order):
+            self.copy(3, number, order).wait()
+            self.own[...] = self.summed(number, order, 1).reshape(self.own.shape)
+
+        self.by_order(number, go)
+        self.copy(4, number).start()
+
+    def sixth(self, number):
+        self.copy(4, number).wait()
+        three = lax.rem(number, 3)
+        total = self.own[...].astype(jnp.float32) + self.cross[three].astype(jnp.float32)
+        self.total[three, self.bit] = total.astype(jnp.bfloat16)
+        self.copy(5, number).start()
+
+    def out_copies(self, number):
+        x_count, rows = self.entry[1], self.own.shape[0]
+        three = lax.rem(number, 3)
+        columns = pl.ds(pl.multiple_of(number // x_count * COLS, COLS), COLS)
+        copies = []
+        for half in range(2):
+            at = pl.multiple_of((2 * lax.rem(number, x_count) + half) * rows, rows)
+            copies.append(
+                pltpu.make_async_copy(
+                    self.total.at[three, half],
+                    self.out.at[pl.ds(at, rows), columns],
+                    self.out_sem.at[half, three],
+                )
+            )
+        return copies
+
+    def seventh(self, number):
+        self.copy(5, number).wait()
+        for copy in self.out_copies(number):
+            copy.start()
+
+    def finish(self, number):
+        for copy in self.out_copies(number):
+            copy.wait()
 
 
 def reduce_kernel(entries, row_count, shards, *refs):
@@ -1627,15 +1829,16 @@
     SECOND: 0,
     ATTEND_OUTPUT: 8,
     ATTENTION: 10,
-    QUERIES: 26,
-    KEYS: 31,
-    FIRST: 32,
-    MIXER_OUTPUT: 41,
-    HALO: 43,
-    MIXER_INPUT: 44,
-    CLOSE: 47,
+    QUERIES: 18,
+    KEYS: 23,
+    FIRST: 24,
+    MIXER_OUTPUT: 33,
+    HALO: 35,
+    MIXER_INPUT: 36,
+    CLOSE: 39,
 }
-LOCAL_PAIRS = (18, 19, 26, 27)
+FOLDED = 1
+LOCAL_PAIRS = (14, 15, 18, 19)
 
 
 def backward_kernel(names, entries, row_count, shards, *refs):
@@ -1668,8 +1871,17 @@
         *scratch,
     ) = scratch
     local = types.SimpleNamespace()
-    exchange = Exchange(entries, row_count, shards, outs, scratch, LOCAL_PAIRS, local)
+    plain, chunk = [], 0
+    for number, entry in enumerate(entries):
+        if number != FOLDED:
+            plain.append(entry[:4] + (chunk,))
+            chunk += entry[1] * entry[3]
+    plain_outs = [out for number, out in enumerate(outs) if number != FOLDED]
+    fold_count = len(fold_scratch(shards, 2))
+    fold_refs, scratch = scratch[:fold_count], scratch[fold_count:]
+    exchange = Exchange(plain, row_count, shards, plain_outs, scratch, LOCAL_PAIRS, local)
     exchange.last_rows = 16
+    exchange.fold = Fold(exchange, entries[FOLDED], outs[FOLDED], fold_refs)
     x_all, g_all = exchange.x_all, exchange.g_all
     seq, row = exchange.seq, exchange.row
     tokens, width = gradient.shape
@@ -2083,9 +2295,11 @@
         when(ATTENTION, staged_free)
 
         def attention(j):
-            attention_head(j // KV_HEADS, lax.rem(j, KV_HEADS))
-
-        when(ATTENTION, attention, 0, rows * KV_HEADS)
+            pairs = KV_HEADS // 2
+            for which in range(2):
+                attention_head(j // pairs, 2 * lax.rem(j, pairs) + which)
+
+        when(ATTENTION, attention, 0, rows * KV_HEADS // 2)
 
         def to_queries(j):
             raw_load.wait()
@@ -2213,6 +2427,7 @@
             pltpu.SemaphoreType.DMA((2, 5)),
             pltpu.SemaphoreType.DMA((len(entries) + 10,)),
             pltpu.SemaphoreType.DMA((2,)),
+            *fold_scratch(shards, block_rows),
             *exchange_scratch(row_count, shards, block_rows, x_blocks, g_blocks, tokens),
         ],
         compiler_params=pltpu.CompilerParams(

time: 423 us -> 399 us (0.943)
  Pallas kernels: 422 us -> 398 us
    pallas_call x1, Pallas kernels: 366 us -> 342 us  [backward(): pl.pallas_call(kernel, out_shape=[jax.ShapeDtypeStruct((x_count * block_r...]
where the time goes in v7:
time: 399 us
  Pallas kernels  398 us (100%)
    pallas_call x1, Pallas kernels, backward(): pl.pallas_call(kernel, out_shape=[jax.ShapeDtypeStruct((x_count * block_r...  342 us
    pallas_call x1, Pallas kernels, forward(): pl.pallas_call(functools.partial(forward_kernel, list(arrays), list(outs)...  45.5 us
    pallas_call x1, Pallas kernels, to_full(): pl.pallas_call(functools.partial(finish_kernel, cuts, len(lows), shards),...  10.1 us

profile of v7, /device:TPU:0, one launch (start us, length us, event | category | flops | bytes accessed | tf_op | source)
XLA Modules:
  0.0 398.5 jit_solution(15389071303108126992)
XLA Ops:
  0.7 45.5 %shard_map.373 = (f32[256,1024]{1,0:T(8,128)}, f32[256,1024]{1,0:T(8,128)}, f32[256,1024]{1,0:T(8,128)}, f32[256,1024]{1,0:T(8,128)}, bf16[256,4608]{1,0:T(8,128...) custom-call(bf16[256,1024]{1,0:T(8,128)(2,1)} %bitcast.4, ...), custom_call_target="tpu_custom_call" | custom-call | flops 11143809024 | bytes 43530504 | tf_op jit(solution)/shard_map/pallas_call | solution.py:1811
  46.2 342.1 %shard_map.374 = (bf16[128,9216]{1,0:T(8,128)(2,1)}, bf16[576,1024]{1,0:T(8,128)(2,1)}, bf16[128,1024]{1,0:T(8,128)(2,1)}, bf16[128,2048]{1,0:T(8,128)(2,1)}, bf...) custom-call(bf16[4,2,2,64,256]{4,3,2,1,0:T(8,128)(2,1)} %get-tuple-e, ...), custom_call_target="tpu_custom_call" | custom-call | flops 37044092928 | bytes 72351744 | tf_op jit(solution)/shard_map/pallas_call | solution.py:2399
  388.3 10.1 %shard_map.375 = (f32[128,4608]{1,0:T(8,128)}, f32[128,4608]{1,0:T(8,128)}, f32[128,4608]{1,0:T(8,128)}, f32[128,4608]{1,0:T(8,128)}, f32[576,1024]{1,0:T(8,128)...) custom-call(bf16[256,1024]{1,0:T(8,128)(2,1)} %get-tuple-element.95., ...), custom_call_target="tpu_custom_call" | custom-call | flops 4456448 | bytes 26738688 | tf_op jit(solution)/shard_map/pallas_call | solution.py:1228

commit v8 on v7

--- a/solution.py
+++ b/solution.py
@@ -1276,6 +1276,10 @@
     return jnp.concatenate(parts, axis=0).astype(jnp.bfloat16)
 
 
+def single_row(lengths, total_length):
+    return jnp.where(lengths[1, 0] == total_length, 1, 0)
+
+
 def segment_start(lengths, which, place):
     end, start = jnp.int32(0), jnp.zeros(place.shape, jnp.int32)
     for number in range(lengths.shape[1]):
@@ -1395,6 +1399,9 @@
         for copy in tile_copies(steps[number], number):
             copy.start()
     at.halo_in[...] = jnp.zeros_like(at.halo_in)
+    half_length = total_length // 2
+    other_half = pl.multiple_of((1 - bits[2]) * half_length, half_length)
+    at.both[1, pl.ds(other_half, half_length)] = jnp.zeros((half_length, width), jnp.bfloat16)
     barrier = pltpu.get_barrier_semaphore()
     others = partner + [lax.rem(seq + step, shards) for step in (1, shards - 1)]
     for other in others:
@@ -1566,11 +1573,16 @@
         odd = jnp.where(first, pltpu.roll(keys, HEAD_DIM, 1), values).astype(jnp.bfloat16)
         for which, value in enumerate((even, odd)):
             columns = pl.ds((2 * pair + which) * lane, lane)
-            at.both[:, own, columns] = value.reshape(rows, length, lane)
-
-    def piece(owner, which=None):
+            at.own_both[:, :, columns] = value.reshape(rows, length, lane)
+
+    single = single_row(at.lengths, total_length)
+    row_of = (single, 1 - single)
+    for place in range(rows):
+        at.both[place, own] = at.own_both[row_of[place]]
+
+    def piece(owner, place):
         span = pl.ds(pl.multiple_of(owner * length, length), length)
-        return at.both.at[:, span] if which is None else at.both.at[which, span]
+        return at.both.at[place, span] if place is not None else at.both.at[:, span]
 
     def send(number, part, bit):
         return pltpu.make_async_remote_copy(
@@ -1582,16 +1594,11 @@
             device_id_type=MESH,
         )
 
-    def flip(owner, bit):
-        value = lax.rem(owner // (1 << bit), 2)
-        return owner + (1 << bit) * (1 - 2 * value)
-
     across, along = partner[1], partner[2]
-    corner = flip(across, 2)
-    near_zero, far_one = send(0, piece(seq, 0), 1), send(1, piece(seq, 1), 2)
-    near_one, far_zero = send(2, piece(seq, 1), 1), send(3, piece(seq, 0), 2)
-    twin = send(4, piece(seq), 0)
-    for copy in (near_zero, far_one, near_one, far_zero, twin):
+    corner = along + 2 * (1 - 2 * bits[1])
+    near, far = send(0, piece(seq, 0), 1), send(1, piece(seq, 0), 2)
+    near_short, twin = send(2, piece(seq, 1), 1), send(3, piece(seq, None), 0)
+    for copy in (near, far, near_short, twin):
         copy.start()
     streaming[0] = False
     for copy in saves:
@@ -1621,12 +1628,13 @@
 
     transposed(at.low_one, at.turned_one)
     save(at.turned_one, at.mixer_in_x)
-    near_zero.wait()
-    far_one.wait()
-    near_forward = send(5, piece(across, 0), 2)
-    far_forward = send(6, piece(along, 1), 1)
-    near_forward.start()
-    far_forward.start()
+    near.wait()
+    forward_copy, near_share = send(4, piece(across, 0), 2), send(5, piece(across, 0), 0)
+    forward_copy.start()
+    near_share.start()
+    far.wait()
+    far_share = send(6, piece(along, 0), 0)
+    far_share.start()
     transposed(at.low_two, at.turned_two)
     save(at.turned_two, at.gated_x)
 
@@ -1635,7 +1643,7 @@
     together = 4
     chip = seq // 2
 
-    def attend(other):
+    def attend(other, places):
         @pl.when(other <= chip)
         def _():
             span = pl.ds(pl.multiple_of(other * 2 * length, 2 * length), 2 * length)
@@ -1643,9 +1651,8 @@
             key_at = lax.broadcasted_iota(jnp.int32, shape, 1) + other * 2 * length
             query_at = lax.broadcasted_iota(jnp.int32, shape, 0) + seq * length
             first = lanes_below((2 * length, lane), HEAD_DIM, lane)
-            for which in range(rows):
-                start = at.seg_start[pl.ds(which * length, length)]
-                start = jnp.concatenate([start, start], axis=1)
+            for which in places:
+                start = segment_start(at.lengths, row_of[which], query_at)
                 allowed = jnp.logical_and(key_at >= start, key_at <= query_at)
                 allowed = jnp.concatenate([allowed, allowed], axis=0)
 
@@ -1655,11 +1662,12 @@
                         at.both[which, span, pl.ds(pl.multiple_of(head * lane, lane), lane)]
                         for head in heads
                     ]
-                    places = [which * pairs_of + head for head in heads]
+                    spots = [which * pairs_of + head for head in heads]
                     scores = [
-                        dot_nt(at.paired[place], both) for place, both in zip(places, boths)
+                        dot_nt(at.paired[row_of[which] * pairs_of + head], both)
+                        for head, both in zip(heads, boths)
                     ]
-                    for place, score, both in zip(places, scores, boths):
+                    for place, score, both in zip(spots, scores, boths):
                         weights = jnp.where(allowed, jnp.exp(score), 0.0).astype(jnp.bfloat16)
                         right = jnp.where(first, 1.0, both.astype(jnp.float32))
                         at.sums[place] += jnp.dot(
@@ -1670,21 +1678,26 @@
                 lax.fori_loop(0, pairs_of // together, some, 0)
 
     twin.wait()
-    attend(chip)
-    near_one.wait()
-    near_share = send(7, piece(across), 0)
-    near_share.start()
-    far_zero.wait()
-    far_share = send(8, piece(along), 0)
-    far_share.start()
+    attend(chip, (0, 1))
+    near_share.wait()
+    attend(across // 2, (0,))
+    far_share.wait()
+    attend(along // 2, (0,))
+    near_short.wait()
+    short_share = send(7, piece(across, 1), 0)
+    short_share.start()
+    forward_copy.wait()
+    corner_share = send(8, piece(corner, 0), 0)
+    corner_share.start()
     transposed(at.low_three, at.turned_three)
     save(at.turned_three, at.first_in_x)
-    near_share.wait()
-    attend(across // 2)
+    short_share.wait()
+    attend(across // 2, (1,))
+    corner_share.wait()
+    save(at.both, at.keys_values)
+    attend(corner // 2, (0,))
     transposed(at.low_four, at.turned_four)
     save(at.turned_four, at.attend_in_x)
-    far_share.wait()
-    attend(along // 2)
 
     block_rows = at.turned_active.shape[3]
     x_count = at.turned_active.shape[2]
@@ -1700,19 +1713,12 @@
                     block * block_rows : (block + 1) * block_rows
                 ]
     save(at.turned_active, at.active_x)
-    near_forward.wait()
-    far_forward.wait()
-    corner_share = send(9, piece(corner), 0)
-    corner_share.start()
-    corner_share.wait()
-    save(at.both, at.keys_values)
-    attend(corner // 2)
-
     first = lanes_below((length, lane), HEAD_DIM, lane)
     for which in range(rows):
         span = pl.ds(which * length, length)
         for head in range(pairs_of):
-            value = at.sums[which * pairs_of + head]
+            place = jnp.where(single == which, 0, 1)
+            value = at.sums[place * pairs_of + head]
             value = value * (1.0 / pltpu.roll(value, HEAD_DIM, 1))
             value = jnp.where(first, pltpu.roll(value[:length], HEAD_DIM, 1), value[length:])
             at.attended[span, pl.ds(head * lane, lane)] = value.astype(jnp.bfloat16)
@@ -1783,6 +1789,7 @@
         queries_low=pltpu.VMEM((tokens, width), low),
         scaled=pltpu.VMEM((tokens, width), low),
         both=pltpu.VMEM((rows, total_length, width), low),
+        own_both=pltpu.VMEM((rows, length, width), low),
         paired=pltpu.VMEM((pairs, 2 * length, 2 * HEAD_DIM), low),
         sums=pltpu.VMEM((pairs, 2 * length, 2 * HEAD_DIM), full),
         turned_one=pltpu.VMEM(x_shape(width), low),
@@ -2108,7 +2115,8 @@
         columns = pl.ds(pl.multiple_of(head * 2 * HEAD_DIM, 2 * HEAD_DIM), 2 * HEAD_DIM)
         query = two_heads(queries[span, columns], True)
         upper = two_heads(attended_grad[span, columns], False)
-        both = keys_values[row_at, :, columns]
+        place = jnp.where(single_row(at.lengths, keys_values.shape[1]) == row_at, 0, 1)
+        both = keys_values[place, :, columns]
         key_at = lax.broadcasted_iota(jnp.int32, (both.shape[0], length), 0)
         query_at = lax.broadcasted_iota(jnp.int32, (both.shape[0], length), 1) + seq * length
         start = segment_start(at.lengths, row_at, query_at[0:8])[0:1]

time: 399 us -> 391 us (0.980)
  Pallas kernels: 398 us -> 389 us
    pallas_call x1, Pallas kernels: 342 us -> 337 us  [backward(): pl.pallas_call(kernel, out_shape=[jax.ShapeDtypeStruct((x_count * block_r...]
where the time goes in v8:
time: 391 us; the launch traced here: 390 us
  Pallas kernels  389 us (99%)
    pallas_call x1, Pallas kernels, backward(): pl.pallas_call(kernel, out_shape=[jax.ShapeDtypeStruct((x_count * block_r...  337 us
    pallas_call x1, Pallas kernels, forward(): pl.pallas_call(functools.partial(forward_kernel, list(arrays), list(outs)...  42 us
    pallas_call x1, Pallas kernels, to_full(): pl.pallas_call(functools.partial(finish_kernel, cuts, len(lows), shards),...  10.1 us

profile of v8, /device:TPU:0, one launch (start us, length us, event | category | flops | bytes accessed | tf_op | source)
XLA Modules:
  0.0 389.9 jit_solution(10313375115424729497)
XLA Ops:
  0.7 42.0 %shard_map.373 = (f32[256,1024]{1,0:T(8,128)}, f32[256,1024]{1,0:T(8,128)}, f32[256,1024]{1,0:T(8,128)}, f32[256,1024]{1,0:T(8,128)}, bf16[256,4608]{1,0:T(8,128...) custom-call(bf16[256,1024]{1,0:T(8,128)(2,1)} %bitcast.4, ...), custom_call_target="tpu_custom_call" | custom-call | flops 11143809024 | bytes 43530504 | tf_op jit(solution)/shard_map/pallas_call | solution.py:1818
  42.7 336.9 %shard_map.374 = (bf16[128,9216]{1,0:T(8,128)(2,1)}, bf16[576,1024]{1,0:T(8,128)(2,1)}, bf16[128,1024]{1,0:T(8,128)(2,1)}, bf16[128,2048]{1,0:T(8,128)(2,1)}, bf...) custom-call(bf16[4,2,2,64,256]{4,3,2,1,0:T(8,128)(2,1)} %get-tuple-e, ...), custom_call_target="tpu_custom_call" | custom-call | flops 37044092928 | bytes 72351744 | tf_op jit(solution)/shard_map/pallas_call | solution.py:2407
  379.6 10.1 %shard_map.375 = (f32[128,4608]{1,0:T(8,128)}, f32[128,4608]{1,0:T(8,128)}, f32[128,4608]{1,0:T(8,128)}, f32[128,4608]{1,0:T(8,128)}, f32[576,1024]{1,0:T(8,128)...) custom-call(bf16[256,1024]{1,0:T(8,128)(2,1)} %get-tuple-element.95., ...), custom_call_target="tpu_custom_call" | custom-call | flops 4456448 | bytes 26738688 | tf_op jit(solution)/shard_map/pallas_call | solution.py:1228
